TPU v7x, 32 devices: a whole 2x2x4 slice. The times are simulated.
32 devices in a mesh: expert: 8 (over z, y), tensor: 4 (over x, core).
Axes of the slice: x: 2, y: 2, z: 4, core: 2. Of those that a mesh axis runs over, the one named last changes fastest.
Arguments:
- tokens: bfloat16 [32768, 1024], P(('expert', 'tensor')), may hold values from -6 to 6
- routes: int32 [32768, 1], P(('expert', 'tensor')), may hold values from 0 to 15; in each aligned block of 1024 rows (0 to 1023, 1024 to 2047, ...) at most 128 rows name the same one
- cotangent: bfloat16 [32768, 1024], P(('expert', 'tensor')), may hold values from -6 to 6
- ln_gain: bfloat16 [16, 1024], P('expert'), may hold values from 0.099609375 to 1.8984375
- layer_norm_bias: bfloat16 [16, 1024], P('expert'), may hold values from -1.796875 to 1.796875
- centroid: bfloat16 [16, 1024], P('expert'), may hold values from -0.119628906 to 0.119628906
- w_in: bfloat16 [16, 1024, 4096], P('expert', None, 'tensor'), may hold values from -0.1875 to 0.1875
- w_out: bfloat16 [16, 4096, 1024], P('expert', 'tensor'), may hold values from -0.1875 to 0.1875
Outputs:
- layer_out: bfloat16 [32768, 1024], P(('expert', 'tensor'))
- tokens_grad: float32 [32768, 1024], P(('expert', 'tensor'))
- gain_grad: float32 [16, 1024], P('expert')
- bias_grad: float32 [16, 1024], P('expert')
- centroid_grad: float32 [16, 1024], P('expert')
- w_in_grad: float32 [16, 1024, 4096], P('expert', None, 'tensor')
- w_out_grad: float32 [16, 4096, 1024], P('expert', 'tensor')
Inputs may be any that keep to these rules, and one draw needn't show every extreme that they name: `routes`: of the tokens of one device (aligned blocks of 1024 rows) at most 128 name one expert; some expert receives exactly 128 from some device in every draw.
All inputs are finite; a program needn't handle non-finite values.
Results may differ from a plain program's by a relative error of at most 0.0063.
Values may be sent and summed in bfloat16 or wider, within the bound.
No kernel may reach another device: no remote copies, remote signals or barrier semaphores. Data moves between devices by JAX's collectives and lax.ppermute only.
A program may use at most 256 MiB of HBM per device.

v0:
```python
import jax
import jax.numpy as jnp
from jax import lax
from jax.sharding import PartitionSpec as P

epsilon = 1e-05


def gelu_slope(preact):
    cumul = 0.5 * (1.0 + lax.erf(preact * 0.7071067811865476))
    density = jnp.exp(-0.5 * preact * preact) * 0.3989422804014327
    return cumul + preact * density


def per_device(tokens, routes, cotangent, ln_gain, layer_norm_bias, centroid, w_in, w_out):
    groups = lax.axis_size("expert")
    local_experts = ln_gain.shape[0]
    all_experts = groups * local_experts
    tok_count = tokens.shape[0]
    width = tokens.shape[1]
    capacity = 2 * tok_count // all_experts
    targets = routes[:, 0]
    onehot = (targets[:, None] == jnp.arange(all_experts, dtype=jnp.int32)[None, :]).astype(
        jnp.int32
    )
    ranks = jnp.sum(jnp.cumsum(onehot, axis=0) * onehot, axis=1) - 1
    slot_index = targets * capacity + ranks

    def place(values):
        buffer = jnp.zeros((all_experts * capacity, width), jnp.bfloat16).at[slot_index].set(values)
        return buffer.reshape(groups, local_experts, capacity, width)

    def unplace(arrived):
        return arrived.reshape(all_experts * capacity, width)[slot_index]

    arrived_x = lax.all_to_all(place(tokens), "expert", split_axis=0, concat_axis=2, tiled=True)
    inputs = arrived_x[0]
    xfloat = inputs.astype(jnp.float32)
    row_mean = jnp.mean(xfloat, axis=-1, keepdims=True)
    centered_rows = xfloat - row_mean
    variance = jnp.mean(centered_rows * centered_rows, axis=-1, keepdims=True)
    inverse_deviation = lax.rsqrt(variance + epsilon)
    standardized_input = centered_rows * inverse_deviation
    gain_float = ln_gain.astype(jnp.float32)[:, None, :]
    normed_rows = (
        standardized_input * gain_float + layer_norm_bias.astype(jnp.float32)[:, None, :]
    ).astype(jnp.bfloat16)
    logits = jnp.einsum("emd,ed->em", inputs, centroid, preferred_element_type=jnp.float32)
    gate_val = jax.nn.sigmoid(logits)
    full_in, full_out = (w_in, w_out)
    normed_all = lax.all_gather(normed_rows, "tensor", axis=1, tiled=True)
    preact = jnp.einsum("erd,edh->erh", normed_all, full_in, preferred_element_type=jnp.float32)
    hidden = jax.nn.gelu(preact, approximate=False).astype(jnp.bfloat16)
    partial_out = jnp.einsum("erh,ehd->erd", hidden, full_out, preferred_element_type=jnp.float32)
    mixed = lax.psum_scatter(partial_out, "tensor", scatter_dimension=1, tiled=True)
    gated = (gate_val[..., None] * mixed).astype(jnp.bfloat16)
    returned = lax.all_to_all(gated[None], "expert", split_axis=2, concat_axis=0, tiled=True)
    layer_out = (tokens.astype(jnp.float32) + unplace(returned).astype(jnp.float32)).astype(
        jnp.bfloat16
    )
    arrived_dy = lax.all_to_all(place(cotangent), "expert", split_axis=0, concat_axis=2, tiled=True)
    dy_float = arrived_dy[0].astype(jnp.float32)
    gate_grad = jnp.sum(dy_float * mixed, axis=-1)
    logit_grad = gate_grad * gate_val * (1.0 - gate_val)
    mixed_grad = (gate_val[..., None] * dy_float).astype(jnp.bfloat16)
    mixed_all = lax.all_gather(mixed_grad, "tensor", axis=1, tiled=True)
    hidden_grad = jnp.einsum(
        "erd,ehd->erh", mixed_all, full_out, preferred_element_type=jnp.float32
    )
    pre_grad = (hidden_grad * gelu_slope(preact)).astype(jnp.bfloat16)
    out_wgrad = jnp.einsum("erh,erd->ehd", hidden, mixed_all, preferred_element_type=jnp.float32)
    in_wgrad = jnp.einsum("erd,erh->edh", normed_all, pre_grad, preferred_element_type=jnp.float32)
    normed_part = jnp.einsum("erh,edh->erd", pre_grad, full_in, preferred_element_type=jnp.float32)
    normed_gradient = lax.psum_scatter(normed_part, "tensor", scatter_dimension=1, tiled=True)
    gain_portion = jnp.sum(normed_gradient * standardized_input, axis=1)
    bias_part = jnp.sum(normed_gradient, axis=1)
    center_part = jnp.einsum("em,emd->ed", logit_grad, xfloat)
    gain_grad, bias_grad, centroid_grad = lax.psum((gain_portion, bias_part, center_part), "tensor")
    scaled_gradient = normed_gradient * gain_float
    inner_product_mean = jnp.mean(scaled_gradient, axis=-1, keepdims=True)
    cross_term_mean = jnp.mean(scaled_gradient * standardized_input, axis=-1, keepdims=True)
    expert_gradient = inverse_deviation * (
        scaled_gradient - inner_product_mean - standardized_input * cross_term_mean
    )
    expert_gradient = (
        expert_gradient + logit_grad[..., None] * centroid.astype(jnp.float32)[:, None, :]
    )
    back_rows = lax.all_to_all(
        expert_gradient.astype(jnp.bfloat16)[None],
        "expert",
        split_axis=2,
        concat_axis=0,
        tiled=True,
    )
    tokens_grad = cotangent.astype(jnp.float32) + unplace(back_rows).astype(jnp.float32)
    return (layer_out, tokens_grad, gain_grad, bias_grad, centroid_grad, in_wgrad, out_wgrad)


def solution(mesh):
    placed = (
        P(("expert", "tensor"), None),
        P(("expert", "tensor"), None),
        P(("expert", "tensor"), None),
        P("expert", None),
        P("expert", None),
        P("expert", None),
        P("expert", None, "tensor"),
        P("expert", "tensor", None),
    )
    return jax.shard_map(
        per_device,
        mesh=mesh,
        in_specs=placed,
        out_specs=(
            P(("expert", "tensor"), None),
            P(("expert", "tensor"), None),
            P("expert", None),
            P("expert", None),
            P("expert", None),
            P("expert", None, "tensor"),
            P("expert", "tensor", None),
        ),
        check_vma=False,
    )
```

profile of v0, /device:TPU:0, one launch (start us, length us, event | category | flops | bytes accessed | tf_op | source)
XLA Modules:
  0.0 1178.7 jit_solution(12039802455304334203)
XLA Ops:
  7.2 0.7 fusion.27
  7.9 4.5 reduce-window.6
  12.8 0.7 fusion.26
  13.5 0.7 compare_select_fusion
  14.2 8.6 scatter_custom_fusion
  22.8 7.3 all-to-all-start
  30.9 0.7 convert_element_type.71
  31.6 91.8 %all-to-all-done = bf16[8,2,128,1024]{3,2,1,0:T(8,128)(2,1)} async-done(((bf16[8,2,128,1024]{3,2,1,0:T(8,128)(2,1)}), bf16[8,2,128,1024]{3,2,1,0:T(8,128)(2,1)}, u32[]{:S(2)}, u32[]{:S(2)}) %all-to-all-start) | async-done | bytes 4194336 | tf_op jit(solution)/shard_map/all_to_all | solution.py:36
  123.4 2.8 convert_reduce_fusion
  126.3 3.0 fusion.16
  129.3 2.6 copy.31
  131.9 2.0 copy-done
  133.9 3.0 add_convert_fusion.1
  137.3 104.8 %all-gather.3.cloned.1.call-done = bf16[2,4096,1024]{2,1,0:T(8,128)(2,1)} async-done(((bf16[2,1024,1024]{2,1,0:T(8,128)(2,1)}), bf16[2,4096,1024]{2,1,0:T(8,128)(2,1)}) %all-gather.3.cloned.1.call-update) | async-done | bytes 16777232 | tf_op jit(solution)/shard_map/all_gather | solution.py:51
  242.1 37.9 %fusion.18 = (u8[4096,1024]{1,0:T(8,128)(4,1)}, u8[4096,1024]{1,0:T(8,128)(4,1)}, f32[2,4096,1024]{2,1,0:T(8,128)}) fusion(bf16[2,4096,1024]{2,1,0:T(8,128)(2,1)} %all-gather.3.cloned.1.call-done, bf16[2,1024,1024]{2,1,0:T(8,128)(2,1)} %param.14), kind=kOutput, calls=%fused_computation.47 | convolution fusion | flops 17280532480 | bytes 62914560 | tf_op jit(solution)/shard_map/erd,edh->erh/dot_general | solution.py:52
  280.0 80.2 %fusion.2 = bf16[2,4096,1024]{2,1,0:T(8,128)(2,1)} fusion(f32[2,4096,1024]{2,1,0:T(8,128)} %get-tuple-element.22, u8[4096,1024]{1,0:T(8,128)(4,1)} %get-tuple-element.8, u8[4096,1024]{1,0:T(8,128)(4,1)} %get-tuple-element.7), kind=kLoop, calls=%fused_computation.8 | loop fusion | flops 587202560 | bytes 58720256 | tf_op jit(solution)/shard_map/convert_element_type | solution.py:53
  360.2 26.1 %fusion.37 = f32[2,4096,1024]{2,1,0:T(8,128)} fusion(bf16[2,4096,1024]{2,1,0:T(8,128)(2,1)} %fusion.2, bf16[2,1024,1024]{2,1,0:T(8,128)(2,1)S(1)} %copy-done.10), kind=kOutput, calls=%fused_computation.82 | convolution fusion | flops 17179869184 | bytes 54525952 | tf_op jit(solution)/shard_map/erh,ehd->erd/dot_general | solution.py:54
  386.4 9.0 scatter_custom_fusion.1
  395.4 99.0 %all_to_all.54 = bf16[8,2,128,1024]{3,2,1,0:T(8,128)(2,1)S(1)} all-to-all(bf16[8,2,128,1024]{3,2,1,0:T(8,128)(2,1)} %bitcast.88), channel_id=1, replica_groups=mesh['expert'=8,'tensor'=4] {'expert'}, dimensions={0} | all-to-all | bytes 8388608 | tf_op jit(solution)/shard_map/all_to_all | solution.py:61
  494.4 1.0 convert_bitcast_fusion
  495.5 4.3 copy.34
  499.8 1.2 fusion.33
  501.0 120.5 %reduce-scatter.3.cloned.1.call-done = f32[2,1024,1024]{2,1,0:T(8,128)} async-done(((f32[2,4096,1024]{2,1,0:T(8,128)}), f32[2,1024,1024]{2,1,0:T(8,128)}) %reduce-scatter.3.cloned.1.call-update) | async-done | bytes 8388624 | tf_op jit(solution)/shard_map/reduce_scatter | solution.py:55
  621.4 6.7 multiply_reduce_fusion.1
  628.4 1.3 slice-done.1
  629.7 6.0 multiply_convert_fusion
  635.8 106.0 %all-gather.5.cloned.1.call-done = bf16[2,4096,1024]{2,1,0:T(8,128)(2,1)} async-done(((bf16[2,1024,1024]{2,1,0:T(8,128)(2,1)}), bf16[2,4096,1024]{2,1,0:T(8,128)(2,1)}) %all-gather.5.cloned.1.call-update) | async-done | bytes 16777232 | tf_op jit(solution)/shard_map/all_gather | solution.py:66
  741.8 33.8 %fusion.8 = bf16[2,4096,1024]{2,1,0:T(8,128)(2,1)} fusion(f32[2,4096,1024]{2,1,0:T(8,128)} %get-tuple-element.22, bf16[2,4096,1024]{2,1,0:T(8,128)(2,1)} %all-gather.5.cloned.1.call-done, bf16[2,1024,1024]{2,1,0:T(8,128)(2,1)} %param.15), kind=kOutput, calls=%fused_computation.14 | convolution fusion | flops 17263755264 | bytes 71303168 | tf_op jit(solution)/shard_map/erd,ehd->erh/dot_general | solution.py:67
  775.7 26.1 %fusion.38 = f32[2,4096,1024]{2,1,0:T(8,128)} fusion(bf16[2,4096,1024]{2,1,0:T(8,128)(2,1)} %fusion.8, bf16[2,1024,1024]{2,1,0:T(8,128)(2,1)S(1)} %copy-done.11), kind=kOutput, calls=%fused_computation.83 | convolution fusion | flops 17179869184 | bytes 54525952 | tf_op jit(solution)/shard_map/erh,edh->erd/dot_general | solution.py:73
  801.8 8.8 copy.32
  810.6 5.3 all-to-all-start.1
  815.9 3.9 fusion.31
  819.8 89.8 %all-to-all-done.1 = bf16[1,2,1024,1024]{3,1,0,2:T(2,128)(2,1)} async-done(((bf16[1,2,1024,1024]{3,1,0,2:T(2,128)(2,1)}), bf16[1,2,1024,1024]{3,1,0,2:T(2,128)(2,1)}, u32[]{:S(2)}, u32[]{:S(2)}) %all-to-all-start.1) | async-done | bytes 4194336 | tf_op jit(solution)/shard_map/all_to_all | solution.py:57
  909.6 5.6 copy.33
  915.1 7.7 gather_fusion
  922.9 3.9 add_convert_fusion.2
  926.7 110.1 %reduce-scatter.5.cloned.1.call-done = f32[2,1024,1024]{2,1,0:T(8,128)} async-done(((f32[2,4096,1024]{2,1,0:T(8,128)}), f32[2,1024,1024]{2,1,0:T(8,128)}) %reduce-scatter.5.cloned.1.call-update) | async-done | bytes 8388624 | tf_op jit(solution)/shard_map/reduce_scatter | solution.py:74
  1036.8 6.5 multiply_reduce_fusion
  1043.9 5.0 fusion.20
  1048.8 6.3 copy.35
  1055.2 5.7 all-to-all-start.3
  1060.9 25.6 %fusion.40 = f32[2,1024,1024]{2,1,0:T(8,128)} fusion(bf16[2,4096,1024]{2,1,0:T(8,128)(2,1)} %fusion.2, bf16[2,4096,1024]{2,1,0:T(8,128)(2,1)} %all-gather.5.cloned.1.call-done), kind=kOutput, calls=%fused_computation.85 | convolution fusion | flops 17179869184 | bytes 41943040 | tf_op jit(solution)/shard_map/erh,erd->ehd/dot_general | solution.py:71
  1086.5 25.8 %fusion.39 = f32[2,1024,1024]{2,1,0:T(8,128)} fusion(bf16[2,4096,1024]{2,1,0:T(8,128)(2,1)} %all-gather.3.cloned.1.call-done, bf16[2,4096,1024]{2,1,0:T(8,128)(2,1)} %fusion.8), kind=kOutput, calls=%fused_computation.84 | convolution fusion | flops 17179869184 | bytes 41943040 | tf_op jit(solution)/shard_map/erd,erh->edh/dot_general | solution.py:72
  1112.3 11.9 %all-reduce = (f32[2,1024]{1,0:T(2,128)}, f32[2,1024]{1,0:T(2,128)}, f32[2,1024]{1,0:T(2,128)}) all-reduce(f32[2,1024]{1,0:T(2,128)S(1)} %get-tuple-element.9, f32[2,1024]{1,0:T(2,128)S(1)} %get-tuple-element.12, f32[2,1024]{1,0:T(2,128)S(1)} %bitcast.94), channel_id=1, replica_groups=mesh['expert'=8,'tensor'=4] {'tensor'}, use_global_device_ids=true, to_apply=%region_13.14 | all-reduce | flops 6144 | bytes 49152 | tf_op jit(solution)/shard_map/psum | solution.py:78
  1124.2 29.9 %all-to-all-done.3 = bf16[1,2,1024,1024]{3,1,0,2:T(2,128)(2,1)} async-done(((bf16[1,2,1024,1024]{3,1,0,2:T(2,128)(2,1)}), bf16[1,2,1024,1024]{3,1,0,2:T(2,128)(2,1)}, u32[]{:S(2)}, u32[]{:S(2)}) %all-to-all-start.3) | async-done | bytes 4194336 | tf_op jit(solution)/shard_map/all_to_all | solution.py:88
  1154.1 5.5 copy.36
  1159.7 7.7 gather_fusion.1
  1167.4 4.5 convert_add_fusion
  (50 shorter events, 2.4 us)
Async XLA Ops:
  22.8 100.6 %all-to-all-start = ((bf16[8,2,128,1024]{3,2,1,0:T(8,128)(2,1)}), bf16[8,2,128,1024]{3,2,1,0:T(8,128)(2,1)}, u32[]{:S(2)}, u32[]{:S(2)}) async-start(bf16[8,2,128,1024]{3,2,1,0:T(8,128)(2,1)} %bitcast.87), calls=%async_computation | async-start | bytes 8388608 | tf_op jit(solution)/shard_map/all_to_all | solution.py:36
  30.1 211.9 %all-gather.3.cloned.1.call-start = ((), (), s32[]{:S(2)}) async-start(), calls=%async_computation.6 | async-start | bytes 20971520 | tf_op jit(solution)/shard_map/all_gather | solution.py:51
  30.9 249.1 %copy-start.5 = (f32[2,1024]{1,0:T(2,128)}, f32[2,1024]{1,0:T(2,128)S(1)}, u32[]{:S(2)}) copy-start(f32[2,1024]{1,0:T(2,128)S(1)} %convert_element_type.70) | copy-start | bytes 24580
  126.2 5.7 copy-start.3
  129.3 2.7 copy-start.7
  131.9 2.0 copy-start
  136.9 484.5 %reduce-scatter.3.cloned.1.call-start = ((), (), s32[]{:S(2)}) async-start(), calls=%async_computation.7 | async-start | bytes 41943040 | tf_op jit(solution)/shard_map/reduce_scatter | solution.py:55
  280.0 80.2 %copy-start.10 = (bf16[2,1024,1024]{2,1,0:T(8,128)(2,1)S(1)}, bf16[2,1024,1024]{2,1,0:T(8,128)(2,1)}, u32[]{:S(2)}) copy-start(bf16[2,1024,1024]{2,1,0:T(8,128)(2,1)} %param.15) | copy-start | bytes 12582916
  386.4 355.4 %all-gather.5.cloned.1.call-start = ((), (), s32[]{:S(2)}) async-start(), calls=%async_computation.8 | async-start | bytes 20971520 | tf_op jit(solution)/shard_map/all_gather | solution.py:66
  494.4 5.3 copy-start.1
  494.4 5.3 copy-start.9
  621.4 7.0 slice-start
  621.4 8.2 slice-start.1
  635.7 401.1 %reduce-scatter.5.cloned.1.call-start = ((), (), s32[]{:S(2)}) async-start(), calls=%async_computation.9 | async-start | bytes 41943040 | tf_op jit(solution)/shard_map/reduce_scatter | solution.py:74
  741.8 33.8 %copy-start.11 = (bf16[2,1024,1024]{2,1,0:T(8,128)(2,1)S(1)}, bf16[2,1024,1024]{2,1,0:T(8,128)(2,1)}, u32[]{:S(2)}) copy-start(bf16[2,1024,1024]{2,1,0:T(8,128)(2,1)} %param.14) | copy-start | bytes 12582916
  810.6 99.0 %all-to-all-start.1 = ((bf16[1,2,1024,1024]{3,1,0,2:T(2,128)(2,1)}), bf16[1,2,1024,1024]{3,1,0,2:T(2,128)(2,1)}, u32[]{:S(2)}, u32[]{:S(2)}) async-start(bf16[1,2,1024,1024]{3,1,0,2:T(2,128)(2,1)} %copy.32), calls=%async_computation.2 | async-start | bytes 8388608 | tf_op jit(solution)/shard_map/all_to_all | solution.py:57
  909.6 127.3 %copy-start.4 = (f32[2,1024]{1,0:T(2,128)S(1)}, f32[2,1024]{1,0:T(2,128)}, u32[]{:S(2)}) copy-start(f32[2,1024]{1,0:T(2,128)} %copy-done.3) | copy-start | bytes 24580
  909.6 127.3 %copy-start.6 = (f32[2,1024]{1,0:T(2,128)S(1)}, f32[2,1024]{1,0:T(2,128)}, u32[]{:S(2)}) copy-start(f32[2,1024]{1,0:T(2,128)} %copy-done.5) | copy-start | bytes 24580
  909.6 127.3 %copy-start.8 = (f32[2,1024]{1,0:T(2,128)S(1)}, f32[2,1024]{1,0:T(2,128)}, u32[]{:S(2)}) copy-start(f32[2,1024]{1,0:T(2,128)} %copy-done.7) | copy-start | bytes 24580
  1036.8 7.0 copy-start.2
  1055.2 99.0 %all-to-all-start.3 = ((bf16[1,2,1024,1024]{3,1,0,2:T(2,128)(2,1)}), bf16[1,2,1024,1024]{3,1,0,2:T(2,128)(2,1)}, u32[]{:S(2)}, u32[]{:S(2)}) async-start(bf16[1,2,1024,1024]{3,1,0,2:T(2,128)(2,1)} %copy.35), calls=%async_computation.5 | async-start | bytes 8388608 | tf_op jit(solution)/shard_map/all_to_all | solution.py:88
Sparse Core Ops, SparseCore 0:
  137.0 104.9 all-gather.2
  386.5 234.8 reduce-scatter.2
  635.8 105.9 all-gather.4
  801.9 234.8 reduce-scatter.4
where the time goes:
time: 1190 us; the launch traced here: 1180 us
  waiting for transfers between devices  653 us (55%)
  matrix products  180 us (15%)
  other arithmetic  131 us (11%)
  blocking collectives  111 us (9%)
  local copies, waits for them, and re-layouts  70.5 us (6%)
  starting transfers between devices  18.8 us (2%)
  between operations  14.2 us (1%)
    reduce_scatter x1, waiting for transfers between devices, per_device(): lax.psum_scatter(partial_out, 'tensor', scatter_dimension=1, tiled=True)  120 us
    reduce_scatter x1, waiting for transfers between devices, per_device(): lax.psum_scatter(normed_part, 'tensor', scatter_dimension=1, tiled=True)  110 us
    all_gather x1, waiting for transfers between devices, per_device(): mixed_all = lax.all_gather(mixed_grad, 'tensor', axis=1, tiled=True)  106 us
    all_gather x1, waiting for transfers between devices, per_device(): normed_all = lax.all_gather(normed_rows, 'tensor', axis=1, tiled=True)  105 us
    all_to_all x1, blocking collectives, per_device(): lax.all_to_all(place(cotangent), 'expert', split_axis=0, concat_axis=2, t...  99 us
    all_to_all x1, waiting for transfers between devices, per_device(): lax.all_to_all(place(tokens), 'expert', split_axis=0, concat_axis=2, tile...  91.8 us
    all_to_all x1, waiting for transfers between devices, per_device(): lax.all_to_all(gated[None], 'expert', split_axis=2, concat_axis=0, tiled=...  89.8 us
    convert_element_type x1, other arithmetic, per_device(): hidden = jax.nn.gelu(preact, approximate=False).astype(jnp.bfloat16)  80.2 us
  transfers between devices with their start and end apart: 7, of which 7 were waited for; matrix products, arithmetic and copies ran while one was open for 8% of the time, Pallas kernels for 0%

commit v1 on v0

v1 whole, which is shorter than its diff:
```python
import jax
import jax.numpy as jnp
from jax import lax
from jax.sharding import Mesh
from jax.sharding import PartitionSpec as P

epsilon = 1e-05
F32 = jnp.float32
BF16 = jnp.bfloat16


def per_device(tokens, routes, cotangent, ln_gain, layer_norm_bias, centroid, w_in, w_out):
    groups, halves, subs = (lax.axis_size(a) for a in ("expert", "half", "sub"))
    half = lax.axis_index("half")
    experts = groups * halves
    count, width = tokens.shape
    capacity = 2 * count // experts
    targets = routes[:, 0]

    onehot = targets[:, None] == jnp.arange(experts, dtype=jnp.int32)[None, :]
    order = jnp.arange(count, dtype=jnp.int32)
    earlier = (order[:, None] >= order[None, :]).astype(BF16)
    ranks = jnp.dot(earlier, onehot.astype(BF16), preferred_element_type=F32)
    ranks = jnp.sum(jnp.where(onehot, ranks, 0.0), axis=1).astype(jnp.int32) - 1
    slot = targets * capacity + ranks
    slots = jnp.arange(experts * capacity, dtype=jnp.int32)

    def place(values):
        chosen = (slots[:, None] == slot[None, :]).astype(BF16)
        return jnp.dot(chosen, values, preferred_element_type=F32).astype(BF16)

    def unplace(arrived):
        chosen = (slot[:, None] == slots[None, :]).astype(BF16)
        return jnp.dot(chosen, arrived, preferred_element_type=F32)

    def exchange(rows):
        rows = rows.reshape(experts, capacity, width)
        return lax.all_to_all(
            rows, ("expert", "half"), split_axis=0, concat_axis=0, tiled=True
        ).reshape(experts * capacity, width)

    def over(axis, value):
        size = lax.axis_size(axis)
        return lax.ppermute(value, axis, [(i, size - 1 - i) for i in range(size)])

    def pick(stacked, index):
        return lax.dynamic_index_in_dim(stacked, index, 0, keepdims=False)

    def blocks_of(weight):
        own, send = pick(weight, half), pick(weight, 1 - half)
        beside = over("half", send)
        return [own, over("sub", own), beside, over("sub", beside)]

    x = exchange(place(tokens)).astype(F32)
    ins, outs = blocks_of(w_in), blocks_of(w_out)
    dy = exchange(place(cotangent)).astype(F32)

    gain = pick(ln_gain, half).astype(F32)[None, :]
    bias = pick(layer_norm_bias, half).astype(F32)[None, :]
    center = pick(centroid, half).astype(F32)[None, :]
    centered = x - jnp.mean(x, axis=-1, keepdims=True)
    inverse = lax.rsqrt(jnp.mean(centered * centered, axis=-1, keepdims=True) + epsilon)
    xhat = centered * inverse
    normed = (xhat * gain + bias).astype(BF16)
    gate = jax.nn.sigmoid(jnp.sum(x * center, axis=-1, keepdims=True))

    hiddens, slopes = [], []
    mixed = 0.0
    for first, second in zip(ins, outs):
        z = jnp.dot(normed, first, preferred_element_type=F32)
        cumul = 0.5 * (1.0 + lax.erf(z * 0.7071067811865476))
        density = jnp.exp(-0.5 * z * z) * 0.3989422804014327
        hidden = (z * cumul).astype(BF16)
        hiddens.append(hidden)
        slopes.append((cumul + z * density).astype(BF16))
        mixed = mixed + jnp.dot(hidden, second, preferred_element_type=F32)
    returned = exchange((gate * mixed).astype(BF16))

    logit_grad = jnp.sum(dy * mixed, axis=-1, keepdims=True) * gate * (1.0 - gate)
    mixed_grad = (gate * dy).astype(BF16)
    rows_in = (((0,), (0,)), ((), ()))
    last = (((1,), (1,)), ((), ()))
    pre_grads = []
    normed_grad = 0.0
    for first, second, slope in zip(ins, outs, slopes):
        hidden_grad = lax.dot_general(mixed_grad, second, last, preferred_element_type=F32)
        pre_grad = (hidden_grad * slope.astype(F32)).astype(BF16)
        pre_grads.append(pre_grad)
        normed_grad = normed_grad + lax.dot_general(
            pre_grad, first, last, preferred_element_type=F32
        )
    u = normed_grad * gain
    expert_grad = (
        inverse
        * (u - jnp.mean(u, axis=-1, keepdims=True) - xhat * jnp.mean(u * xhat, axis=-1, keepdims=True))
        + logit_grad * center
    )
    back = exchange(expert_grad.astype(BF16))

    def shared(parts):
        kept = parts[0] + over("sub", parts[1].astype(BF16)).astype(F32)
        sent = parts[2] + over("sub", parts[3].astype(BF16)).astype(F32)
        got = over("half", sent.astype(BF16)).astype(F32)
        return jnp.stack([jnp.where(half == i, kept, got) for i in range(2)])

    out_wgrad = shared(
        [lax.dot_general(h, mixed_grad, rows_in, preferred_element_type=F32) for h in hiddens]
    )
    in_wgrad = shared(
        [lax.dot_general(normed, p, rows_in, preferred_element_type=F32) for p in pre_grads]
    )
    small = jnp.stack(
        [
            jnp.sum(normed_grad * xhat, axis=0),
            jnp.sum(normed_grad, axis=0),
            jnp.sum(logit_grad * x, axis=0),
        ]
    )
    small = jnp.where((jnp.arange(halves) == half)[:, None, None], small[None], 0.0)
    small = lax.psum(small, ("half", "sub"))
    layer_out = (tokens.astype(F32) + unplace(returned)).astype(BF16)
    tokens_grad = cotangent.astype(F32) + unplace(back)
    return (layer_out, tokens_grad, small[:, 0], small[:, 1], small[:, 2], in_wgrad, out_wgrad)


def solution(mesh):
    groups, tensor = mesh.shape["expert"], mesh.shape["tensor"]
    halves = 2
    split = Mesh(
        mesh.devices.reshape(groups, halves, tensor // halves), ("expert", "half", "sub")
    )
    rows, within = P(("expert", "half", "sub"), None), P("expert", None)
    columns = P("expert", None, ("half", "sub"))
    depth = P("expert", ("half", "sub"), None)
    return jax.shard_map(
        per_device,
        mesh=split,
        in_specs=(rows, rows, rows, within, within, within, columns, depth),
        out_specs=(rows, rows, within, within, within, columns, depth),
        check_vma=False,
    )
```

time: 1190 us -> 662 us (0.56)
  waiting for transfers between devices: 653 us -> 276 us
  blocking collectives: 111 us -> 21 us
  other arithmetic: 131 us -> 45.4 us
  local copies, waits for them, and re-layouts: 70.5 us -> 5.39 us
  matrix products: 180 us -> 243 us
  starting transfers between devices: 18.8 us -> 62.8 us
  between operations: 14.2 us -> 1.52 us
    reduce_scatter x2 -> x0, waiting for transfers between devices: 231 us -> none  [the longest x1 120 us: per_device(): lax.psum_scatter(partial_out, 'tensor', scatter_dimension=1, tiled=True)]
    ppermute x0 -> x12, waiting for transfers between devices: none -> 224 us  [over(): return lax.ppermute(value, axis, [(i, size - 1 - i) for i in range(size)])]
    all_gather x2 -> x0, waiting for transfers between devices: 211 us -> none  [the longest x1 106 us: per_device(): mixed_all = lax.all_gather(mixed_grad, 'tensor', axis=1, tiled=True)]
    all_to_all x3 -> x4, waiting for transfers between devices: 212 us -> 51.9 us  [exchange(): lax.all_to_all(rows, ('expert', 'half'), split_axis=0, concat_axis=0, til...]
    all_to_all x1 -> x0, blocking collectives: 99 us -> none  [per_device(): lax.all_to_all(place(cotangent), 'expert', split_axis=0, concat_axis=2, t...]
    convert_element_type x9 -> x4, other arithmetic: 96.2 us -> 20 us  [the longest x2 8.06 us: per_device(): normed = (xhat * gain + bias).astype(BF16)]
    dot_general x8 -> x29, matrix products: 180 us -> 243 us  [the longest x4 42.7 us: per_device(): mixed = mixed + jnp.dot(hidden, second, preferred_element_type=F32)]
    all_to_all x3 -> x4, starting transfers between devices: 18.3 us -> 56.9 us  [exchange(): lax.all_to_all(rows, ('expert', 'half'), split_axis=0, concat_axis=0, til...]
  transfers between devices with their start and end apart: 7 -> 16, of which waited for: 7 -> 6; matrix products, arithmetic and copies ran while one was open for 8% -> 25% of each run, Pallas kernels for 0% -> 0%
where the time goes in v1:
time: 662 us; the launch traced here: 655 us
  waiting for transfers between devices  276 us (42%)
  matrix products  243 us (37%)
  starting transfers between devices  62.8 us (9%)
  other arithmetic  45.4 us (7%)
  blocking collectives  21 us (3%)
    ppermute x12, waiting for transfers between devices, over(): return lax.ppermute(value, axis, [(i, size - 1 - i) for i in range(size)])  224 us
    all_to_all x4, starting transfers between devices, exchange(): lax.all_to_all(rows, ('expert', 'half'), split_axis=0, concat_axis=0, til...  56.9 us
    all_to_all x4, waiting for transfers between devices, exchange(): lax.all_to_all(rows, ('expert', 'half'), split_axis=0, concat_axis=0, til...  51.9 us
    dot_general x4, matrix products, per_device(): mixed = mixed + jnp.dot(hidden, second, preferred_element_type=F32)  42.7 us
    dot_general x4, matrix products, per_device(): lax.dot_general(pre_grad, first, last, preferred_element_type=F32)  41.7 us
    dot_general x4, matrix products, per_device(): lax.dot_general(mixed_grad, second, last, preferred_element_type=F32)  39 us
    dot_general x4, matrix products, per_device(): z = jnp.dot(normed, first, preferred_element_type=F32)  35.6 us
    dot_general x4, matrix products, per_device(): lax.dot_general(h, mixed_grad, rows_in, preferred_element_type=F32)  29.3 us
  transfers between devices with their start and end apart: 16, of which 6 were waited for; matrix products, arithmetic and copies ran while one was open for 25% of the time, Pallas kernels for 0%

profile of v1, /device:TPU:0, one launch (start us, length us, event | category | flops | bytes accessed | tf_op | source)
XLA Modules:
  0.0 655.3 jit_solution(11740361200029574741)
XLA Ops:
  3.2 7.6 %fusion.37 = bf16[2048,1024]{1,0:T(8,128)(2,1)} fusion(bf16[1024,1024]{1,0:T(8,128)(2,1)} %param.8, s32[1024]{0:T(1024)S(1)} %get-tuple-element.34), kind=kOutput, calls=%fused_computation.86 | convolution fusion | flops 4299161600 | bytes 6295552 | tf_op jit(solution)/shard_map/dot_general | solution.py:30
  10.8 8.4 %all-to-all-start = ((bf16[16,128,1024]{2,1,0:T(8,128)(2,1)}), bf16[16,128,1024]{2,1,0:T(8,128)(2,1)}, u32[]{:S(2)}, u32[]{:S(2)}) async-start(bf16[16,128,1024]{2,1,0:T(8,128)(2,1)} %bitcast.126), calls=%async_computation | async-start | bytes 8388608 | tf_op jit(solution)/shard_map/all_to_all | solution.py:38
  26.9 6.0 fusion.38
  32.9 79.9 %collective-permute-done.2 = bf16[1024,1024]{1,0:T(8,128)(2,1)} collective-permute-done((bf16[1024,1024]{1,0:T(8,128)(2,1)S(1)}, bf16[1024,1024]{1,0:T(8,128)(2,1)}, u32[]{:S(2)}, u32[]{:S(2)}) %collective-permute-start.2) | collective-permute-done | bytes 2097184 | tf_op jit(solution)/shard_map/ppermute | solution.py:44
  112.8 43.5 %collective-permute-done.3 = bf16[1024,1024]{1,0:T(8,128)(2,1)} collective-permute-done((bf16[1024,1024]{1,0:T(8,128)(2,1)S(1)}, bf16[1024,1024]{1,0:T(8,128)(2,1)}, u32[]{:S(2)}, u32[]{:S(2)}) %collective-permute-start.3) | collective-permute-done | bytes 2097184 | tf_op jit(solution)/shard_map/ppermute | solution.py:44
  156.3 7.7 %all-to-all-start.2 = ((bf16[16,128,1024]{2,1,0:T(8,128)(2,1)}), bf16[16,128,1024]{2,1,0:T(8,128)(2,1)}, u32[]{:S(2)}, u32[]{:S(2)}) async-start(bf16[16,128,1024]{2,1,0:T(8,128)(2,1)} %bitcast.125), calls=%async_computation.2 | async-start | bytes 8388608 | tf_op jit(solution)/shard_map/all_to_all | solution.py:38
  164.1 3.8 multiply_reduce_fusion.4
  170.9 3.3 add_convert_fusion.1
  174.2 4.8 add_convert_fusion.2
  179.0 7.0 %multiply_convert_fusion.8 = (bf16[2048,1024]{1,0:T(8,128)(2,1)S(1)}, f32[2048,1024]{1,0:T(8,128)}) fusion(bf16[2048,1024]{1,0:T(8,128)(2,1)S(1)} %bitcast.123, bf16[1024,1024]{1,0:T(8,128)(2,1)S(1)} %get-tuple-element.22), kind=kOutput, calls=%fused_computation.52 | convolution fusion | flops 4305453056 | bytes 18874368 | tf_op jit(solution)/shard_map/dot_general | solution.py:70
  186.0 9.7 %multiply_convert_fusion.6 = (bf16[2048,1024]{1,0:T(8,128)(2,1)S(1)}, f32[2048,1024]{1,0:T(8,128)}) fusion(bf16[2048,1024]{1,0:T(8,128)(2,1)S(1)} %add_convert_fusion.1, bf16[1024,1024]{1,0:T(8,128)(2,1)} %collective-permute-done.2), kind=kOutput, calls=%fused_computation.47 | convolution fusion | flops 4305453056 | bytes 18874368 | tf_op jit(solution)/shard_map/dot_general | solution.py:70
  195.8 9.8 %multiply_convert_fusion.7 = (bf16[2048,1024]{1,0:T(8,128)(2,1)S(1)}, f32[2048,1024]{1,0:T(8,128)}) fusion(bf16[2048,1024]{1,0:T(8,128)(2,1)S(1)} %add_convert_fusion.1, bf16[1024,1024]{1,0:T(8,128)(2,1)} %collective-permute-done), kind=kOutput, calls=%fused_computation.49 | convolution fusion | flops 4305453056 | bytes 18874368 | tf_op jit(solution)/shard_map/dot_general | solution.py:70
  205.6 9.8 %fusion.46 = f32[2048,1024]{1,0:T(8,128)} fusion(bf16[2048,1024]{1,0:T(8,128)(2,1)S(1)} %get-tuple-element.37, bf16[1024,1024]{1,0:T(8,128)(2,1)} %get-tuple-element.20), kind=kOutput, calls=%fused_computation.123 | convolution fusion | flops 4294967296 | bytes 14680064 | tf_op jit(solution)/shard_map/dot_general | solution.py:76
  215.3 8.3 %fusion.48 = f32[2048,1024]{1,0:T(8,128)} fusion(bf16[2048,1024]{1,0:T(8,128)(2,1)S(1)} %get-tuple-element.35, bf16[1024,1024]{1,0:T(8,128)(2,1)} %collective-permute-done.3), kind=kOutput, calls=%fused_computation.125 | convolution fusion | flops 4294967296 | bytes 14680064 | tf_op jit(solution)/shard_map/dot_general | solution.py:76
  223.7 8.3 %fusion.47 = f32[2048,1024]{1,0:T(8,128)} fusion(bf16[2048,1024]{1,0:T(8,128)(2,1)S(1)} %get-tuple-element.39, bf16[1024,1024]{1,0:T(8,128)(2,1)} %collective-permute-done.1), kind=kOutput, calls=%fused_computation.124 | convolution fusion | flops 4294967296 | bytes 14680064 | tf_op jit(solution)/shard_map/dot_general | solution.py:76
  232.0 9.1 %multiply_convert_fusion.5 = (bf16[2048,1024]{1,0:T(8,128)(2,1)}, f32[2048,1024]{1,0:T(8,128)}) fusion(bf16[2048,1024]{1,0:T(8,128)(2,1)S(1)} %add_convert_fusion.1, bf16[1024,1024]{1,0:T(8,128)(2,1)} %collective-permute-done.4), kind=kOutput, calls=%fused_computation.44 | convolution fusion | flops 4305453056 | bytes 18874368 | tf_op jit(solution)/shard_map/dot_general | solution.py:70
  241.1 4.1 all-to-all-done.2
  245.2 16.3 %fusion.22 = (f32[2048]{0:T(1024)S(1)}, bf16[2048,1024]{1,0:T(8,128)(2,1)}, bf16[2048,1024]{1,0:T(8,128)(2,1)S(1)}) fusion(bf16[16,128,1024]{2,1,0:T(8,128)(2,1)} %all-to-all-done.2, f32[2048]{0:T(1024)S(1)} %fusion.45, bf16[2048,1024]{1,0:T(8,128)(2,1)} %get-tuple-element.41, bf16[1024,1024]{1,0:T(8,128)(2,1)} %collective-permute-done.5, ...), kind=kOutput, calls=%fused_computation.31 | convolution fusion | flops 4315936768 | bytes 44056576 | tf_op jit(solution)/shard_map/dot_general | solution.py:76
  261.5 4.4 fusion.20
  266.0 9.5 %multiply_convert_fusion.3 = bf16[2048,1024]{1,0:T(8,128)(2,1)S(1)} fusion(bf16[2048,1024]{1,0:T(8,128)(2,1)S(1)} %bitcast.124, bf16[1024,1024]{1,0:T(8,128)(2,1)} %get-tuple-element.20, f32[2048,1024]{1,0:T(8,128)} %get-tuple-element.38), kind=kOutput, calls=%fused_computation.42 | convolution fusion | flops 4320133120 | bytes 18874368 | tf_op jit(solution)/shard_map/dot_general | solution.py:86
  275.5 7.1 %fusion.49 = f32[2048,1024]{1,0:T(8,128)} fusion(bf16[2048,1024]{1,0:T(8,128)(2,1)S(1)} %multiply_convert_fusion.3, bf16[1024,1024]{1,0:T(8,128)(2,1)S(1)} %get-tuple-element.22), kind=kOutput, calls=%fused_computation.126 | convolution fusion | flops 4294967296 | bytes 14680064 | tf_op jit(solution)/shard_map/dot_general | solution.py:89
  282.6 10.8 %multiply_convert_fusion = bf16[2048,1024]{1,0:T(8,128)(2,1)} fusion(bf16[2048,1024]{1,0:T(8,128)(2,1)S(1)} %get-tuple-element.19, bf16[1024,1024]{1,0:T(8,128)(2,1)} %collective-permute-done.5, f32[2048,1024]{1,0:T(8,128)} %get-tuple-element.42), kind=kOutput, calls=%fused_computation.38 | convolution fusion | flops 4320133120 | bytes 18874368 | tf_op jit(solution)/shard_map/dot_general | solution.py:86
  293.4 9.0 %multiply_convert_fusion.1 = bf16[2048,1024]{1,0:T(8,128)(2,1)S(1)} fusion(bf16[2048,1024]{1,0:T(8,128)(2,1)S(1)} %get-tuple-element.19, bf16[1024,1024]{1,0:T(8,128)(2,1)} %collective-permute-done.3, f32[2048,1024]{1,0:T(8,128)S(1)} %bitcast.144), kind=kOutput, calls=%fused_computation.40 | convolution fusion | flops 4320133120 | bytes 18874368 | tf_op jit(solution)/shard_map/dot_general | solution.py:86
  302.5 9.7 %multiply_convert_fusion.2 = bf16[2048,1024]{1,0:T(8,128)(2,1)S(1)} fusion(bf16[2048,1024]{1,0:T(8,128)(2,1)S(1)} %get-tuple-element.19, bf16[1024,1024]{1,0:T(8,128)(2,1)} %collective-permute-done.1, f32[2048,1024]{1,0:T(8,128)S(1)} %bitcast.146), kind=kOutput, calls=%fused_computation.41 | convolution fusion | flops 4320133120 | bytes 18874368 | tf_op jit(solution)/shard_map/dot_general | solution.py:86
  312.2 10.0 %fusion.50 = f32[2048,1024]{1,0:T(8,128)} fusion(bf16[2048,1024]{1,0:T(8,128)(2,1)S(1)} %multiply_convert_fusion.2, bf16[1024,1024]{1,0:T(8,128)(2,1)} %collective-permute-done), kind=kOutput, calls=%fused_computation.127 | convolution fusion | flops 4294967296 | bytes 14680064 | tf_op jit(solution)/shard_map/dot_general | solution.py:89
  322.2 8.6 %fusion.51 = f32[2048,1024]{1,0:T(8,128)} fusion(bf16[2048,1024]{1,0:T(8,128)(2,1)S(1)} %multiply_convert_fusion.1, bf16[1024,1024]{1,0:T(8,128)(2,1)} %collective-permute-done.2), kind=kOutput, calls=%fused_computation.128 | convolution fusion | flops 4294967296 | bytes 14680064 | tf_op jit(solution)/shard_map/dot_general | solution.py:89
  330.9 16.0 %multiply_reduce_fusion.1 = (f32[1024]{0:T(1024)S(1)}, f32[2048]{0:T(1024)S(1)}, f32[2048]{0:T(1024)S(1)}, f32[1024]{0:T(1024)S(1)}, f32[2048,1024]{1,0:T(8,128)}) fusion(bf16[16,128,1024]{2,1,0:T(8,128)(2,1)} %all-to-all-done, f32[2048]{0:T(1024)S(1)} %copy-done.12, f32[2048]{0:T(1024)S(1)} %copy-done.10, f32[1024]{0:T(1024)S(1)} %bitcast.129, ...), kind=kOutput, calls=%fused_computation.35 | convolution fusion | flops 4322224128 | bytes 44085248 | tf_op jit(solution)/shard_map/dot_general | solution.py:89
  346.9 7.5 %add_convert_fusion = bf16[2048,1024]{1,0:T(8,128)(2,1)} fusion(bf16[16,128,1024]{2,1,0:T(8,128)(2,1)} %all-to-all-done, f32[2048,1024]{1,0:T(8,128)} %get-tuple-element.43, f32[1024]{0:T(1024)S(1)} %bitcast.134, f32[2048]{0:T(1024)S(1)} %subtract_multiply_fusion, f32[2048]{0:T(1024)S(1)} %broadcast_multiply_fusion, f32[2048]{0:T(1024)S(1)} %broadcast_multiply_fusion.1, ...), kind=kLoop, calls=%fused_computation.36 | loop fusion | flops 23068672 | bytes 16826368 | tf_op jit(solution)/shard_map/convert_element_type | solution.py:98
  354.4 21.2 %all-to-all-start.3 = ((bf16[16,128,1024]{2,1,0:T(8,128)(2,1)}), bf16[16,128,1024]{2,1,0:T(8,128)(2,1)}, u32[]{:S(2)}, u32[]{:S(2)}) async-start(bf16[16,128,1024]{2,1,0:T(8,128)(2,1)} %bitcast.122), calls=%async_computation.3 | async-start | bytes 8388608 | tf_op jit(solution)/shard_map/all_to_all | solution.py:38
  375.6 9.5 %convolution_convert_fusion = bf16[1024,1024]{1,0:T(8,128)(2,1)} fusion(bf16[2048,1024]{1,0:T(8,128)(2,1)} %get-tuple-element.41, bf16[2048,1024]{1,0:T(8,128)(2,1)} %copy-done), kind=kOutput, calls=%fused_computation.92 | convolution fusion | flops 4296015872 | bytes 10485760 | tf_op jit(solution)/shard_map/dot_general | solution.py:107
  385.2 5.9 convolution_convert_fusion.1
  391.0 5.7 convolution_convert_fusion.2
  396.8 5.7 convolution_convert_fusion.3
  403.5 3.1 multiply_reduce_fusion
  406.6 47.7 %all-to-all-done.3 = bf16[16,128,1024]{2,1,0:T(8,128)(2,1)} async-done(((bf16[16,128,1024]{2,1,0:T(8,128)(2,1)}), bf16[16,128,1024]{2,1,0:T(8,128)(2,1)}, u32[]{:S(2)}, u32[]{:S(2)}) %all-to-all-start.3) | async-done | bytes 4194336 | tf_op jit(solution)/shard_map/all_to_all | solution.py:38
  454.3 19.6 %all-to-all-start.1 = ((bf16[16,128,1024]{2,1,0:T(8,128)(2,1)}), bf16[16,128,1024]{2,1,0:T(8,128)(2,1)}, u32[]{:S(2)}, u32[]{:S(2)}) async-start(bf16[16,128,1024]{2,1,0:T(8,128)(2,1)} %bitcast.121), calls=%async_computation.1 | async-start | bytes 8388608 | tf_op jit(solution)/shard_map/all_to_all | solution.py:38
  474.0 21.0 %psum.7 = f32[2,3,1024]{2,0,1:T(2,128)S(1)} all-reduce(f32[2,3,1024]{2,0,1:T(2,128)S(1)} %broadcast_select_fusion), channel_id=1, replica_groups=mesh['expert'=8,'half'=2,'sub'=2] {'half','sub'}, use_global_device_ids=true, to_apply=%region_10.11 | all-reduce | flops 6144 | bytes 49152 | tf_op jit(solution)/shard_map/psum | solution.py:120
  495.1 7.7 %fusion.53 = f32[1024,1024]{1,0:T(8,128)S(1)} fusion(bf16[2048,1024]{1,0:T(8,128)(2,1)} %copy-done.29, bf16[2048,1024]{1,0:T(8,128)(2,1)} %copy-done), kind=kOutput, calls=%fused_computation.130 | convolution fusion | flops 4294967296 | bytes 12582912 | tf_op jit(solution)/shard_map/dot_general | solution.py:107
  502.8 6.2 add_convert_fusion.3
  509.2 7.1 %add_convert_fusion.4 = bf16[1024,1024]{1,0:T(8,128)(2,1)} fusion(bf16[1024,1024]{1,0:T(8,128)(2,1)} %collective-permute-done.7, bf16[2048,1024]{1,0:T(8,128)(2,1)S(1)} %copy-done.5, bf16[2048,1024]{1,0:T(8,128)(2,1)S(1)} %copy-done.28), kind=kOutput, calls=%fused_computation.76 | convolution fusion | flops 4298113024 | bytes 12582912 | tf_op jit(solution)/shard_map/dot_general | solution.py:110
  518.8 4.8 fusion.52
  523.6 64.8 %collective-permute-done.11 = bf16[1024,1024]{1,0:T(8,128)(2,1)} collective-permute-done((bf16[1024,1024]{1,0:T(8,128)(2,1)S(1)}, bf16[1024,1024]{1,0:T(8,128)(2,1)}, u32[]{:S(2)}, u32[]{:S(2)}) %collective-permute-start.11) | collective-permute-done | bytes 2097184 | tf_op jit(solution)/shard_map/ppermute | solution.py:44
  588.3 3.9 fusion.30
  592.3 4.2 pad_maximum_fusion.1
  596.5 36.0 %collective-permute-done.8 = bf16[1024,1024]{1,0:T(8,128)(2,1)S(1)} collective-permute-done((bf16[1024,1024]{1,0:T(8,128)(2,1)}, bf16[1024,1024]{1,0:T(8,128)(2,1)S(1)}, u32[]{:S(2)}, u32[]{:S(2)}) %collective-permute-start.8) | collective-permute-done | bytes 2097184 | tf_op jit(solution)/shard_map/ppermute | solution.py:44
  634.2 4.3 pad_maximum_fusion
  638.5 8.6 %convert_add_fusion.2 = f32[1024,1024]{1,0:T(8,128)} fusion(bf16[1024,1024]{1,0:T(8,128)(2,1)S(1)} %copy-done.23, bf16[2048,1024]{1,0:T(8,128)(2,1)} %bitcast.22, s32[1024]{0:T(1024)S(1)} %bitcast.141), kind=kOutput, calls=%fused_computation.78 | convolution fusion | flops 4299161600 | bytes 10489856 | tf_op jit(solution)/shard_map/dot_general | solution.py:34
  647.1 8.0 %add_convert_fusion.5 = bf16[1024,1024]{1,0:T(8,128)(2,1)} fusion(bf16[1024,1024]{1,0:T(8,128)(2,1)S(1)} %copy-done.24, bf16[2048,1024]{1,0:T(8,128)(2,1)} %bitcast.17, s32[1024]{0:T(1024)S(1)} %bitcast.142), kind=kOutput, calls=%fused_computation.79 | convolution fusion | flops 4300210176 | bytes 8392704 | tf_op jit(solution)/shard_map/dot_general | solution.py:34
  (124 shorter events, 18.7 us)
Async XLA Ops:
  10.8 145.6 %all-to-all-start = ((bf16[16,128,1024]{2,1,0:T(8,128)(2,1)}), bf16[16,128,1024]{2,1,0:T(8,128)(2,1)}, u32[]{:S(2)}, u32[]{:S(2)}) async-start(bf16[16,128,1024]{2,1,0:T(8,128)(2,1)} %bitcast.126), calls=%async_computation | async-start | bytes 8388608 | tf_op jit(solution)/shard_map/all_to_all | solution.py:38
  22.1 90.7 %collective-permute-start.2 = (bf16[1024,1024]{1,0:T(8,128)(2,1)S(1)}, bf16[1024,1024]{1,0:T(8,128)(2,1)}, u32[]{:S(2)}, u32[]{:S(2)}) collective-permute-start(bf16[1024,1024]{1,0:T(8,128)(2,1)S(1)} %get-tuple-element.23), channel_id=1, source_target_pairs={{0,2},{2,0},{1,3},{3,1},{4,6},{6,4},{5,7},{7,5},{8,10},{10,8},{9,1... | collective-permute-start | bytes 6291464 | tf_op jit(solution)/shard_map/ppermute | solution.py:44
  25.7 130.6 %collective-permute-start.3 = (bf16[1024,1024]{1,0:T(8,128)(2,1)S(1)}, bf16[1024,1024]{1,0:T(8,128)(2,1)}, u32[]{:S(2)}, u32[]{:S(2)}) collective-permute-start(bf16[1024,1024]{1,0:T(8,128)(2,1)S(1)} %get-tuple-element.21), channel_id=1, source_target_pairs={{0,2},{2,0},{1,3},{3,1},{4,6},{6,4},{5,7},{7,5},{8,10},{10,8},{9,1... | collective-permute-start | bytes 6291464 | tf_op jit(solution)/shard_map/ppermute | solution.py:44
  26.3 169.5 %collective-permute-start = (bf16[1024,1024]{1,0:T(8,128)(2,1)S(1)}, bf16[1024,1024]{1,0:T(8,128)(2,1)}, u32[]{:S(2)}, u32[]{:S(2)}) collective-permute-start(bf16[1024,1024]{1,0:T(8,128)(2,1)S(1)} %get-tuple-element.22), channel_id=1, source_target_pairs={{0,1},{1,0},{2,3},{3,2},{4,5},{5,4},{6,7},{7,6},{8,9},{9,8},{10,11... | collective-permute-start | bytes 6291464 | tf_op jit(solution)/shard_map/ppermute | solution.py:44
  26.3 197.4 %collective-permute-start.1 = (bf16[1024,1024]{1,0:T(8,128)(2,1)}, bf16[1024,1024]{1,0:T(8,128)(2,1)}, u32[]{:S(2)}, u32[]{:S(2)}) collective-permute-start(bf16[1024,1024]{1,0:T(8,128)(2,1)} %get-tuple-element.20), channel_id=1, source_target_pairs={{0,1},{1,0},{2,3},{3,2},{4,5},{5,4},{6,7},{7,6},{8,9},{9,8},{10,11... | collective-permute-start | bytes 6291464 | tf_op jit(solution)/shard_map/ppermute | solution.py:44
  26.8 137.2 %copy-start.15 = (f32[1,1024]{1,0:T(1,128)}, f32[1,1024]{1,0:T(1,128)S(1)}, u32[]{:S(2)}) copy-start(f32[1,1024]{1,0:T(1,128)S(1)} %get-tuple-element.45) | copy-start | bytes 12292
  26.8 147.4 %copy-start.13 = (f32[1,1024]{1,0:T(1,128)}, f32[1,1024]{1,0:T(1,128)S(1)}, u32[]{:S(2)}) copy-start(f32[1,1024]{1,0:T(1,128)S(1)} %get-tuple-element.44) | copy-start | bytes 12292
  112.8 119.2 %collective-permute-start.4 = (bf16[1024,1024]{1,0:T(8,128)(2,1)}, bf16[1024,1024]{1,0:T(8,128)(2,1)}, u32[]{:S(2)}, u32[]{:S(2)}) collective-permute-start(bf16[1024,1024]{1,0:T(8,128)(2,1)} %collective-permute-done.2), channel_id=1, source_target_pairs={{0,1},{1,0},{2,3},{3,2},{4,5},{5,4},{6,7},{7,6},{8,9},{9,8},{10,11... | collective-permute-start | bytes 6291464 | tf_op jit(solution)/shard_map/ppermute | solution.py:44
  156.3 84.8 %collective-permute-start.5 = (bf16[1024,1024]{1,0:T(8,128)(2,1)}, bf16[1024,1024]{1,0:T(8,128)(2,1)}, u32[]{:S(2)}, u32[]{:S(2)}) collective-permute-start(bf16[1024,1024]{1,0:T(8,128)(2,1)} %collective-permute-done.3), channel_id=1, source_target_pairs={{0,1},{1,0},{2,3},{3,2},{4,5},{5,4},{6,7},{7,6},{8,9},{9,8},{10,11... | collective-permute-start | bytes 6291464 | tf_op jit(solution)/shard_map/ppermute | solution.py:44
  156.3 88.9 %all-to-all-start.2 = ((bf16[16,128,1024]{2,1,0:T(8,128)(2,1)}), bf16[16,128,1024]{2,1,0:T(8,128)(2,1)}, u32[]{:S(2)}, u32[]{:S(2)}) async-start(bf16[16,128,1024]{2,1,0:T(8,128)(2,1)} %bitcast.125), calls=%async_computation.2 | async-start | bytes 8388608 | tf_op jit(solution)/shard_map/all_to_all | solution.py:38
  167.9 6.3 copy-start.9
  174.2 57.8 %copy-start.3 = (bf16[2048,1024]{1,0:T(8,128)(2,1)}, bf16[2048,1024]{1,0:T(8,128)(2,1)S(1)}, u32[]{:S(2)}) copy-start(bf16[2048,1024]{1,0:T(8,128)(2,1)S(1)} %add_convert_fusion.1) | copy-start | bytes 12582916
  186.0 19.6 %copy-start.29 = (bf16[2048,1024]{1,0:T(8,128)(2,1)}, bf16[2048,1024]{1,0:T(8,128)(2,1)S(1)}, u32[]{:S(2)}) copy-start(bf16[2048,1024]{1,0:T(8,128)(2,1)S(1)} %get-tuple-element.37) | copy-start | bytes 12582916
  195.7 19.6 %copy-start.25 = (bf16[2048,1024]{1,0:T(8,128)(2,1)}, bf16[2048,1024]{1,0:T(8,128)(2,1)S(1)}, u32[]{:S(2)}) copy-start(bf16[2048,1024]{1,0:T(8,128)(2,1)S(1)} %get-tuple-element.35) | copy-start | bytes 12582916
  205.6 18.1 %copy-start.32 = (bf16[2048,1024]{1,0:T(8,128)(2,1)}, bf16[2048,1024]{1,0:T(8,128)(2,1)S(1)}, u32[]{:S(2)}) copy-start(bf16[2048,1024]{1,0:T(8,128)(2,1)S(1)} %get-tuple-element.39) | copy-start | bytes 12582916
  261.5 40.9 %copy-start = (bf16[2048,1024]{1,0:T(8,128)(2,1)}, bf16[2048,1024]{1,0:T(8,128)(2,1)S(1)}, u32[]{:S(2)}) copy-start(bf16[2048,1024]{1,0:T(8,128)(2,1)S(1)} %get-tuple-element.19) | copy-start | bytes 12582916
  275.5 7.1 %copy-start.30 = (bf16[2048,1024]{1,0:T(8,128)(2,1)}, bf16[2048,1024]{1,0:T(8,128)(2,1)S(1)}, u32[]{:S(2)}) copy-start(bf16[2048,1024]{1,0:T(8,128)(2,1)S(1)} %multiply_convert_fusion.3) | copy-start | bytes 12582916
  275.5 17.9 %slice-start = ((s8[8388608]{0:T(1024)(128)(4,1)}), s8[4194304]{0:T(1024)(128)(4,1)S(1)}, s32[]{:S(2)}) async-start(s8[8388608]{0:T(1024)(128)(4,1)} %bitcast.143), calls=%async_computation.4 | async-start | bytes 8388608
  282.6 10.8 %slice-start.1 = ((s8[8388608]{0:T(1024)(128)(4,1)}), s8[4194304]{0:T(1024)(128)(4,1)S(1)}, s32[]{:S(2)}) async-start(s8[8388608]{0:T(1024)(128)(4,1)} %bitcast.143), calls=%async_computation.5 | async-start | bytes 8388608
  282.6 19.9 %slice-start.2 = ((s8[8388608]{0:T(1024)(128)(4,1)}), s8[4194304]{0:T(1024)(128)(4,1)S(1)}, s32[]{:S(2)}) async-start(s8[8388608]{0:T(1024)(128)(4,1)} %bitcast.145), calls=%async_computation.6 | async-start | bytes 8388608
  293.4 9.1 %slice-start.3 = ((s8[8388608]{0:T(1024)(128)(4,1)}), s8[4194304]{0:T(1024)(128)(4,1)S(1)}, s32[]{:S(2)}) async-start(s8[8388608]{0:T(1024)(128)(4,1)} %bitcast.145), calls=%async_computation.7 | async-start | bytes 8388608
  302.4 19.7 %copy-start.27 = (bf16[2048,1024]{1,0:T(8,128)(2,1)}, bf16[2048,1024]{1,0:T(8,128)(2,1)S(1)}, u32[]{:S(2)}) copy-start(bf16[2048,1024]{1,0:T(8,128)(2,1)S(1)} %multiply_convert_fusion.1) | copy-start | bytes 12582916
  312.2 10.0 %copy-start.34 = (bf16[2048,1024]{1,0:T(8,128)(2,1)}, bf16[2048,1024]{1,0:T(8,128)(2,1)S(1)}, u32[]{:S(2)}) copy-start(bf16[2048,1024]{1,0:T(8,128)(2,1)S(1)} %multiply_convert_fusion.2) | copy-start | bytes 12582916
  322.2 8.7 %copy-start.7 = (bf16[2048,1024]{1,0:T(8,128)(2,1)S(1)}, bf16[2048,1024]{1,0:T(8,128)(2,1)}, u32[]{:S(2)}) copy-start(bf16[2048,1024]{1,0:T(8,128)(2,1)} %multiply_convert_fusion) | copy-start | bytes 12582916
  322.2 8.7 %copy-start.10 = (f32[2048]{0:T(1024)S(1)}, f32[2048]{0:T(1024)}, u32[]{:S(2)}) copy-start(f32[2048]{0:T(1024)} %copy-done.9) | copy-start | bytes 24580
  322.2 8.7 %copy-start.12 = (f32[2048]{0:T(1024)S(1)}, f32[2048]{0:T(1024)}, u32[]{:S(2)}) copy-start(f32[2048]{0:T(1024)} %copy-done.11) | copy-start | bytes 24580
  322.2 8.7 %copy-start.14 = (f32[1,1024]{1,0:T(1,128)S(1)}, f32[1,1024]{1,0:T(1,128)}, u32[]{:S(2)}) copy-start(f32[1,1024]{1,0:T(1,128)} %copy-done.13) | copy-start | bytes 12292
  330.9 16.0 %copy-start.16 = (f32[1,1024]{1,0:T(1,128)S(1)}, f32[1,1024]{1,0:T(1,128)}, u32[]{:S(2)}) copy-start(f32[1,1024]{1,0:T(1,128)} %copy-done.15) | copy-start | bytes 12292
  354.4 21.2 %copy-start.17 = (s32[1024,1]{0,1:T(1,128)S(1)}, s32[1024,1]{0,1:T(1,128)}, u32[]{:S(2)}) copy-start(s32[1024,1]{0,1:T(1,128)} %param.9) | copy-start | bytes 12292
  354.4 21.2 %copy-start.18 = (s32[1024]{0:T(1024)S(1)}, s32[1024]{0:T(1024)}, u32[]{:S(2)}) copy-start(s32[1024]{0:T(1024)} %get-tuple-element.33) | copy-start | bytes 12292
  354.4 100.0 %all-to-all-start.3 = ((bf16[16,128,1024]{2,1,0:T(8,128)(2,1)}), bf16[16,128,1024]{2,1,0:T(8,128)(2,1)}, u32[]{:S(2)}, u32[]{:S(2)}) async-start(bf16[16,128,1024]{2,1,0:T(8,128)(2,1)} %bitcast.122), calls=%async_computation.3 | async-start | bytes 8388608 | tf_op jit(solution)/shard_map/all_to_all | solution.py:38
  375.6 9.5 %copy-start.1 = (bf16[2048,1024]{1,0:T(8,128)(2,1)S(1)}, bf16[2048,1024]{1,0:T(8,128)(2,1)}, u32[]{:S(2)}) copy-start(bf16[2048,1024]{1,0:T(8,128)(2,1)} %copy-done) | copy-start | bytes 12582916
  375.6 9.5 %copy-start.33 = (bf16[2048,1024]{1,0:T(8,128)(2,1)S(1)}, bf16[2048,1024]{1,0:T(8,128)(2,1)}, u32[]{:S(2)}) copy-start(bf16[2048,1024]{1,0:T(8,128)(2,1)} %copy-done.32) | copy-start | bytes 12582916
  385.1 5.9 copy-start.4
  385.1 5.9 copy-start.8
  385.1 117.7 %collective-permute-start.10 = (bf16[1024,1024]{1,0:T(8,128)(2,1)}, bf16[1024,1024]{1,0:T(8,128)(2,1)}, u32[]{:S(2)}, u32[]{:S(2)}) collective-permute-start(bf16[1024,1024]{1,0:T(8,128)(2,1)} %convolution_convert_fusion), channel_id=1, source_target_pairs={{0,1},{1,0},{2,3},{3,2},{4,5},{5,4},{6,7},{7,6},{8,9},{9,8},{10,11... | collective-permute-start | bytes 6291464 | tf_op jit(solution)/shard_map/ppermute | solution.py:44
  402.5 121.0 %collective-permute-start.9 = (bf16[1024,1024]{1,0:T(8,128)(2,1)}, bf16[1024,1024]{1,0:T(8,128)(2,1)}, u32[]{:S(2)}, u32[]{:S(2)}) collective-permute-start(bf16[1024,1024]{1,0:T(8,128)(2,1)} %convolution_convert_fusion.1), channel_id=1, source_target_pairs={{0,1},{1,0},{2,3},{3,2},{4,5},{5,4},{6,7},{7,6},{8,9},{9,8},{10,11... | collective-permute-start | bytes 6291464 | tf_op jit(solution)/shard_map/ppermute | solution.py:44
  403.0 106.1 %collective-permute-start.7 = (bf16[1024,1024]{1,0:T(8,128)(2,1)}, bf16[1024,1024]{1,0:T(8,128)(2,1)}, u32[]{:S(2)}, u32[]{:S(2)}) collective-permute-start(bf16[1024,1024]{1,0:T(8,128)(2,1)} %convolution_convert_fusion.2), channel_id=1, source_target_pairs={{0,1},{1,0},{2,3},{3,2},{4,5},{5,4},{6,7},{7,6},{8,9},{9,8},{10,11... | collective-permute-start | bytes 6291464 | tf_op jit(solution)/shard_map/ppermute | solution.py:44
  403.0 193.5 %collective-permute-start.6 = (bf16[1024,1024]{1,0:T(8,128)(2,1)}, bf16[1024,1024]{1,0:T(8,128)(2,1)S(1)}, u32[]{:S(2)}, u32[]{:S(2)}) collective-permute-start(bf16[1024,1024]{1,0:T(8,128)(2,1)} %convolution_convert_fusion.3), channel_id=1, source_target_pairs={{0,1},{1,0},{2,3},{3,2},{4,5},{5,4},{6,7},{7,6},{8,9},{9,8},{10,11... | collective-permute-start | bytes 6291464 | tf_op jit(solution)/shard_map/ppermute | solution.py:44
  454.3 192.7 %all-to-all-start.1 = ((bf16[16,128,1024]{2,1,0:T(8,128)(2,1)}), bf16[16,128,1024]{2,1,0:T(8,128)(2,1)}, u32[]{:S(2)}, u32[]{:S(2)}) async-start(bf16[16,128,1024]{2,1,0:T(8,128)(2,1)} %bitcast.121), calls=%async_computation.1 | async-start | bytes 8388608 | tf_op jit(solution)/shard_map/all_to_all | solution.py:38
  495.0 7.8 %copy-start.2 = (bf16[2048,1024]{1,0:T(8,128)(2,1)S(1)}, bf16[2048,1024]{1,0:T(8,128)(2,1)}, u32[]{:S(2)}) copy-start(bf16[2048,1024]{1,0:T(8,128)(2,1)} %copy-done) | copy-start | bytes 12582916
  495.0 7.8 %copy-start.26 = (bf16[2048,1024]{1,0:T(8,128)(2,1)S(1)}, bf16[2048,1024]{1,0:T(8,128)(2,1)}, u32[]{:S(2)}) copy-start(bf16[2048,1024]{1,0:T(8,128)(2,1)} %copy-done.25) | copy-start | bytes 12582916
  502.8 6.4 copy-start.5
  502.8 6.4 copy-start.28
  509.1 9.7 %copy-start.31 = (bf16[2048,1024]{1,0:T(8,128)(2,1)S(1)}, bf16[2048,1024]{1,0:T(8,128)(2,1)}, u32[]{:S(2)}) copy-start(bf16[2048,1024]{1,0:T(8,128)(2,1)} %copy-done.30) | copy-start | bytes 12582916
  509.1 79.2 %collective-permute-start.11 = (bf16[1024,1024]{1,0:T(8,128)(2,1)S(1)}, bf16[1024,1024]{1,0:T(8,128)(2,1)}, u32[]{:S(2)}, u32[]{:S(2)}) collective-permute-start(bf16[1024,1024]{1,0:T(8,128)(2,1)S(1)} %add_convert_fusion.3), channel_id=1, source_target_pairs={{0,2},{2,0},{1,3},{3,1},{4,6},{6,4},{5,7},{7,5},{8,10},{10,8},{9,1... | collective-permute-start | bytes 6291464 | tf_op jit(solution)/shard_map/ppermute | solution.py:44
  516.3 116.2 %collective-permute-start.8 = (bf16[1024,1024]{1,0:T(8,128)(2,1)}, bf16[1024,1024]{1,0:T(8,128)(2,1)S(1)}, u32[]{:S(2)}, u32[]{:S(2)}) collective-permute-start(bf16[1024,1024]{1,0:T(8,128)(2,1)} %add_convert_fusion.4), channel_id=1, source_target_pairs={{0,2},{2,0},{1,3},{3,1},{4,6},{6,4},{5,7},{7,5},{8,10},{10,8},{9,1... | collective-permute-start | bytes 6291464 | tf_op jit(solution)/shard_map/ppermute | solution.py:44
  638.5 8.6 %copy-start.24 = (bf16[1024,1024]{1,0:T(8,128)(2,1)S(1)}, bf16[1024,1024]{1,0:T(8,128)(2,1)}, u32[]{:S(2)}) copy-start(bf16[1024,1024]{1,0:T(8,128)(2,1)} %param.8) | copy-start | bytes 6291460
  (8 other events, 37.3 us)

commit v2 on v1

v2 whole, which is shorter than its diff:
```python
import functools

import jax
import jax.numpy as jnp
from jax import lax
from jax.experimental import pallas as pl
from jax.experimental.pallas import tpu as pltpu
from jax.sharding import Mesh
from jax.sharding import PartitionSpec as P

epsilon = 1e-05
F32 = jnp.float32
BF16 = jnp.bfloat16
LAST = (((1,), (1,)), ((), ()))
ROWS = (((0,), (0,)), ((), ()))
VMEM_LIMIT = 58 * 2**20
TILE = 512


def product(a, b, dims=(((1,), (0,)), ((), ()))):
    return lax.dot_general(a, b, dims, preferred_element_type=F32)


def standardize(x):
    centered = x - jnp.mean(x, axis=-1, keepdims=True)
    inverse = lax.rsqrt(jnp.mean(centered * centered, axis=-1, keepdims=True) + epsilon)
    return centered * inverse, inverse


def steps_of(weights):
    for first, second in weights:
        step = min(TILE, first.shape[1]) if first.shape[1] % TILE == 0 else first.shape[1]
        for start in range(0, first.shape[1], step):
            yield first[:, start : start + step], second[start : start + step, :]


def through(normed, weights, hidden_ref, slope_ref):
    total, at = None, 0
    for first, second in steps_of(weights):
        z = product(normed, first)
        cumul = 0.5 * (1.0 + lax.erf(z * 0.7071067811865476))
        density = jnp.exp(-0.5 * z * z) * 0.3989422804014327
        hidden = (z * cumul).astype(BF16)
        hidden_ref[:, at : at + z.shape[1]] = hidden
        slope_ref[:, at : at + z.shape[1]] = (cumul + z * density).astype(BF16)
        part = product(hidden, second)
        total = part if total is None else total + part
        at += z.shape[1]
    return total


def paired(refs):
    return list(zip(refs[::2], refs[1::2]))


def forward_near(x, gain, bias, center, *rest):
    weights, (normed, hidden, slope, mixed, gates) = paired(rest[:-6]), rest[-5:]
    values = x[...].astype(F32)
    rows = (standardize(values)[0] * gain[...] + bias[...]).astype(BF16)
    normed[...] = rows
    mixed[...] = through(rows, weights, hidden, slope)
    gate = jax.nn.sigmoid(jnp.sum(values * center[...], axis=-1, keepdims=True))
    gates[...] = jnp.broadcast_to(gate, gates.shape)


def forward_more(rows, near, *rest):
    weights, (hidden, slope, mixed) = paired(rest[:-3]), rest[-3:]
    mixed[...] = near[...] + through(rows[...], weights, hidden, slope)


def forward_last(rows, near, gates, first, second, kept_hidden, kept_slope, hidden, slope, gated):
    del kept_hidden, kept_slope
    whole = near[...] + through(rows[...], [(first, second)], hidden, slope)
    gated[...] = (gates[:, :1] * whole).astype(BF16)


def backward(x, dy, gated, s1, s2, gates, gain, center, *rest):
    weights, (g1, g2, expert_grad, sums) = paired(rest[:-4]), rest[-4:]
    rows = x[...].astype(F32)
    gate = gates[:, :1]
    upper = dy[...].astype(F32)
    mixed_grad = (gate * upper).astype(BF16)
    total, at = None, 0
    for first, second in steps_of(weights):
        slope, grad, start = (s1, g1, at) if at < s1.shape[1] else (s2, g2, at - s1.shape[1])
        hidden_grad = product(mixed_grad, second, LAST)
        columns = pl.ds(start, second.shape[0])
        pre_grad = (hidden_grad * slope[:, columns].astype(F32)).astype(BF16)
        grad[:, columns] = pre_grad
        added = product(pre_grad, first, LAST)
        total = added if total is None else total + added
        at += second.shape[0]
    xhat, inverse = standardize(rows)
    logit_grad = jnp.sum(upper * gated[...].astype(F32), axis=-1, keepdims=True) * (1.0 - gate)
    u = total * gain[...]
    expert_grad[...] = (
        inverse
        * (u - jnp.mean(u, axis=-1, keepdims=True) - xhat * jnp.mean(u * xhat, axis=-1, keepdims=True))
        + logit_grad * center[...]
    ).astype(BF16)

    @pl.when(pl.program_id(0) == 0)
    def _():
        sums[...] = jnp.zeros_like(sums)

    sums[0:1, :] += jnp.sum(total * xhat, axis=0, keepdims=True)
    sums[1:2, :] += jnp.sum(total, axis=0, keepdims=True)
    sums[2:3, :] += jnp.sum(logit_grad * rows, axis=0, keepdims=True)


def call(kernel, name, steps, ins, outs, **more):
    def spec(shape, block, index):
        if block == "out":
            return pl.BlockSpec(memory_space=pl.ANY)
        if block is None:
            return pl.BlockSpec(shape, lambda *_: (0,) * len(shape), pipeline_mode=pl.Buffered(1))
        return pl.BlockSpec(block, index)

    return pl.pallas_call(
        kernel,
        grid=(steps,),
        in_specs=[spec(a.shape, block, index) for a, block, index in ins],
        out_specs=[pl.BlockSpec(block, index) for _, _, block, index in outs],
        out_shape=[jax.ShapeDtypeStruct(shape, dtype) for shape, dtype, _, _ in outs],
        compiler_params=pltpu.CompilerParams(vmem_limit_bytes=VMEM_LIMIT),
        cost_estimate=pl.CostEstimate(flops=1000, transcendentals=0, bytes_accessed=1000),
        name=name,
        **more,
    )(*[a for a, _, _ in ins])


def tiles(array, tile):
    return array, (tile, array.shape[1]), lambda i: (i, 0)


def rows_out(shape, dtype, tile):
    return shape, dtype, (tile, shape[1]), lambda i: (i, 0)


def whole(array):
    return array, None, None


def weight_grad(left, right, units, width, dtype, name, beside=None, apart=False):
    (a, i), (b, j) = left, right
    tile = min(TILE, units)
    steps = units // tile

    def kernel(a, b, *rest):
        total = product(a[...], b[...], ROWS).astype(dtype)
        if not apart and beside is None:
            rest[0][...] = total
        for n in range(steps if apart or beside is not None else 0):

            @pl.when(pl.program_id(0) == n)
            def _():
                if apart:
                    rest[n][...] = total
                else:
                    rest[-1][0] = total
                    rest[-1][1] = rest[n][...]

    ins = [
        (a, (a.shape[0], tile), lambda n: (0, i * steps + n)),
        (b, (b.shape[0], width), lambda n: (0, j)),
    ]
    if apart:
        return call(kernel, name, steps, ins, [((tile, width), dtype, (tile, width), lambda n: (0, 0))] * steps)
    if beside is None:
        return call(kernel, name, steps, ins, [rows_out((units, width), dtype, tile)])[0]
    out = (2, units, width), dtype, (2, tile, width), lambda n: (0, n, 0)
    return call(kernel, name, steps, ins + [whole(p) for p in beside], [out])[0]


def first_weight_grad(hidden, dy, gates, units, name):
    count, width = dy.shape
    tile = min(TILE, units)

    def kernel(a, dy, gates, out, mixed_grad):
        @pl.when(pl.program_id(0) == 0)
        def _():
            mixed_grad[...] = (gates[:, :1] * dy[...].astype(F32)).astype(BF16)

        out[...] = product(a[...], mixed_grad[...], ROWS).astype(BF16)

    return call(
        kernel,
        name,
        units // tile,
        [(hidden, (count, tile), lambda n: (0, n)), whole(dy), whole(gates)],
        [rows_out((units, width), BF16, tile), ((count, width), BF16, (count, width), lambda n: (0, 0))],
    )


def joined(half, own, beside, across, name):
    count, width = own.shape
    tile = min(256, count)

    def kernel(half, own, beside, *rest):
        across, out = rest[:-1], rest[-1]
        across = [a[...] for a in across] if len(across) == 2 else [across[0][0], across[0][1]]
        kept = own[...] + across[0].astype(F32)
        other = beside[...].astype(F32) + across[1].astype(F32)
        mine = half[0] == 0
        out[0] = jnp.where(mine, kept, other)
        out[1] = jnp.where(mine, other, kept)

    rows = pl.BlockSpec((tile, width), lambda i, _: (i, 0))
    both = pl.BlockSpec((2, tile, width), lambda i, _: (0, i, 0))
    return pl.pallas_call(
        kernel,
        grid_spec=pltpu.PrefetchScalarGridSpec(
            num_scalar_prefetch=1,
            grid=(count // tile,),
            in_specs=[rows, rows] + ([rows, rows] if len(across) == 2 else [both]),
            out_specs=both,
        ),
        out_shape=jax.ShapeDtypeStruct((2, count, width), F32),
        compiler_params=pltpu.CompilerParams(vmem_limit_bytes=VMEM_LIMIT),
        cost_estimate=pl.CostEstimate(flops=1000, transcendentals=0, bytes_accessed=1000),
        name=name,
    )(half.astype(jnp.int32)[None], own, beside, *across)


def taken_back(base, slot, arrived, dtype, name):
    count, width = base.shape
    tile = min(256, count)

    def kernel(base, slot, arrived, out):
        slots = lax.broadcasted_iota(jnp.int32, (tile, arrived.shape[0]), 1)
        chosen = jnp.where(slot[...] == slots, 1.0, 0.0).astype(BF16)
        out[...] = (base[...].astype(F32) + product(chosen, arrived[...])).astype(dtype)

    return call(
        kernel,
        name,
        count // tile,
        [tiles(base, tile), tiles(slot, tile), whole(arrived)],
        [rows_out((count, width), dtype, tile)],
    )[0]


def waited(array):
    def kernel(array, out):
        out[...] = array[...].astype(F32)

    return pl.pallas_call(
        kernel,
        grid=(1,),
        in_specs=[pl.BlockSpec((16, 128), lambda i: (0, 0))],
        out_specs=pl.BlockSpec((16, 128), lambda i: (0, 0)),
        out_shape=jax.ShapeDtypeStruct((16, 128), F32),
        cost_estimate=pl.CostEstimate(flops=10**11, transcendentals=0, bytes_accessed=10**8),
        name="waited",
    )(array)


def after(value, *others):
    return lax.optimization_barrier((value, *others))[0]


def per_device(tokens, routes, cotangent, ln_gain, layer_norm_bias, centroid, w_in, w_out):
    groups, halves = lax.axis_size("expert"), lax.axis_size("half")
    half = lax.axis_index("half")
    experts = groups * halves
    count, width = tokens.shape
    capacity = 2 * count // experts
    arriving = experts * capacity
    units = w_in.shape[2]
    tile = min(TILE, arriving)
    targets = routes[:, 0]

    onehot = targets[:, None] == jnp.arange(experts, dtype=jnp.int32)[None, :]
    order = jnp.arange(count, dtype=jnp.int32)
    earlier = (order[:, None] >= order[None, :]).astype(BF16)
    ranks = jnp.dot(earlier, onehot.astype(BF16), preferred_element_type=F32)
    ranks = jnp.sum(jnp.where(onehot, ranks, 0.0), axis=1).astype(jnp.int32) - 1
    slot = targets * capacity + ranks
    slots = jnp.arange(arriving, dtype=jnp.int32)

    def place(values):
        chosen = (slots[:, None] == slot[None, :]).astype(BF16)
        return jnp.dot(chosen, values, preferred_element_type=F32).astype(BF16)

    def exchange(rows):
        rows = rows.reshape(experts, capacity, width)
        return lax.all_to_all(
            rows, ("expert", "half"), split_axis=0, concat_axis=0, tiled=True
        ).reshape(arriving, width)

    def over(axis, value):
        size = lax.axis_size(axis)
        return lax.ppermute(value, axis, [(i, size - 1 - i) for i in range(size)])

    def diagonal(value):
        return lax.ppermute(value, ("sub", "half"), [(i, 3 - i) for i in range(4)])

    def pick(stacked, index):
        return lax.dynamic_index_in_dim(stacked, index, 0, keepdims=False)

    gain = pick(ln_gain, half).astype(F32)[None, :]
    bias = pick(layer_norm_bias, half).astype(F32)[None, :]
    center = pick(centroid, half).astype(F32)[None, :]

    own = [pick(w_in, half), pick(w_out, half)]
    other = [over("half", pick(w, 1 - half)) for w in (w_in, w_out)]
    across = [over("sub", w) for w in own]
    ends = [0, units // 4, units * 3 // 4, units]

    def piece(number):
        start, end = ends[number : number + 2]
        return [other[0][:, start:end], other[1][start:end]]

    far = [over("sub", w) for w in piece(0)]
    x = exchange(place(tokens))
    far[1], *_ = lax.optimization_barrier((far[1], far[0], *across))
    x, dy_sent, mark, own[0], own[1], other[0], other[1], across[0], across[1], far[0], far[1] = lax.optimization_barrier(
        (x, place(cotangent), waited(far[1]), *own, *other, *across, *far)
    )
    dy = exchange(dy_sent)
    far += [over("sub", w) for w in piece(1)]
    near_weights = [*own, *other, *across]

    normed, hidden1, slope1, mixed, gates = call(
        forward_near,
        "forward_near",
        arriving // tile,
        [tiles(x, tile)] + [whole(a) for a in (gain, bias, center, *near_weights)]
        + [(mark, "out", None)],
        [
            rows_out((arriving, width), BF16, tile),
            rows_out((arriving, 3 * units), BF16, tile),
            rows_out((arriving, 3 * units), BF16, tile),
            rows_out((arriving, width), F32, tile),
            rows_out((arriving, 128), F32, tile),
        ],
    )
    normed, *far = lax.optimization_barrier((normed, *far))
    last = [over("sub", after(w, normed)) for w in piece(2)]
    some = ((arriving, units), BF16, (tile, ends[2]), lambda i: (i, 0))
    hidden2, slope2, mixed = call(
        forward_more,
        "forward_more",
        arriving // tile,
        [tiles(normed, tile), tiles(mixed, tile)] + [whole(w) for w in far],
        [some, some, rows_out((arriving, width), F32, tile)],
    )
    far += last
    some = ((arriving, units), BF16, (tile, units - ends[2]), lambda i: (i, ends[2] // (units - ends[2])))
    hidden2, slope2, gated = call(
        forward_last,
        "forward_last",
        arriving // tile,
        [tiles(normed, tile), tiles(mixed, tile), tiles(gates, tile)]
        + [whole(w) for w in last]
        + [(hidden2, "out", None), (slope2, "out", None)],
        [some, some, rows_out((arriving, width), BF16, tile)],
        input_output_aliases={5: 0, 6: 1},
    )
    gated, dy = lax.optimization_barrier((gated, dy))
    returned = exchange(gated)

    def block_in(near, far, number):
        return (near, number) if number < 3 else (far, number - 3)

    def out_part(number, dtype):
        left = block_in(hidden1, hidden2, number)
        return weight_grad(left, (mixed_grad, 0), units, width, dtype, "out_weight_grad")

    def in_part(number, dtype, beside=None, apart=False):
        right = block_in(grad1, grad2, number)
        return weight_grad((normed, 0), right, width, units, dtype, "in_weight_grad", beside, apart)

    out_sent, mixed_grad = first_weight_grad(hidden2, dy, gates, units, "out_weight_grad")
    out_sent = [out_part(2, BF16), out_sent]
    out_across = [over("sub", out_sent[0]), diagonal(out_sent[1])]
    grad1, grad2, expert_grad, sums = call(
        backward,
        "backward",
        arriving // tile,
        [tiles(a, tile) for a in (x, after(dy, *out_sent), gated, slope1, slope2, gates)]
        + [whole(a) for a in (gain, center, *near_weights, *far)],
        [
            rows_out((arriving, 3 * units), BF16, tile),
            rows_out((arriving, units), BF16, tile),
            rows_out((arriving, width), BF16, tile),
            ((8, width), F32, (8, width), lambda i: (0, 0)),
        ],
    )
    in_sent = [over("half", p) for p in in_part(3, BF16, apart=True)]
    out_sent = out_part(1, BF16)
    normed, out_sent = lax.optimization_barrier((normed, out_sent))
    in_across = in_part(2, BF16, in_sent)
    moved = [over("sub", sums), over("half", sums), diagonal(sums)]
    expert_grad, returned, in_across, *moved = lax.optimization_barrier(
        (expert_grad, returned, in_across, *out_across, *moved)
    )
    out_across, moved = moved[:2], moved[2:]
    back = exchange(expert_grad)
    in_across = over("sub", in_across)
    out_beside, in_beside = over("half", out_sent), over("half", in_part(1, BF16))
    layer_out = taken_back(tokens, slot[:, None], returned, BF16, "layer_out")
    out_wgrad = joined(half, out_part(0, F32), out_beside, out_across, "out_weight_grad_joined")
    in_own, layer_out, out_wgrad = lax.optimization_barrier((in_part(0, F32), layer_out, out_wgrad))
    in_wgrad = joined(half, in_own, in_beside, [in_across], "in_weight_grad_joined")
    kept, other_sums = sums + moved[0], moved[1] + moved[2]
    small = jnp.where((jnp.arange(halves) == half)[:, None, None], kept[None], other_sums[None])
    tokens_grad = taken_back(cotangent, slot[:, None], back, F32, "tokens_grad")
    return (layer_out, tokens_grad, small[:, 0], small[:, 1], small[:, 2], in_wgrad, out_wgrad)


def solution(mesh):
    groups, tensor = mesh.shape["expert"], mesh.shape["tensor"]
    halves = 2
    split = Mesh(
        mesh.devices.reshape(groups, tensor // halves, halves), ("expert", "sub", "half")
    )
    rows, within = P(("expert", "sub", "half"), None), P("expert", None)
    columns = P("expert", None, ("sub", "half"))
    depth = P("expert", ("sub", "half"), None)
    return jax.shard_map(
        per_device,
        mesh=split,
        in_specs=(rows, rows, rows, within, within, within, columns, depth),
        out_specs=(rows, rows, within, within, within, columns, depth),
        check_vma=False,
    )
```

time: 662 us -> 465 us (0.70)
  Pallas kernels: 0 us -> 231 us
  matrix products: 243 us -> 14.1 us
  waiting for transfers between devices: 276 us -> 146 us
  other arithmetic: 45.4 us -> 1.92 us
  blocking collectives: 21 us -> 0 us
  starting transfers between devices: 62.8 us -> 46.3 us
  local copies, waits for them, and re-layouts: 5.39 us -> 17.7 us
    pallas_call x0 -> x17, Pallas kernels: none -> 231 us  [the longest x14 215 us: call(): pl.pallas_call(kernel, grid=(steps,), in_specs=[spec(a.shape, block, inde...]
    dot_general x26 -> x0, matrix products: 228 us -> none  [the longest x4 42.7 us: per_device(): mixed = mixed + jnp.dot(hidden, second, preferred_element_type=F32)]
    ppermute x12 -> x18, waiting for transfers between devices: 224 us -> 146 us  [over(): return lax.ppermute(value, axis, [(i, size - 1 - i) for i in range(size)])]
    all_to_all x4, waiting for transfers between devices: 51.9 us -> 0.01 us  [exchange(): lax.all_to_all(rows, ('expert', 'half'), split_axis=0, concat_axis=0, til...]
    all_to_all x4, starting transfers between devices: 56.9 us -> 28.7 us  [exchange(): lax.all_to_all(rows, ('expert', 'half'), split_axis=0, concat_axis=0, til...]
    psum x1 -> x0, blocking collectives: 21 us -> none  [per_device(): small = lax.psum(small, ('half', 'sub'))]
    convert_element_type x4 -> x2, other arithmetic: 20 us -> 1.2 us  [the longest x1 0.6 us: per_device(): center = pick(centroid, half).astype(F32)[None, :]]
    another operation x5 -> x0, other arithmetic: 14.1 us -> none  [the longest x4 14.1 us: shared(): return jnp.stack([jnp.where(half == i, kept, got) for i in range(2)])]
  transfers between devices with their start and end apart: 16 -> 24, of which waited for: 6 -> 9; matrix products, arithmetic and copies ran while one was open for 25% -> 6% of each run, Pallas kernels for 0% -> 48%
where the time goes in v2:
time: 465 us; the launch traced here: 458 us
  Pallas kernels  231 us (50%)
  waiting for transfers between devices  146 us (31%)
  starting transfers between devices  46.3 us (10%)
  local copies, waits for them, and re-layouts  17.7 us (4%)
  matrix products  14.1 us (3%)
    pallas_call x14, Pallas kernels, call(): pl.pallas_call(kernel, grid=(steps,), in_specs=[spec(a.shape, block, inde...  215 us
    ppermute x18, waiting for transfers between devices, over(): return lax.ppermute(value, axis, [(i, size - 1 - i) for i in range(size)])  146 us
    all_to_all x4, starting transfers between devices, exchange(): lax.all_to_all(rows, ('expert', 'half'), split_axis=0, concat_axis=0, til...  28.7 us
    ppermute x18, starting transfers between devices, over(): return lax.ppermute(value, axis, [(i, size - 1 - i) for i in range(size)])  15.9 us
    pallas_call x2, Pallas kernels, joined(): pl.pallas_call(kernel, grid_spec=pltpu.PrefetchScalarGridSpec(num_scalar_...  15.3 us
    dot_general x2, matrix products, place(): return jnp.dot(chosen, values, preferred_element_type=F32).astype(BF16)  13.6 us
  transfers between devices with their start and end apart: 24, of which 9 were waited for; matrix products, arithmetic and copies ran while one was open for 6% of the time, Pallas kernels for 48%

profile of v2, /device:TPU:0, one launch (start us, length us, event | category | flops | bytes accessed | tf_op | source)
XLA Modules:
  0.0 458.3 jit_solution(11770722391143315801)
XLA Ops:
  0.6 4.2 dynamic-slice_bitcast_fusion.1
  5.3 2.5 dynamic-slice_bitcast_fusion
  7.8 2.9 collective-permute-start.4
  11.9 6.0 %fusion.5 = bf16[2048,1024]{1,0:T(8,128)(2,1)} fusion(bf16[1024,1024]{1,0:T(8,128)(2,1)S(1)} %copy-done.8, s32[1024]{0:T(1024)S(1)} %get-tuple-element.123), kind=kOutput, calls=%fused_computation.7 | convolution fusion | flops 4299161600 | bytes 6295552 | tf_op jit(solution)/shard_map/dot_general | solution.py:283
  17.9 6.5 %all-to-all-start = ((bf16[16,128,1024]{2,1,0:T(8,128)(2,1)}), bf16[16,128,1024]{2,1,0:T(8,128)(2,1)}, u32[]{:S(2)}, u32[]{:S(2)}) async-start(bf16[16,128,1024]{2,1,0:T(8,128)(2,1)} %bitcast.30), calls=%async_computation | async-start | bytes 8388608 | tf_op jit(solution)/shard_map/all_to_all | solution.py:287
  24.4 1.1 slice.37
  25.5 1.6 collective-permute-start.3
  27.1 1.1 slice.36
  28.7 7.6 %fusion.6 = bf16[2048,1024]{1,0:T(8,128)(2,1)} fusion(bf16[1024,1024]{1,0:T(8,128)(2,1)} %base.3, s32[1024]{0:T(1024)S(1)} %get-tuple-element.123), kind=kOutput, calls=%fused_computation.8 | convolution fusion | flops 4299161600 | bytes 6295552 | tf_op jit(solution)/shard_map/dot_general | solution.py:283
  36.3 21.0 %collective-permute-done.4.rest_4_ = bf16[1024,1024]{1,0:T(8,128)(2,1)} collective-permute-done((bf16[1024,1024]{1,0:T(8,128)(2,1)S(1)}, bf16[1024,1024]{1,0:T(8,128)(2,1)}, u32[]{:S(2)}, u32[]{:S(2)}) %collective-permute-start.4) | collective-permute-done | bytes 2097184 | tf_op jit(solution)/shard_map/ppermute | solution.py:293
  57.3 44.9 %collective-permute-done.5.rest_5_ = bf16[1024,1024]{1,0:T(8,128)(2,1)} collective-permute-done((bf16[1024,1024]{1,0:T(8,128)(2,1)}, bf16[1024,1024]{1,0:T(8,128)(2,1)}, u32[]{:S(2)}, u32[]{:S(2)}) %collective-permute-start.5) | collective-permute-done | bytes 2097184 | tf_op jit(solution)/shard_map/ppermute | solution.py:293
  102.2 11.1 %collective-permute-done.3.rest_0_.rest_6_ = bf16[1024,256]{1,0:T(8,128)(2,1)S(1)} collective-permute-done((bf16[1024,256]{1,0:T(8,128)(2,1)S(1)}, bf16[1024,256]{1,0:T(8,128)(2,1)S(1)}, u32[]{:S(2)}, u32[]{:S(2)}) %collective-permute-start.3) | collective-permute-done | bytes 524320 | tf_op jit(solution)/shard_map/ppermute | solution.py:293
  113.4 10.6 %collective-permute-done.1.array.rest_1_.rest_7_ = bf16[256,1024]{1,0:T(8,128)(2,1)S(1)} collective-permute-done((bf16[256,1024]{1,0:T(8,128)(2,1)S(1)}, bf16[256,1024]{1,0:T(8,128)(2,1)S(1)}, u32[]{:S(2)}, u32[]{:S(2)}) %collective-permute-start.1) | collective-permute-done | bytes 524320 | tf_op jit(solution)/shard_map/ppermute | solution.py:293
  124.8 1.3 waited.1.rest_6_
  126.1 6.4 %all-to-all-start.1 = ((bf16[16,128,1024]{2,1,0:T(8,128)(2,1)}), bf16[16,128,1024]{2,1,0:T(8,128)(2,1)}, u32[]{:S(2)}, u32[]{:S(2)}) async-start(bf16[16,128,1024]{2,1,0:T(8,128)(2,1)} %bitcast.29), calls=%async_computation.1 | async-start | bytes 8388608 | tf_op jit(solution)/shard_map/all_to_all | solution.py:287
  132.6 1.3 slice.29
  133.9 1.6 collective-permute-start.6
  135.4 1.3 slice.30
  138.5 41.7 %forward_near.1 = (bf16[2048,1024]{1,0:T(8,128)(2,1)}, bf16[2048,3072]{1,0:T(8,128)(2,1)}, bf16[2048,3072]{1,0:T(8,128)(2,1)}, f32[2048,1024]{1,0:T(8,128)}, f32[2048,128]{1,0:T(8,128)}) custom-call(bf16[2048,1024]{1,0:T(8,128)(2,1)} %bitcast.2.x, f32[1,1024]{1,0:T(1,128)} %dynamic-slice_convert_fusion.2.gain, f32[1,1024]{1,0:T(1,128)} %get-tuple-element.125.bias, ...), custom_call_target="tpu_custom_call" | custom-call | flops 1000 | bytes 1000 | tf_op jit(solution)/shard_map/forward_near/pallas_call | solution.py:119
  180.3 1.9 slice.32
  182.1 1.1 slice.31
  183.2 1.6 collective-permute-start.9
  185.3 15.0 %forward_more.1 = (bf16[2048,1024]{1,0:T(8,128)(2,1)}, bf16[2048,1024]{1,0:T(8,128)(2,1)}, f32[2048,1024]{1,0:T(8,128)}) custom-call(bf16[2048,1024]{1,0:T(8,128)(2,1)} %get-tuple-element.91.rows.a, f32[2048,1024]{1,0:T(8,128)} %get-tuple-element.75.near, bf16[1024,256]{1,0:T(8,128)(2,1)} %copy-done.4, bf16[256,1024]{1,0:T(8,128)(2,1)} %copy-done.5, ...), custom_call_target="tpu_custom_call" | custom-call | flops 1000 | bytes 1000 | tf_op jit(solution)/shard_map/forward_more/pallas_call | solution.py:119
  200.4 8.2 %collective-permute-done.8.first.rest_10_ = bf16[1024,256]{1,0:T(8,128)(2,1)S(1)} collective-permute-done((bf16[1024,256]{1,0:T(8,128)(2,1)S(1)}, bf16[1024,256]{1,0:T(8,128)(2,1)S(1)}, u32[]{:S(2)}, u32[]{:S(2)}) %collective-permute-start.8) | collective-permute-done | bytes 524320 | tf_op jit(solution)/shard_map/ppermute | solution.py:293
  209.3 10.7 %forward_last.1 = (bf16[2048,1024]{1,0:T(8,128)(2,1)}, bf16[2048,1024]{1,0:T(8,128)(2,1)}, bf16[2048,1024]{1,0:T(8,128)(2,1)}) custom-call(bf16[2048,1024]{1,0:T(8,128)(2,1)} %get-tuple-element.91.rows.a, f32[2048,1024]{1,0:T(8,128)} %get-tuple-element.80.near, f32[2048,128]{1,0:T(8,128)} %get-tuple-element.81.gates, ...), custom_call_target="tpu_custom_call", output_to_operand_aliasing={{0}: (5, {}), {1}: (6, {})} | custom-call | flops 1000 | bytes 1000 | tf_op jit(solution)/shard_map/forward_last/pallas_call | solution.py:119
  220.0 9.8 %all-to-all-start.2 = ((bf16[16,128,1024]{2,1,0:T(8,128)(2,1)}), bf16[16,128,1024]{2,1,0:T(8,128)(2,1)}, u32[]{:S(2)}, u32[]{:S(2)}) async-start(bf16[16,128,1024]{2,1,0:T(8,128)(2,1)} %bitcast.27), calls=%async_computation.2 | async-start | bytes 8388608 | tf_op jit(solution)/shard_map/all_to_all | solution.py:287
  229.9 9.6 %out_weight_grad.4 = (bf16[1024,1024]{1,0:T(8,128)(2,1)}, bf16[2048,1024]{1,0:T(8,128)(2,1)}) custom-call(bf16[2048,1024]{1,0:T(8,128)(2,1)} %get-tuple-element.86.a, bf16[2048,1024]{1,0:T(8,128)(2,1)} %bitcast.8.dy, f32[2048,128]{1,0:T(8,128)} %get-tuple-element.81.gates), custom_call_target="tpu_custom_call" | custom-call | flops 1000 | bytes 1000 | tf_op jit(solution)/shard_map/out_weight_grad/pallas_call | solution.py:119
  239.5 8.7 %out_weight_grad.6 = bf16[1024,1024]{1,0:T(8,128)(2,1)} custom-call(bf16[2048,3072]{1,0:T(8,128)(2,1)} %get-tuple-element.74.a, bf16[2048,1024]{1,0:T(8,128)(2,1)} %get-tuple-element.90.b), custom_call_target="tpu_custom_call" | custom-call | flops 1000 | bytes 1000 | tf_op jit(solution)/shard_map/out_weight_grad/pallas_call | solution.py:119
  248.2 1.5 collective-permute-start.12
  249.9 57.0 %backward.1 = (bf16[2048,3072]{1,0:T(8,128)(2,1)}, bf16[2048,1024]{1,0:T(8,128)(2,1)}, bf16[2048,1024]{1,0:T(8,128)(2,1)}, f32[8,1024]{1,0:T(8,128)}) custom-call(bf16[2048,1024]{1,0:T(8,128)(2,1)} %bitcast.2.x, bf16[2048,1024]{1,0:T(8,128)(2,1)} %bitcast.8.dy, bf16[2048,1024]{1,0:T(8,128)(2,1)} %get-tuple-element.94.gated, ...), custom_call_target="tpu_custom_call" | custom-call | flops 1000 | bytes 1000 | tf_op jit(solution)/shard_map/backward/pallas_call | solution.py:119
  306.9 9.2 %in_weight_grad.5 = (bf16[512,1024]{1,0:T(8,128)(2,1)}, bf16[512,1024]{1,0:T(8,128)(2,1)}) custom-call(bf16[2048,1024]{1,0:T(8,128)(2,1)} %get-tuple-element.91.rows.a, bf16[2048,1024]{1,0:T(8,128)(2,1)} %get-tuple-element.99.b), custom_call_target="tpu_custom_call" | custom-call | flops 1000 | bytes 1000 | tf_op jit(solution)/shard_map/in_weight_grad/pallas_call | solution.py:119
  316.7 1.5 collective-permute-start.14
  319.5 1.1 collective-permute-done.11.rest_1_
  320.7 1.5 collective-permute-start.16
  322.1 8.5 %out_weight_grad.5 = bf16[1024,1024]{1,0:T(8,128)(2,1)} custom-call(bf16[2048,3072]{1,0:T(8,128)(2,1)} %get-tuple-element.74.a, bf16[2048,1024]{1,0:T(8,128)(2,1)} %get-tuple-element.90.b), custom_call_target="tpu_custom_call" | custom-call | flops 1000 | bytes 1000 | tf_op jit(solution)/shard_map/out_weight_grad/pallas_call | solution.py:119
  330.7 10.1 %in_weight_grad.6 = bf16[2,1024,1024]{2,1,0:T(8,128)(2,1)} custom-call(bf16[2048,1024]{1,0:T(8,128)(2,1)} %get-tuple-element.91.rows.a, bf16[2048,3072]{1,0:T(8,128)(2,1)} %get-tuple-element.97.b, bf16[512,1024]{1,0:T(8,128)(2,1)} %copy-done.10, bf16[512,1024]{1,0:T(8,128)(2,1)} %copy-done.11), custom_call_target="tpu_custom_call" | custom-call | flops 1000 | bytes 1000 | tf_op jit(solution)/shard_map/in_weight_grad/pallas_call | solution.py:119
  340.7 1.5 collective-permute-done.14
  342.3 5.9 %all-to-all-start.3 = ((bf16[16,128,1024]{2,1,0:T(8,128)(2,1)}), bf16[16,128,1024]{2,1,0:T(8,128)(2,1)}, u32[]{:S(2)}, u32[]{:S(2)}) async-start(bf16[16,128,1024]{2,1,0:T(8,128)(2,1)} %bitcast.28), calls=%async_computation.3 | async-start | bytes 8388608 | tf_op jit(solution)/shard_map/all_to_all | solution.py:287
  348.3 1.6 collective-permute-start.19
  349.9 8.6 %in_weight_grad.7 = bf16[1024,1024]{1,0:T(8,128)(2,1)} custom-call(bf16[2048,1024]{1,0:T(8,128)(2,1)} %get-tuple-element.91.rows.a, bf16[2048,3072]{1,0:T(8,128)(2,1)} %get-tuple-element.97.b), custom_call_target="tpu_custom_call" | custom-call | flops 1000 | bytes 1000 | tf_op jit(solution)/shard_map/in_weight_grad/pallas_call | solution.py:119
  359.0 1.0 copy.22.slot
  360.0 8.9 %out_weight_grad.7.own = f32[1024,1024]{1,0:T(8,128)} custom-call(bf16[2048,3072]{1,0:T(8,128)(2,1)} %get-tuple-element.74.a, bf16[2048,1024]{1,0:T(8,128)(2,1)} %get-tuple-element.90.b), custom_call_target="tpu_custom_call" | custom-call | flops 1000 | bytes 1000 | tf_op jit(solution)/shard_map/out_weight_grad/pallas_call | solution.py:119
  369.0 8.9 %in_weight_grad.4.own = f32[1024,1024]{1,0:T(8,128)} custom-call(bf16[2048,1024]{1,0:T(8,128)(2,1)} %get-tuple-element.91.rows.a, bf16[2048,3072]{1,0:T(8,128)(2,1)} %get-tuple-element.97.b), custom_call_target="tpu_custom_call" | custom-call | flops 1000 | bytes 1000 | tf_op jit(solution)/shard_map/in_weight_grad/pallas_call | solution.py:119
  377.9 8.6 %layer_out.1 = bf16[1024,1024]{1,0:T(8,128)(2,1)} custom-call(bf16[1024,1024]{1,0:T(8,128)(2,1)} %base.2, s32[1024,1]{1,0:T(8,128)} %copy.22.slot, bf16[2048,1024]{1,0:T(8,128)(2,1)} %bitcast.11.arrived), custom_call_target="tpu_custom_call" | custom-call | flops 1000 | bytes 1000 | tf_op jit(solution)/shard_map/layer_out/pallas_call | solution.py:119
  386.5 7.6 %out_weight_grad_joined.1 = f32[2,1024,1024]{2,1,0:T(8,128)} custom-call(s32[1]{0:T(128)} %bitcast.12.half, f32[1024,1024]{1,0:T(8,128)} %out_weight_grad.7.own, bf16[1024,1024]{1,0:T(8,128)(2,1)} %collective-permute-done.17.beside, bf16[1024,1024]{1,0:T(8,128)(2,1)} %collective-permute-done.12.rest_0_, bf16[1024,1024]{1,0:T(8,128)(2,1)} %collective-permute-done.13.rest_1_), custom_call_target="tpu_custom_call" | custom-call | flops 1000 | bytes 1000 | tf_op jit(solution)/shard_map/out_weight_grad_joined/pallas_call | solution.py:210
  394.9 46.7 %collective-permute-done.19.rest_0_ = bf16[2,1024,1024]{2,1,0:T(8,128)(2,1)} collective-permute-done((bf16[2,1024,1024]{2,1,0:T(8,128)(2,1)}, bf16[2,1024,1024]{2,1,0:T(8,128)(2,1)}, u32[]{:S(2)}, u32[]{:S(2)}) %collective-permute-start.19) | collective-permute-done | bytes 4194336 | tf_op jit(solution)/shard_map/ppermute | solution.py:293
  441.5 7.7 %in_weight_grad_joined.1 = f32[2,1024,1024]{2,1,0:T(8,128)} custom-call(s32[1]{0:T(128)} %bitcast.12.half, f32[1024,1024]{1,0:T(8,128)} %in_weight_grad.4.own, bf16[1024,1024]{1,0:T(8,128)(2,1)} %collective-permute-done.18.beside, bf16[2,1024,1024]{2,1,0:T(8,128)(2,1)} %collective-permute-done.19.rest_0_), custom_call_target="tpu_custom_call" | custom-call | flops 1000 | bytes 1000 | tf_op jit(solution)/shard_map/in_weight_grad_joined/pallas_call | solution.py:210
  449.2 8.9 %tokens_grad.1 = f32[1024,1024]{1,0:T(8,128)} custom-call(bf16[1024,1024]{1,0:T(8,128)(2,1)} %base.3, s32[1024,1]{1,0:T(8,128)} %copy.22.slot, bf16[2048,1024]{1,0:T(8,128)(2,1)} %bitcast.14.arrived), custom_call_target="tpu_custom_call" | custom-call | flops 1000 | bytes 1000 | tf_op jit(solution)/shard_map/tokens_grad/pallas_call | solution.py:119
  (78 shorter events, 9.6 us)
Async XLA Ops:
  0.6 4.6 %copy-start.1 = (bf16[2,1024,1024]{2,1,0:T(8,128)(2,1)S(1)}, bf16[2,1024,1024]{2,1,0:T(8,128)(2,1)}, u32[]{:S(2)}) copy-start(bf16[2,1024,1024]{2,1,0:T(8,128)(2,1)} %param.15) | copy-start | bytes 12582916
  4.8 3.0 copy-start
  4.8 6.0 %copy-start.13 = (s32[1024,1]{0,1:T(1,128)S(1)}, s32[1024,1]{0,1:T(1,128)}, u32[]{:S(2)}) copy-start(s32[1024,1]{0,1:T(1,128)} %param.9) | copy-start | bytes 12292
  4.8 7.1 %copy-start.8 = (bf16[1024,1024]{1,0:T(8,128)(2,1)S(1)}, bf16[1024,1024]{1,0:T(8,128)(2,1)}, u32[]{:S(2)}) copy-start(bf16[1024,1024]{1,0:T(8,128)(2,1)} %base.2) | copy-start | bytes 6291460
  4.8 19.6 %collective-permute-start.2 = (bf16[1024,1024]{1,0:T(8,128)(2,1)}, bf16[1024,1024]{1,0:T(8,128)(2,1)}, u32[]{:S(2)}, u32[]{:S(2)}) collective-permute-start(bf16[1024,1024]{1,0:T(8,128)(2,1)} %get-tuple-element.118), channel_id=1, source_target_pairs={{0,1},{1,0},{2,3},{3,2},{4,5},{5,4},{6,7},{7,6},{8,9},{9,8},{10,11... | collective-permute-start | bytes 6291464 | tf_op jit(solution)/shard_map/ppermute | solution.py:293
  7.8 19.3 %collective-permute-start = (bf16[1024,1024]{1,0:T(8,128)(2,1)}, bf16[1024,1024]{1,0:T(8,128)(2,1)}, u32[]{:S(2)}, u32[]{:S(2)}) collective-permute-start(bf16[1024,1024]{1,0:T(8,128)(2,1)} %get-tuple-element.116), channel_id=1, source_target_pairs={{0,1},{1,0},{2,3},{3,2},{4,5},{5,4},{6,7},{7,6},{8,9},{9,8},{10,11... | collective-permute-start | bytes 6291464 | tf_op jit(solution)/shard_map/ppermute | solution.py:293
  7.8 49.5 %collective-permute-start.4 = (bf16[1024,1024]{1,0:T(8,128)(2,1)S(1)}, bf16[1024,1024]{1,0:T(8,128)(2,1)}, u32[]{:S(2)}, u32[]{:S(2)}) collective-permute-start(bf16[1024,1024]{1,0:T(8,128)(2,1)S(1)} %get-tuple-element.63.rest_0_), channel_id=1, source_target_pairs={{0,2},{2,0},{1,3},{3,1},{4,6},{6,4},{5,7},{7,5},{8,10},{10,8},{9,1... | collective-permute-start | bytes 6291464 | tf_op jit(solution)/shard_map/ppermute | solution.py:293
  10.7 91.5 %collective-permute-start.5 = (bf16[1024,1024]{1,0:T(8,128)(2,1)}, bf16[1024,1024]{1,0:T(8,128)(2,1)}, u32[]{:S(2)}, u32[]{:S(2)}) collective-permute-start(bf16[1024,1024]{1,0:T(8,128)(2,1)} %get-tuple-element.64.rest_1_), channel_id=1, source_target_pairs={{0,2},{2,0},{1,3},{3,1},{4,6},{6,4},{5,7},{7,5},{8,10},{10,8},{9,1... | collective-permute-start | bytes 6291464 | tf_op jit(solution)/shard_map/ppermute | solution.py:293
  17.9 108.2 %all-to-all-start = ((bf16[16,128,1024]{2,1,0:T(8,128)(2,1)}), bf16[16,128,1024]{2,1,0:T(8,128)(2,1)}, u32[]{:S(2)}, u32[]{:S(2)}) async-start(bf16[16,128,1024]{2,1,0:T(8,128)(2,1)} %bitcast.30), calls=%async_computation | async-start | bytes 8388608 | tf_op jit(solution)/shard_map/all_to_all | solution.py:287
  25.5 87.9 %collective-permute-start.3 = (bf16[1024,256]{1,0:T(8,128)(2,1)S(1)}, bf16[1024,256]{1,0:T(8,128)(2,1)S(1)}, u32[]{:S(2)}, u32[]{:S(2)}) collective-permute-start(bf16[1024,256]{1,0:T(8,128)(2,1)S(1)} %slice.37), channel_id=1, source_target_pairs={{0,2},{2,0},{1,3},{3,1},{4,6},{6,4},{5,7},{7,5},{8,10},{10,8},{9,1... | collective-permute-start | bytes 1572872 | tf_op jit(solution)/shard_map/ppermute | solution.py:293
  28.1 95.8 %collective-permute-start.1 = (bf16[256,1024]{1,0:T(8,128)(2,1)S(1)}, bf16[256,1024]{1,0:T(8,128)(2,1)S(1)}, u32[]{:S(2)}, u32[]{:S(2)}) collective-permute-start(bf16[256,1024]{1,0:T(8,128)(2,1)S(1)} %slice.36), channel_id=1, source_target_pairs={{0,2},{2,0},{1,3},{3,1},{4,6},{6,4},{5,7},{7,5},{8,10},{10,8},{9,1... | collective-permute-start | bytes 1572872 | tf_op jit(solution)/shard_map/ppermute | solution.py:293
  113.4 12.7 %copy-start.4 = (bf16[1024,256]{1,0:T(8,128)(2,1)}, bf16[1024,256]{1,0:T(8,128)(2,1)S(1)}, u32[]{:S(2)}) copy-start(bf16[1024,256]{1,0:T(8,128)(2,1)S(1)} %collective-permute-done.3.rest_0_.rest_6_) | copy-start | bytes 1572868
  124.0 0.8 copy-start.5
  126.1 94.0 %all-to-all-start.1 = ((bf16[16,128,1024]{2,1,0:T(8,128)(2,1)}), bf16[16,128,1024]{2,1,0:T(8,128)(2,1)}, u32[]{:S(2)}, u32[]{:S(2)}) async-start(bf16[16,128,1024]{2,1,0:T(8,128)(2,1)} %bitcast.29), calls=%async_computation.1 | async-start | bytes 8388608 | tf_op jit(solution)/shard_map/all_to_all | solution.py:287
  132.5 4.8 %copy-start.16 = (bf16[2,1024]{1,0:T(2,128)(2,1)S(1)}, bf16[2,1024]{1,0:T(2,128)(2,1)}, u32[]{:S(2)}) copy-start(bf16[2,1024]{1,0:T(2,128)(2,1)} %param.11) | copy-start | bytes 12292
  132.5 5.4 %copy-start.17 = (bf16[2,1024]{1,0:T(2,128)(2,1)S(1)}, bf16[2,1024]{1,0:T(2,128)(2,1)}, u32[]{:S(2)}) copy-start(bf16[2,1024]{1,0:T(2,128)(2,1)} %param.13) | copy-start | bytes 12292
  132.5 5.4 %copy-start.18 = (bf16[2,1024]{1,0:T(2,128)(2,1)S(1)}, bf16[2,1024]{1,0:T(2,128)(2,1)}, u32[]{:S(2)}) copy-start(bf16[2,1024]{1,0:T(2,128)(2,1)} %param.12) | copy-start | bytes 12292
  133.9 49.3 %collective-permute-start.6 = (bf16[1024,512]{1,0:T(8,128)(2,1)S(1)}, bf16[1024,512]{1,0:T(8,128)(2,1)S(1)}, u32[]{:S(2)}, u32[]{:S(2)}) collective-permute-start(bf16[1024,512]{1,0:T(8,128)(2,1)S(1)} %slice.29), channel_id=1, source_target_pairs={{0,2},{2,0},{1,3},{3,1},{4,6},{6,4},{5,7},{7,5},{8,10},{10,8},{9,1... | collective-permute-start | bytes 3145736 | tf_op jit(solution)/shard_map/ppermute | solution.py:293
  136.7 46.5 %collective-permute-start.7 = (bf16[512,1024]{1,0:T(8,128)(2,1)S(1)}, bf16[512,1024]{1,0:T(8,128)(2,1)S(1)}, u32[]{:S(2)}, u32[]{:S(2)}) collective-permute-start(bf16[512,1024]{1,0:T(8,128)(2,1)S(1)} %slice.30), channel_id=1, source_target_pairs={{0,2},{2,0},{1,3},{3,1},{4,6},{6,4},{5,7},{7,5},{8,10},{10,8},{9,1... | collective-permute-start | bytes 3145736 | tf_op jit(solution)/shard_map/ppermute | solution.py:293
  183.2 2.1 copy-start.2
  183.2 2.1 copy-start.3
  183.2 17.1 %collective-permute-start.9 = (bf16[256,1024]{1,0:T(8,128)(2,1)}, bf16[256,1024]{1,0:T(8,128)(2,1)S(1)}, u32[]{:S(2)}, u32[]{:S(2)}) collective-permute-start(bf16[256,1024]{1,0:T(8,128)(2,1)} %slice.32), channel_id=1, source_target_pairs={{0,2},{2,0},{1,3},{3,1},{4,6},{6,4},{5,7},{7,5},{8,10},{10,8},{9,1... | collective-permute-start | bytes 1572872 | tf_op jit(solution)/shard_map/ppermute | solution.py:293
  184.8 23.7 %collective-permute-start.8 = (bf16[1024,256]{1,0:T(8,128)(2,1)S(1)}, bf16[1024,256]{1,0:T(8,128)(2,1)S(1)}, u32[]{:S(2)}, u32[]{:S(2)}) collective-permute-start(bf16[1024,256]{1,0:T(8,128)(2,1)S(1)} %slice.31), channel_id=1, source_target_pairs={{0,2},{2,0},{1,3},{3,1},{4,6},{6,4},{5,7},{7,5},{8,10},{10,8},{9,1... | collective-permute-start | bytes 1572872 | tf_op jit(solution)/shard_map/ppermute | solution.py:293
  200.4 8.2 %copy-start.6 = (bf16[256,1024]{1,0:T(8,128)(2,1)}, bf16[256,1024]{1,0:T(8,128)(2,1)S(1)}, u32[]{:S(2)}) copy-start(bf16[256,1024]{1,0:T(8,128)(2,1)S(1)} %collective-permute-done.9.second.rest_11_) | copy-start | bytes 1572868
  208.5 0.8 copy-start.7
  220.0 122.3 %all-to-all-start.2 = ((bf16[16,128,1024]{2,1,0:T(8,128)(2,1)}), bf16[16,128,1024]{2,1,0:T(8,128)(2,1)}, u32[]{:S(2)}, u32[]{:S(2)}) async-start(bf16[16,128,1024]{2,1,0:T(8,128)(2,1)} %bitcast.27), calls=%async_computation.2 | async-start | bytes 8388608 | tf_op jit(solution)/shard_map/all_to_all | solution.py:287
  239.5 10.2 %copy-start.19 = (bf16[1024,1024]{1,0:T(8,128)(2,1)S(1)}, bf16[1024,1024]{1,0:T(8,128)(2,1)}, u32[]{:S(2)}) copy-start(bf16[1024,1024]{1,0:T(8,128)(2,1)} %get-tuple-element.92) | copy-start | bytes 6291460
  248.2 94.1 %collective-permute-start.12 = (bf16[1024,1024]{1,0:T(8,128)(2,1)}, bf16[1024,1024]{1,0:T(8,128)(2,1)}, u32[]{:S(2)}, u32[]{:S(2)}) collective-permute-start(bf16[1024,1024]{1,0:T(8,128)(2,1)} %out_weight_grad.6), channel_id=1, source_target_pairs={{0,2},{2,0},{1,3},{3,1},{4,6},{6,4},{5,7},{7,5},{8,10},{10,8},{9,1... | collective-permute-start | bytes 6291464 | tf_op jit(solution)/shard_map/ppermute | solution.py:293
  249.7 92.6 %collective-permute-start.13 = (bf16[1024,1024]{1,0:T(8,128)(2,1)S(1)}, bf16[1024,1024]{1,0:T(8,128)(2,1)}, u32[]{:S(2)}, u32[]{:S(2)}) collective-permute-start(bf16[1024,1024]{1,0:T(8,128)(2,1)S(1)} %copy-done.19), channel_id=1, source_target_pairs={{0,3},{1,2},{2,1},{3,0},{4,7},{5,6},{6,5},{7,4},{8,11},{9,10},{10,... | collective-permute-start | bytes 6291464 | tf_op jit(solution)/shard_map/ppermute | solution.py:296
  306.9 9.8 %copy-start.12 = (f32[8,1024]{1,0:T(8,128)S(1)}, f32[8,1024]{1,0:T(8,128)}, u32[]{:S(2)}) copy-start(f32[8,1024]{1,0:T(8,128)} %get-tuple-element.102) | copy-start | bytes 98308
  316.1 3.0 collective-permute-start.10
  316.7 4.0 collective-permute-start.11
  316.7 25.5 %collective-permute-start.14 = (f32[8,1024]{1,0:T(8,128)S(1)}, f32[8,1024]{1,0:T(8,128)S(1)}, u32[]{:S(2)}, u32[]{:S(2)}) collective-permute-start(f32[8,1024]{1,0:T(8,128)S(1)} %copy-done.12), channel_id=1, source_target_pairs={{0,2},{2,0},{1,3},{3,1},{4,6},{6,4},{5,7},{7,5},{8,10},{10,8},{9,1... | collective-permute-start | bytes 98312 | tf_op jit(solution)/shard_map/ppermute | solution.py:293
  319.2 11.5 %copy-start.10 = (bf16[512,1024]{1,0:T(8,128)(2,1)}, bf16[512,1024]{1,0:T(8,128)(2,1)S(1)}, u32[]{:S(2)}) copy-start(bf16[512,1024]{1,0:T(8,128)(2,1)S(1)} %collective-permute-done.10.rest_0_) | copy-start | bytes 3145732
  319.2 23.1 %collective-permute-start.15 = (f32[8,1024]{1,0:T(8,128)S(1)}, f32[8,1024]{1,0:T(8,128)S(1)}, u32[]{:S(2)}, u32[]{:S(2)}) collective-permute-start(f32[8,1024]{1,0:T(8,128)S(1)} %copy-done.12), channel_id=1, source_target_pairs={{0,1},{1,0},{2,3},{3,2},{4,5},{5,4},{6,7},{7,6},{8,9},{9,8},{10,11... | collective-permute-start | bytes 98312 | tf_op jit(solution)/shard_map/ppermute | solution.py:293
  320.7 10.0 %copy-start.11 = (bf16[512,1024]{1,0:T(8,128)(2,1)}, bf16[512,1024]{1,0:T(8,128)(2,1)S(1)}, u32[]{:S(2)}) copy-start(bf16[512,1024]{1,0:T(8,128)(2,1)S(1)} %collective-permute-done.11.rest_1_) | copy-start | bytes 3145732
  320.7 21.6 %collective-permute-start.16 = (f32[8,1024]{1,0:T(8,128)S(1)}, f32[8,1024]{1,0:T(8,128)S(1)}, u32[]{:S(2)}, u32[]{:S(2)}) collective-permute-start(f32[8,1024]{1,0:T(8,128)S(1)} %copy-done.12), channel_id=1, source_target_pairs={{0,3},{1,2},{2,1},{3,0},{4,7},{5,6},{6,5},{7,4},{8,11},{9,10},{10,... | collective-permute-start | bytes 98312 | tf_op jit(solution)/shard_map/ppermute | solution.py:296
  342.3 7.5 %copy-start.9 = (bf16[1024,1024]{1,0:T(8,128)(2,1)S(1)}, bf16[1024,1024]{1,0:T(8,128)(2,1)}, u32[]{:S(2)}) copy-start(bf16[1024,1024]{1,0:T(8,128)(2,1)} %out_weight_grad.5) | copy-start | bytes 6291460
  342.3 106.9 %all-to-all-start.3 = ((bf16[16,128,1024]{2,1,0:T(8,128)(2,1)}), bf16[16,128,1024]{2,1,0:T(8,128)(2,1)}, u32[]{:S(2)}, u32[]{:S(2)}) async-start(bf16[16,128,1024]{2,1,0:T(8,128)(2,1)} %bitcast.28), calls=%async_computation.3 | async-start | bytes 8388608 | tf_op jit(solution)/shard_map/all_to_all | solution.py:287
  348.3 10.7 %copy-start.14 = (s32[1024,1]{0,1:T(1,128)S(1)}, s32[1024,1]{0,1:T(1,128)}, u32[]{:S(2)}) copy-start(s32[1024,1]{0,1:T(1,128)} %param.9) | copy-start | bytes 12292
  348.3 10.7 %copy-start.15 = (s32[1024]{0:T(1024)S(1)}, s32[1024]{0:T(1024)}, u32[]{:S(2)}) copy-start(s32[1024]{0:T(1024)} %get-tuple-element.122) | copy-start | bytes 12292
  348.3 93.2 %collective-permute-start.19 = (bf16[2,1024,1024]{2,1,0:T(8,128)(2,1)}, bf16[2,1024,1024]{2,1,0:T(8,128)(2,1)}, u32[]{:S(2)}, u32[]{:S(2)}) collective-permute-start(bf16[2,1024,1024]{2,1,0:T(8,128)(2,1)} %in_weight_grad.6), channel_id=1, source_target_pairs={{0,2},{2,0},{1,3},{3,1},{4,6},{6,4},{5,7},{7,5},{8,10},{10,8},{9,1... | collective-permute-start | bytes 12582920 | tf_op jit(solution)/shard_map/ppermute | solution.py:293
  349.9 36.6 %collective-permute-start.17 = (bf16[1024,1024]{1,0:T(8,128)(2,1)S(1)}, bf16[1024,1024]{1,0:T(8,128)(2,1)}, u32[]{:S(2)}, u32[]{:S(2)}) collective-permute-start(bf16[1024,1024]{1,0:T(8,128)(2,1)S(1)} %copy-done.9), channel_id=1, source_target_pairs={{0,1},{1,0},{2,3},{3,2},{4,5},{5,4},{6,7},{7,6},{8,9},{9,8},{10,11... | collective-permute-start | bytes 6291464 | tf_op jit(solution)/shard_map/ppermute | solution.py:293
  358.5 36.3 %collective-permute-start.18 = (bf16[1024,1024]{1,0:T(8,128)(2,1)}, bf16[1024,1024]{1,0:T(8,128)(2,1)}, u32[]{:S(2)}, u32[]{:S(2)}) collective-permute-start(bf16[1024,1024]{1,0:T(8,128)(2,1)} %in_weight_grad.7), channel_id=1, source_target_pairs={{0,1},{1,0},{2,3},{3,2},{4,5},{5,4},{6,7},{7,6},{8,9},{9,8},{10,11... | collective-permute-start | bytes 6291464 | tf_op jit(solution)/shard_map/ppermute | solution.py:293

commit v3 on v2

--- a/solution.py
+++ b/solution.py
@@ -74,22 +74,43 @@
     gated[...] = (gates[:, :1] * whole).astype(BF16)
 
 
-def backward(x, dy, gated, s1, s2, gates, gain, center, *rest):
-    weights, (g1, g2, expert_grad, sums) = paired(rest[:-4]), rest[-4:]
+def backward(ends, x, dy, gated, s1, s2, gates, gain, center, *rest):
+    count = 6 + 2 * (len(ends) - 1)
+    refs, (g1, g2, expert_grad, sums), (ins, outs, sems) = rest[:count], rest[count:-3], rest[-3:]
+    units = outs.shape[0] // 4
+    step = min(TILE, units)
+    copies = []
+    for number, (first, second) in enumerate(paired(refs)):
+        columns = pl.ds(number * units if number < 3 else 3 * units + ends[number - 3], first.shape[1])
+        copies += [
+            (min(number, 3), pltpu.make_async_copy(second, outs.at[columns, :], sems.at[2 * number])),
+            (4, pltpu.make_async_copy(first, ins.at[:, columns], sems.at[2 * number + 1])),
+        ]
+    copies.sort(key=lambda c: c[0])
+
+    @pl.when(pl.program_id(0) == 0)
+    def _():
+        for _, copy in copies:
+            copy.start()
+        sums[...] = jnp.zeros_like(sums)
+
     rows = x[...].astype(F32)
     gate = gates[:, :1]
     upper = dy[...].astype(F32)
     mixed_grad = (gate * upper).astype(BF16)
-    total, at = None, 0
-    for first, second in steps_of(weights):
-        slope, grad, start = (s1, g1, at) if at < s1.shape[1] else (s2, g2, at - s1.shape[1])
-        hidden_grad = product(mixed_grad, second, LAST)
-        columns = pl.ds(start, second.shape[0])
-        pre_grad = (hidden_grad * slope[:, columns].astype(F32)).astype(BF16)
-        grad[:, columns] = pre_grad
-        added = product(pre_grad, first, LAST)
-        total = added if total is None else total + added
-        at += second.shape[0]
+    for block in range(5):
+
+        @pl.when(pl.program_id(0) == 0)
+        def _():
+            for used, copy in copies:
+                if used == block:
+                    copy.wait()
+
+        for at in range(block * units, min(block + 1, 4) * units, step):
+            hidden_grad = product(mixed_grad, outs[at : at + step, :], LAST)
+            slope, grad, at = (s1, g1, at) if block < 3 else (s2, g2, at - 3 * units)
+            grad[:, at : at + step] = (hidden_grad * slope[:, at : at + step].astype(F32)).astype(BF16)
+    total = product(g1[...], ins[:, : 3 * units], LAST) + product(g2[...], ins[:, 3 * units :], LAST)
     xhat, inverse = standardize(rows)
     logit_grad = jnp.sum(upper * gated[...].astype(F32), axis=-1, keepdims=True) * (1.0 - gate)
     u = total * gain[...]
@@ -98,11 +119,6 @@
         * (u - jnp.mean(u, axis=-1, keepdims=True) - xhat * jnp.mean(u * xhat, axis=-1, keepdims=True))
         + logit_grad * center[...]
     ).astype(BF16)
-
-    @pl.when(pl.program_id(0) == 0)
-    def _():
-        sums[...] = jnp.zeros_like(sums)
-
     sums[0:1, :] += jnp.sum(total * xhat, axis=0, keepdims=True)
     sums[1:2, :] += jnp.sum(total, axis=0, keepdims=True)
     sums[2:3, :] += jnp.sum(logit_grad * rows, axis=0, keepdims=True)
@@ -141,24 +157,20 @@
     return array, None, None
 
 
-def weight_grad(left, right, units, width, dtype, name, beside=None, apart=False):
+def weight_grad(left, right, units, width, dtype, name, apart=False):
     (a, i), (b, j) = left, right
     tile = min(TILE, units)
     steps = units // tile
 
-    def kernel(a, b, *rest):
+    def kernel(a, b, *outs):
         total = product(a[...], b[...], ROWS).astype(dtype)
-        if not apart and beside is None:
-            rest[0][...] = total
-        for n in range(steps if apart or beside is not None else 0):
+        if not apart:
+            outs[0][...] = total
+        for n in range(steps if apart else 0):
 
             @pl.when(pl.program_id(0) == n)
             def _():
-                if apart:
-                    rest[n][...] = total
-                else:
-                    rest[-1][0] = total
-                    rest[-1][1] = rest[n][...]
+                outs[n][...] = total
 
     ins = [
         (a, (a.shape[0], tile), lambda n: (0, i * steps + n)),
@@ -166,10 +178,7 @@
     ]
     if apart:
         return call(kernel, name, steps, ins, [((tile, width), dtype, (tile, width), lambda n: (0, 0))] * steps)
-    if beside is None:
-        return call(kernel, name, steps, ins, [rows_out((units, width), dtype, tile)])[0]
-    out = (2, units, width), dtype, (2, tile, width), lambda n: (0, n, 0)
-    return call(kernel, name, steps, ins + [whole(p) for p in beside], [out])[0]
+    return call(kernel, name, steps, ins, [rows_out((units, width), dtype, tile)])[0]
 
 
 def first_weight_grad(hidden, dy, gates, units, name):
@@ -192,39 +201,51 @@
     )
 
 
-def joined(half, own, beside, across, name):
-    count, width = own.shape
+def sums_into(number, operands, held, name):
+    count, width = operands[0].shape
     tile = min(256, count)
-
-    def kernel(half, own, beside, *rest):
-        across, out = rest[:-1], rest[-1]
-        across = [a[...] for a in across] if len(across) == 2 else [across[0][0], across[0][1]]
-        kept = own[...] + across[0].astype(F32)
-        other = beside[...].astype(F32) + across[1].astype(F32)
-        mine = half[0] == 0
-        out[0] = jnp.where(mine, kept, other)
-        out[1] = jnp.where(mine, other, kept)
-
-    rows = pl.BlockSpec((tile, width), lambda i, _: (i, 0))
-    both = pl.BlockSpec((2, tile, width), lambda i, _: (0, i, 0))
+    flat, ends = [], []
+    for o in operands:
+        pieces = o if isinstance(o, list) else [o]
+        at = 0
+        for p in pieces:
+            flat.append(p)
+            ends.append((at, at + p.shape[0] // tile))
+            at += p.shape[0] // tile
+
+    def kernel(number, *refs):
+        out = refs[-1]
+        step, total = pl.program_id(0), None
+        for ref, (start, end) in zip(refs, ends):
+            part = ref[...].astype(F32)
+            if (start, end) != (0, count // tile):
+                part = jnp.where((step >= start) & (step < end), part, 0.0)
+            total = part if total is None else total + part
+        out[0] = total
+
+    def rows(start, end):
+        return pl.BlockSpec((tile, width), lambda i, _: (jnp.clip(i - start, 0, end - start - 1), 0))
+
+    extra = [] if held is None else [held]
     return pl.pallas_call(
         kernel,
         grid_spec=pltpu.PrefetchScalarGridSpec(
             num_scalar_prefetch=1,
             grid=(count // tile,),
-            in_specs=[rows, rows] + ([rows, rows] if len(across) == 2 else [both]),
-            out_specs=both,
+            in_specs=[rows(*e) for e in ends] + [pl.BlockSpec(memory_space=pl.ANY)] * len(extra),
+            out_specs=pl.BlockSpec((1, tile, width), lambda i, number: (number[0], i, 0)),
         ),
         out_shape=jax.ShapeDtypeStruct((2, count, width), F32),
+        input_output_aliases={1 + len(flat): 0} if extra else {},
         compiler_params=pltpu.CompilerParams(vmem_limit_bytes=VMEM_LIMIT),
         cost_estimate=pl.CostEstimate(flops=1000, transcendentals=0, bytes_accessed=1000),
         name=name,
-    )(half.astype(jnp.int32)[None], own, beside, *across)
+    )(number.astype(jnp.int32)[None], *flat, *extra)
 
 
 def taken_back(base, slot, arrived, dtype, name):
     count, width = base.shape
-    tile = min(256, count)
+    tile = min(512, count)
 
     def kernel(base, slot, arrived, out):
         slots = lax.broadcasted_iota(jnp.int32, (tile, arrived.shape[0]), 1)
@@ -303,22 +324,26 @@
     center = pick(centroid, half).astype(F32)[None, :]
 
     own = [pick(w_in, half), pick(w_out, half)]
-    other = [over("half", pick(w, 1 - half)) for w in (w_in, w_out)]
+    other = [pick(over("half", w), half) for w in (w_in, w_out)]
     across = [over("sub", w) for w in own]
-    ends = [0, units // 4, units * 3 // 4, units]
+    ends = [0, units // 8, units * 3 // 4, units]
 
     def piece(number):
         start, end = ends[number : number + 2]
-        return [other[0][:, start:end], other[1][start:end]]
-
-    far = [over("sub", w) for w in piece(0)]
+        first = lax.dynamic_slice(w_in, (1 - half, 0, start), (1, width, end - start))
+        return [first[0], lax.dynamic_slice(w_out, (1 - half, start, 0), (1, end - start, width))[0]]
+
+    mark = waited(across[0])
+    far = [diagonal(after(w, mark)) for w in piece(0)]
     x = exchange(place(tokens))
-    far[1], *_ = lax.optimization_barrier((far[1], far[0], *across))
-    x, dy_sent, mark, own[0], own[1], other[0], other[1], across[0], across[1], far[0], far[1] = lax.optimization_barrier(
-        (x, place(cotangent), waited(far[1]), *own, *other, *across, *far)
-    )
+    sent = [*piece(1), *piece(2)]
+    x, dy_sent, mark, *arrived = lax.optimization_barrier(
+        (x, place(cotangent), mark, *own, *other, *across, *far, *sent)
+    )
+    own, other, across, far, sent = (arrived[n : n + 2] for n in (0, 2, 4, 6, 8))
+    later = arrived[10:]
     dy = exchange(dy_sent)
-    far += [over("sub", w) for w in piece(1)]
+    far = list(far) + [diagonal(w) for w in sent]
     near_weights = [*own, *other, *across]
 
     normed, hidden1, slope1, mixed, gates = call(
@@ -336,7 +361,7 @@
         ],
     )
     normed, *far = lax.optimization_barrier((normed, *far))
-    last = [over("sub", after(w, normed)) for w in piece(2)]
+    last = [diagonal(after(w, normed)) for w in later]
     some = ((arriving, units), BF16, (tile, ends[2]), lambda i: (i, 0))
     hidden2, slope2, mixed = call(
         forward_more,
@@ -367,42 +392,50 @@
         left = block_in(hidden1, hidden2, number)
         return weight_grad(left, (mixed_grad, 0), units, width, dtype, "out_weight_grad")
 
-    def in_part(number, dtype, beside=None, apart=False):
+    def in_part(number, dtype, apart=False):
         right = block_in(grad1, grad2, number)
-        return weight_grad((normed, 0), right, width, units, dtype, "in_weight_grad", beside, apart)
+        return weight_grad((normed, 0), right, width, units, dtype, "in_weight_grad", apart)
 
     out_sent, mixed_grad = first_weight_grad(hidden2, dy, gates, units, "out_weight_grad")
     out_sent = [out_part(2, BF16), out_sent]
     out_across = [over("sub", out_sent[0]), diagonal(out_sent[1])]
     grad1, grad2, expert_grad, sums = call(
-        backward,
+        functools.partial(backward, ends),
         "backward",
         arriving // tile,
         [tiles(a, tile) for a in (x, after(dy, *out_sent), gated, slope1, slope2, gates)]
-        + [whole(a) for a in (gain, center, *near_weights, *far)],
+        + [whole(a) for a in (gain, center)]
+        + [(a, "out", None) for a in (*near_weights, *far)],
         [
             rows_out((arriving, 3 * units), BF16, tile),
             rows_out((arriving, units), BF16, tile),
             rows_out((arriving, width), BF16, tile),
             ((8, width), F32, (8, width), lambda i: (0, 0)),
         ],
-    )
-    in_sent = [over("half", p) for p in in_part(3, BF16, apart=True)]
+        scratch_shapes=[
+            pltpu.VMEM((width, 4 * units), BF16),
+            pltpu.VMEM((4 * units, width), BF16),
+            pltpu.SemaphoreType.DMA((12,)),
+        ],
+    )
+    grad2, out_across[1] = lax.optimization_barrier((grad2, out_across[1]))
+    in_sent = [in_part(3, BF16), in_part(2, BF16)]
     out_sent = out_part(1, BF16)
-    normed, out_sent = lax.optimization_barrier((normed, out_sent))
-    in_across = in_part(2, BF16, in_sent)
     moved = [over("sub", sums), over("half", sums), diagonal(sums)]
-    expert_grad, returned, in_across, *moved = lax.optimization_barrier(
-        (expert_grad, returned, in_across, *out_across, *moved)
+    expert_grad, returned, hidden1, in_sent[0], in_sent[1], out_sent, *moved = lax.optimization_barrier(
+        (expert_grad, returned, hidden1, *in_sent, out_sent, *out_across, *moved)
     )
     out_across, moved = moved[:2], moved[2:]
     back = exchange(expert_grad)
-    in_across = over("sub", in_across)
-    out_beside, in_beside = over("half", out_sent), over("half", in_part(1, BF16))
+    in_across = [over("sub", in_sent[1]), diagonal(in_sent[0])]
+    out_beside = over("half", out_sent)
+    in_beside = [over("half", p) for p in in_part(1, BF16, apart=True)]
     layer_out = taken_back(tokens, slot[:, None], returned, BF16, "layer_out")
-    out_wgrad = joined(half, out_part(0, F32), out_beside, out_across, "out_weight_grad_joined")
+    out_wgrad = sums_into(1 - half, [out_across[1], out_beside], None, "out_weight_grad_other")
+    out_wgrad = sums_into(half, [out_part(0, F32), out_across[0]], out_wgrad, "out_weight_grad_own")
     in_own, layer_out, out_wgrad = lax.optimization_barrier((in_part(0, F32), layer_out, out_wgrad))
-    in_wgrad = joined(half, in_own, in_beside, [in_across], "in_weight_grad_joined")
+    in_wgrad = sums_into(1 - half, [in_across[1], in_beside], None, "in_weight_grad_other")
+    in_wgrad = sums_into(half, [in_own, in_across[0]], in_wgrad, "in_weight_grad_own")
     kept, other_sums = sums + moved[0], moved[1] + moved[2]
     small = jnp.where((jnp.arange(halves) == half)[:, None, None], kept[None], other_sums[None])
     tokens_grad = taken_back(cotangent, slot[:, None], back, F32, "tokens_grad")

time: 465 us -> 447 us (0.961)
  waiting for transfers between devices: 146 us -> 121 us
  local copies, waits for them, and re-layouts: 17.7 us -> 26.5 us
    ppermute x18 -> x11, waiting for transfers between devices: 146 us -> 88.1 us  [over(): return lax.ppermute(value, axis, [(i, size - 1 - i) for i in range(size)])]
    ppermute x2 -> x9, waiting for transfers between devices: 0.01 us -> 33.4 us  [diagonal(): return lax.ppermute(value, ('sub', 'half'), [(i, 3 - i) for i in range(4)])]
    squeeze x0 -> x6, local copies, waits for them, and re-layouts: none -> 11.1 us  [the longest x3 6.17 us: piece(): first[0]]
    ppermute x18 -> x11, starting transfers between devices: 15.9 us -> 7.35 us  [over(): return lax.ppermute(value, axis, [(i, size - 1 - i) for i in range(size)])]
    slice x6 -> x0, local copies, waits for them, and re-layouts: 7.7 us -> none  [piece(): return [other[0][:, start:end], other[1][start:end]]]
    ppermute x2 -> x9, starting transfers between devices: 1.69 us -> 8.63 us  [diagonal(): return lax.ppermute(value, ('sub', 'half'), [(i, 3 - i) for i in range(4)])]
    pallas_call x14, Pallas kernels: 215 us -> 209 us  [call(): pl.pallas_call(kernel, grid=(steps,), in_specs=[spec(a.shape, block, inde...]
    pallas_call x2 -> x4, Pallas kernels: 15.3 us -> 20 us  [sums_into(): pl.pallas_call(kernel, grid_spec=pltpu.PrefetchScalarGridSpec(num_scalar_...]
  transfers between devices with their start and end apart: 24 -> 24, of which waited for: 9 -> 8; matrix products, arithmetic and copies ran while one was open for 6% -> 9% of each run, Pallas kernels for 48% -> 50%
where the time goes in v3:
time: 447 us; the launch traced here: 440 us
  Pallas kernels  230 us (51%)
  waiting for transfers between devices  121 us (27%)
  starting transfers between devices  46.9 us (10%)
  local copies, waits for them, and re-layouts  26.5 us (6%)
  matrix products  12.5 us (3%)
    pallas_call x14, Pallas kernels, call(): pl.pallas_call(kernel, grid=(steps,), in_specs=[spec(a.shape, block, inde...  209 us
    ppermute x11, waiting for transfers between devices, over(): return lax.ppermute(value, axis, [(i, size - 1 - i) for i in range(size)])  88.1 us
    ppermute x9, waiting for transfers between devices, diagonal(): return lax.ppermute(value, ('sub', 'half'), [(i, 3 - i) for i in range(4)])  33.4 us
    all_to_all x4, starting transfers between devices, exchange(): lax.all_to_all(rows, ('expert', 'half'), split_axis=0, concat_axis=0, til...  30.9 us
    pallas_call x4, Pallas kernels, sums_into(): pl.pallas_call(kernel, grid_spec=pltpu.PrefetchScalarGridSpec(num_scalar_...  20 us
    dot_general x2, matrix products, place(): return jnp.dot(chosen, values, preferred_element_type=F32).astype(BF16)  12 us
    squeeze x4, local copies, waits for them, and re-layouts, pick(): return lax.dynamic_index_in_dim(stacked, index, 0, keepdims=False)  11.2 us
  transfers between devices with their start and end apart: 24, of which 8 were waited for; matrix products, arithmetic and copies ran while one was open for 9% of the time, Pallas kernels for 50%

profile of v3, /device:TPU:0, one launch (start us, length us, event | category | flops | bytes accessed | tf_op | source)
XLA Modules:
  0.0 440.4 jit_solution(1562176741084981148)
XLA Ops:
  1.2 1.9 dynamic-slice_bitcast_fusion.3.rest_0_
  3.1 2.6 collective-permute-start
  5.9 3.1 dynamic-slice_bitcast_fusion.2.rest_1_
  10.5 6.0 %fusion.5 = bf16[2048,1024]{1,0:T(8,128)(2,1)} fusion(bf16[1024,1024]{1,0:T(8,128)(2,1)S(1)} %copy-done.5, s32[1024]{0:T(1024)S(1)} %get-tuple-element.135), kind=kOutput, calls=%fused_computation.7 | convolution fusion | flops 4299161600 | bytes 6295552 | tf_op jit(solution)/shard_map/dot_general | solution.py:304
  16.6 6.1 %all-to-all-start = ((bf16[16,128,1024]{2,1,0:T(8,128)(2,1)}), bf16[16,128,1024]{2,1,0:T(8,128)(2,1)}, u32[]{:S(2)}, u32[]{:S(2)}) async-start(bf16[16,128,1024]{2,1,0:T(8,128)(2,1)} %bitcast.43), calls=%async_computation | async-start | bytes 8388608 | tf_op jit(solution)/shard_map/all_to_all | solution.py:308
  22.7 1.8 dynamic-slice_bitcast_fusion.9
  24.5 1.7 dynamic-slice_bitcast_fusion.8
  26.1 1.9 dynamic-slice_bitcast_fusion.6
  28.0 1.9 dynamic-slice_bitcast_fusion.7
  29.9 1.4 dynamic-slice_bitcast_fusion.4
  31.3 2.5 dynamic-slice_bitcast_fusion.5
  33.8 6.0 %fusion.6 = bf16[2048,1024]{1,0:T(8,128)(2,1)} fusion(bf16[1024,1024]{1,0:T(8,128)(2,1)S(1)} %copy-done.8, s32[1024]{0:T(1024)S(1)} %get-tuple-element.135), kind=kOutput, calls=%fused_computation.8 | convolution fusion | flops 4299161600 | bytes 6295552 | tf_op jit(solution)/shard_map/dot_general | solution.py:304
  39.8 12.5 %collective-permute-done.array.rest_4_ = bf16[1024,1024]{1,0:T(8,128)(2,1)} collective-permute-done((bf16[1024,1024]{1,0:T(8,128)(2,1)S(1)}, bf16[1024,1024]{1,0:T(8,128)(2,1)}, u32[]{:S(2)}, u32[]{:S(2)}) %collective-permute-start) | collective-permute-done | bytes 2097184 | tf_op jit(solution)/shard_map/ppermute | solution.py:314
  52.3 1.3 waited.1.rest_6_
  55.4 3.1 dynamic-slice_bitcast_fusion.rest_3_
  58.5 3.1 dynamic-slice_bitcast_fusion.1.rest_2_
  61.6 35.6 %collective-permute-done.3.rest_5_ = bf16[1024,1024]{1,0:T(8,128)(2,1)} collective-permute-done((bf16[1024,1024]{1,0:T(8,128)(2,1)}, bf16[1024,1024]{1,0:T(8,128)(2,1)}, u32[]{:S(2)}, u32[]{:S(2)}) %collective-permute-start.3) | collective-permute-done | bytes 2097184 | tf_op jit(solution)/shard_map/ppermute | solution.py:314
  97.2 5.1 %collective-permute-done.4.rest_0_.rest_6_ = bf16[1024,128]{1,0:T(8,128)(2,1)S(1)} collective-permute-done((bf16[1024,128]{1,0:T(8,128)(2,1)S(1)}, bf16[1024,128]{1,0:T(8,128)(2,1)S(1)}, u32[]{:S(2)}, u32[]{:S(2)}) %collective-permute-start.4) | collective-permute-done | bytes 262176 | tf_op jit(solution)/shard_map/ppermute | solution.py:317
  102.3 5.6 %collective-permute-done.5.rest_1_.rest_7_ = bf16[128,1024]{1,0:T(8,128)(2,1)S(1)} collective-permute-done((bf16[128,1024]{1,0:T(8,128)(2,1)S(1)}, bf16[128,1024]{1,0:T(8,128)(2,1)S(1)}, u32[]{:S(2)}, u32[]{:S(2)}) %collective-permute-start.5) | collective-permute-done | bytes 262176 | tf_op jit(solution)/shard_map/ppermute | solution.py:317
  108.6 11.8 %all-to-all-start.1 = ((bf16[16,128,1024]{2,1,0:T(8,128)(2,1)}), bf16[16,128,1024]{2,1,0:T(8,128)(2,1)}, u32[]{:S(2)}, u32[]{:S(2)}) async-start(bf16[16,128,1024]{2,1,0:T(8,128)(2,1)} %bitcast.42), calls=%async_computation.1 | async-start | bytes 8388608 | tf_op jit(solution)/shard_map/all_to_all | solution.py:308
  120.4 1.6 collective-permute-start.6
  123.4 41.8 %forward_near.1 = (bf16[2048,1024]{1,0:T(8,128)(2,1)}, bf16[2048,3072]{1,0:T(8,128)(2,1)}, bf16[2048,3072]{1,0:T(8,128)(2,1)}, f32[2048,1024]{1,0:T(8,128)}, f32[2048,128]{1,0:T(8,128)}) custom-call(bf16[2048,1024]{1,0:T(8,128)(2,1)} %bitcast.2.x, f32[1,1024]{1,0:T(1,128)} %dynamic-slice_convert_fusion.2.gain, f32[1,1024]{1,0:T(1,128)} %get-tuple-element.137.bias, ...), custom_call_target="tpu_custom_call" | custom-call | flops 1000 | bytes 1000 | tf_op jit(solution)/shard_map/forward_near/pallas_call | solution.py:135
  165.2 13.8 %collective-permute-done.7.rest_3_.rest_9_ = bf16[640,1024]{1,0:T(8,128)(2,1)S(1)} collective-permute-done((bf16[640,1024]{1,0:T(8,128)(2,1)S(1)}, bf16[640,1024]{1,0:T(8,128)(2,1)S(1)}, u32[]{:S(2)}, u32[]{:S(2)}) %collective-permute-start.7) | collective-permute-done | bytes 1310752 | tf_op jit(solution)/shard_map/ppermute | solution.py:317
  179.0 1.5 collective-permute-start.9
  180.7 14.4 %forward_more.1 = (bf16[2048,1024]{1,0:T(8,128)(2,1)}, bf16[2048,1024]{1,0:T(8,128)(2,1)}, f32[2048,1024]{1,0:T(8,128)}) custom-call(bf16[2048,1024]{1,0:T(8,128)(2,1)} %get-tuple-element.84.rows.a, f32[2048,1024]{1,0:T(8,128)} %get-tuple-element.85.near, bf16[1024,128]{1,0:T(8,128)(2,1)} %copy-done.10, bf16[128,1024]{1,0:T(8,128)(2,1)} %copy-done.11, ...), custom_call_target="tpu_custom_call" | custom-call | flops 1000 | bytes 1000 | tf_op jit(solution)/shard_map/forward_more/pallas_call | solution.py:135
  195.2 8.9 %collective-permute-done.8.first.rest_10_ = bf16[1024,256]{1,0:T(8,128)(2,1)S(1)} collective-permute-done((bf16[1024,256]{1,0:T(8,128)(2,1)S(1)}, bf16[1024,256]{1,0:T(8,128)(2,1)S(1)}, u32[]{:S(2)}, u32[]{:S(2)}) %collective-permute-start.8) | collective-permute-done | bytes 524320 | tf_op jit(solution)/shard_map/ppermute | solution.py:317
  204.9 10.7 %forward_last.1 = (bf16[2048,1024]{1,0:T(8,128)(2,1)}, bf16[2048,1024]{1,0:T(8,128)(2,1)}, bf16[2048,1024]{1,0:T(8,128)(2,1)}) custom-call(bf16[2048,1024]{1,0:T(8,128)(2,1)} %get-tuple-element.84.rows.a, f32[2048,1024]{1,0:T(8,128)} %get-tuple-element.90.near, f32[2048,128]{1,0:T(8,128)} %get-tuple-element.91.gates, ...), custom_call_target="tpu_custom_call", output_to_operand_aliasing={{0}: (5, {}), {1}: (6, {})} | custom-call | flops 1000 | bytes 1000 | tf_op jit(solution)/shard_map/forward_last/pallas_call | solution.py:135
  215.6 6.9 %all-to-all-start.2 = ((bf16[16,128,1024]{2,1,0:T(8,128)(2,1)}), bf16[16,128,1024]{2,1,0:T(8,128)(2,1)}, u32[]{:S(2)}, u32[]{:S(2)}) async-start(bf16[16,128,1024]{2,1,0:T(8,128)(2,1)} %bitcast.40), calls=%async_computation.2 | async-start | bytes 8388608 | tf_op jit(solution)/shard_map/all_to_all | solution.py:308
  222.5 9.6 %out_weight_grad.4 = (bf16[1024,1024]{1,0:T(8,128)(2,1)}, bf16[2048,1024]{1,0:T(8,128)(2,1)}) custom-call(bf16[2048,1024]{1,0:T(8,128)(2,1)} %get-tuple-element.102.a, bf16[2048,1024]{1,0:T(8,128)(2,1)} %bitcast.14.dy, f32[2048,128]{1,0:T(8,128)} %get-tuple-element.91.gates), custom_call_target="tpu_custom_call" | custom-call | flops 1000 | bytes 1000 | tf_op jit(solution)/shard_map/out_weight_grad/pallas_call | solution.py:135
  232.1 1.4 collective-permute-start.10
  233.5 8.6 %out_weight_grad.5 = bf16[1024,1024]{1,0:T(8,128)(2,1)} custom-call(bf16[2048,3072]{1,0:T(8,128)(2,1)} %get-tuple-element.116.a, bf16[2048,1024]{1,0:T(8,128)(2,1)} %get-tuple-element.103.b), custom_call_target="tpu_custom_call" | custom-call | flops 1000 | bytes 1000 | tf_op jit(solution)/shard_map/out_weight_grad/pallas_call | solution.py:135
  242.7 52.4 %backward.1 = (bf16[2048,3072]{1,0:T(8,128)(2,1)}, bf16[2048,1024]{1,0:T(8,128)(2,1)}, bf16[2048,1024]{1,0:T(8,128)(2,1)}, f32[8,1024]{1,0:T(8,128)}) custom-call(bf16[2048,1024]{1,0:T(8,128)(2,1)} %bitcast.2.x, bf16[2048,1024]{1,0:T(8,128)(2,1)} %bitcast.14.dy, bf16[2048,1024]{1,0:T(8,128)(2,1)} %get-tuple-element.106.gated, ...), custom_call_target="tpu_custom_call" | custom-call | flops 1000 | bytes 1000 | tf_op jit(solution)/shard_map/backward/pallas_call | solution.py:135
  295.1 1.5 collective-permute-start.12
  297.3 8.6 %out_weight_grad.6 = bf16[1024,1024]{1,0:T(8,128)(2,1)} custom-call(bf16[2048,3072]{1,0:T(8,128)(2,1)} %get-tuple-element.116.a, bf16[2048,1024]{1,0:T(8,128)(2,1)} %get-tuple-element.103.b), custom_call_target="tpu_custom_call" | custom-call | flops 1000 | bytes 1000 | tf_op jit(solution)/shard_map/out_weight_grad/pallas_call | solution.py:135
  306.0 8.7 %in_weight_grad.6 = bf16[1024,1024]{1,0:T(8,128)(2,1)} custom-call(bf16[2048,1024]{1,0:T(8,128)(2,1)} %get-tuple-element.84.rows.a, bf16[2048,3072]{1,0:T(8,128)(2,1)} %get-tuple-element.109.b), custom_call_target="tpu_custom_call" | custom-call | flops 1000 | bytes 1000 | tf_op jit(solution)/shard_map/in_weight_grad/pallas_call | solution.py:135
  314.6 9.3 %in_weight_grad.5 = bf16[1024,1024]{1,0:T(8,128)(2,1)} custom-call(bf16[2048,1024]{1,0:T(8,128)(2,1)} %get-tuple-element.84.rows.a, bf16[2048,1024]{1,0:T(8,128)(2,1)} %get-tuple-element.112.b), custom_call_target="tpu_custom_call" | custom-call | flops 1000 | bytes 1000 | tf_op jit(solution)/shard_map/in_weight_grad/pallas_call | solution.py:135
  323.9 2.3 collective-permute-done.12
  326.3 6.1 %all-to-all-start.3 = ((bf16[16,128,1024]{2,1,0:T(8,128)(2,1)}), bf16[16,128,1024]{2,1,0:T(8,128)(2,1)}, u32[]{:S(2)}, u32[]{:S(2)}) async-start(bf16[16,128,1024]{2,1,0:T(8,128)(2,1)} %bitcast.41), calls=%async_computation.3 | async-start | bytes 8388608 | tf_op jit(solution)/shard_map/all_to_all | solution.py:308
  334.7 9.1 %in_weight_grad.7 = (bf16[512,1024]{1,0:T(8,128)(2,1)}, bf16[512,1024]{1,0:T(8,128)(2,1)}) custom-call(bf16[2048,1024]{1,0:T(8,128)(2,1)} %get-tuple-element.84.rows.a, bf16[2048,3072]{1,0:T(8,128)(2,1)} %get-tuple-element.109.b), custom_call_target="tpu_custom_call" | custom-call | flops 1000 | bytes 1000 | tf_op jit(solution)/shard_map/in_weight_grad/pallas_call | solution.py:135
  345.3 8.8 %in_weight_grad.4.refs_0_ = f32[1024,1024]{1,0:T(8,128)} custom-call(bf16[2048,1024]{1,0:T(8,128)(2,1)} %get-tuple-element.84.rows.a, bf16[2048,3072]{1,0:T(8,128)(2,1)} %get-tuple-element.109.b), custom_call_target="tpu_custom_call" | custom-call | flops 1000 | bytes 1000 | tf_op jit(solution)/shard_map/in_weight_grad/pallas_call | solution.py:135
  354.1 9.0 %out_weight_grad.7.refs_0_ = f32[1024,1024]{1,0:T(8,128)} custom-call(bf16[2048,3072]{1,0:T(8,128)(2,1)} %get-tuple-element.116.a, bf16[2048,1024]{1,0:T(8,128)(2,1)} %get-tuple-element.103.b), custom_call_target="tpu_custom_call" | custom-call | flops 1000 | bytes 1000 | tf_op jit(solution)/shard_map/out_weight_grad/pallas_call | solution.py:135
  363.1 8.7 %layer_out.1 = bf16[1024,1024]{1,0:T(8,128)(2,1)} custom-call(bf16[1024,1024]{1,0:T(8,128)(2,1)} %base.2, s32[1024,1]{1,0:T(8,128)} %copy.24.slot, bf16[2048,1024]{1,0:T(8,128)(2,1)} %bitcast.17.arrived), custom_call_target="tpu_custom_call" | custom-call | flops 1000 | bytes 1000 | tf_op jit(solution)/shard_map/layer_out/pallas_call | solution.py:135
  372.5 4.8 %out_weight_grad_other.1.refs_2_ = f32[2,1024,1024]{2,1,0:T(8,128)} custom-call(s32[1]{0:T(128)} %bitcast.19.number, bf16[1024,1024]{1,0:T(8,128)(2,1)} %copy-done.6, bf16[1024,1024]{1,0:T(8,128)(2,1)} %collective-permute-done.15.refs_1_), custom_call_target="tpu_custom_call" | custom-call | flops 1000 | bytes 1000 | tf_op jit(solution)/shard_map/out_weight_grad_other/pallas_call | solution.py:230
  377.3 5.1 %out_weight_grad_own.1 = f32[2,1024,1024]{2,1,0:T(8,128)} custom-call(s32[1]{0:T(128)} %bitcast.18.number, f32[1024,1024]{1,0:T(8,128)} %out_weight_grad.7.refs_0_, bf16[1024,1024]{1,0:T(8,128)(2,1)} %collective-permute-done.11.refs_1_, f32[2,1024,1024]{2,1,0:T(8,128)} %out_weight_grad_other.1.refs_2_), custom_call_target="tpu_custom_call", output_to_operand_aliasing={{}: (3, {})} | custom-call | flops 1000 | bytes 1000 | tf_op jit(solution)/shard_map/out_weight_grad_own/pallas_call | solution.py:230
  383.4 5.0 %in_weight_grad_other.1.refs_2_ = f32[2,1024,1024]{2,1,0:T(8,128)} custom-call(s32[1]{0:T(128)} %bitcast.19.number, bf16[1024,1024]{1,0:T(8,128)(2,1)} %collective-permute-done.17.refs_0_, bf16[512,1024]{1,0:T(8,128)(2,1)} %copy-done.12, bf16[512,1024]{1,0:T(8,128)(2,1)} %collective-permute-done.19.refs_2_), custom_call_target="tpu_custom_call" | custom-call | flops 1000 | bytes 1000 | tf_op jit(solution)/shard_map/in_weight_grad_other/pallas_call | solution.py:230
  388.4 37.7 %collective-permute-done.16.refs_1_ = bf16[1024,1024]{1,0:T(8,128)(2,1)} collective-permute-done((bf16[1024,1024]{1,0:T(8,128)(2,1)S(1)}, bf16[1024,1024]{1,0:T(8,128)(2,1)}, u32[]{:S(2)}, u32[]{:S(2)}) %collective-permute-start.16) | collective-permute-done | bytes 2097184 | tf_op jit(solution)/shard_map/ppermute | solution.py:314
  426.1 5.1 %in_weight_grad_own.1 = f32[2,1024,1024]{2,1,0:T(8,128)} custom-call(s32[1]{0:T(128)} %bitcast.18.number, f32[1024,1024]{1,0:T(8,128)} %in_weight_grad.4.refs_0_, bf16[1024,1024]{1,0:T(8,128)(2,1)} %collective-permute-done.16.refs_1_, f32[2,1024,1024]{2,1,0:T(8,128)} %in_weight_grad_other.1.refs_2_), custom_call_target="tpu_custom_call", output_to_operand_aliasing={{}: (3, {})} | custom-call | flops 1000 | bytes 1000 | tf_op jit(solution)/shard_map/in_weight_grad_own/pallas_call | solution.py:230
  431.2 9.0 %tokens_grad.1 = f32[1024,1024]{1,0:T(8,128)} custom-call(bf16[1024,1024]{1,0:T(8,128)(2,1)} %base.3, s32[1024,1]{1,0:T(8,128)} %copy.24.slot, bf16[2048,1024]{1,0:T(8,128)(2,1)} %bitcast.21.arrived), custom_call_target="tpu_custom_call" | custom-call | flops 1000 | bytes 1000 | tf_op jit(solution)/shard_map/tokens_grad/pallas_call | solution.py:135
  (88 shorter events, 13.9 us)
Async XLA Ops:
  0.6 57.8 %collective-permute-start.1 = (bf16[2,1024,1024]{2,1,0:T(8,128)(2,1)}, bf16[2,1024,1024]{2,1,0:T(8,128)(2,1)}, u32[]{:S(2)}, u32[]{:S(2)}) collective-permute-start(bf16[2,1024,1024]{2,1,0:T(8,128)(2,1)} %param.14), channel_id=1, source_target_pairs={{0,1},{1,0},{2,3},{3,2},{4,5},{5,4},{6,7},{7,6},{8,9},{9,8},{10,11... | collective-permute-start | bytes 12582920 | tf_op jit(solution)/shard_map/ppermute | solution.py:314
  1.1 8.3 %copy-start.17 = (s32[1024,1]{0,1:T(1,128)S(1)}, s32[1024,1]{0,1:T(1,128)}, u32[]{:S(2)}) copy-start(s32[1024,1]{0,1:T(1,128)} %param.9) | copy-start | bytes 12292
  1.2 9.4 %copy-start.5 = (bf16[1024,1024]{1,0:T(8,128)(2,1)S(1)}, bf16[1024,1024]{1,0:T(8,128)(2,1)}, u32[]{:S(2)}) copy-start(bf16[1024,1024]{1,0:T(8,128)(2,1)} %base.2) | copy-start | bytes 6291460
  3.1 13.5 %copy-start = (bf16[1024,1024]{1,0:T(8,128)(2,1)}, bf16[1024,1024]{1,0:T(8,128)(2,1)S(1)}, u32[]{:S(2)}) copy-start(bf16[1024,1024]{1,0:T(8,128)(2,1)S(1)} %dynamic-slice_bitcast_fusion.3.rest_0_) | copy-start | bytes 6291460
  3.1 49.2 %collective-permute-start = (bf16[1024,1024]{1,0:T(8,128)(2,1)S(1)}, bf16[1024,1024]{1,0:T(8,128)(2,1)}, u32[]{:S(2)}, u32[]{:S(2)}) collective-permute-start(bf16[1024,1024]{1,0:T(8,128)(2,1)S(1)} %dynamic-slice_bitcast_fusion.3.rest_0_), channel_id=1, source_target_pairs={{0,2},{2,0},{1,3},{3,1},{4,6},{6,4},{5,7},{7,5},{8,10},{10,8},{9,1... | collective-permute-start | bytes 6291464 | tf_op jit(solution)/shard_map/ppermute | solution.py:314
  5.7 49.7 %collective-permute-start.2 = (bf16[2,1024,1024]{2,1,0:T(8,128)(2,1)}, bf16[2,1024,1024]{2,1,0:T(8,128)(2,1)}, u32[]{:S(2)}, u32[]{:S(2)}) collective-permute-start(bf16[2,1024,1024]{2,1,0:T(8,128)(2,1)} %param.15), channel_id=1, source_target_pairs={{0,1},{1,0},{2,3},{3,2},{4,5},{5,4},{6,7},{7,6},{8,9},{9,8},{10,11... | collective-permute-start | bytes 12582920 | tf_op jit(solution)/shard_map/ppermute | solution.py:314
  9.0 88.2 %collective-permute-start.3 = (bf16[1024,1024]{1,0:T(8,128)(2,1)}, bf16[1024,1024]{1,0:T(8,128)(2,1)}, u32[]{:S(2)}, u32[]{:S(2)}) collective-permute-start(bf16[1024,1024]{1,0:T(8,128)(2,1)} %dynamic-slice_bitcast_fusion.2.rest_1_), channel_id=1, source_target_pairs={{0,2},{2,0},{1,3},{3,1},{4,6},{6,4},{5,7},{7,5},{8,10},{10,8},{9,1... | collective-permute-start | bytes 6291464 | tf_op jit(solution)/shard_map/ppermute | solution.py:314
  16.6 91.3 %all-to-all-start = ((bf16[16,128,1024]{2,1,0:T(8,128)(2,1)}), bf16[16,128,1024]{2,1,0:T(8,128)(2,1)}, u32[]{:S(2)}, u32[]{:S(2)}) async-start(bf16[16,128,1024]{2,1,0:T(8,128)(2,1)} %bitcast.43), calls=%async_computation | async-start | bytes 8388608 | tf_op jit(solution)/shard_map/all_to_all | solution.py:308
  22.6 11.1 %copy-start.8 = (bf16[1024,1024]{1,0:T(8,128)(2,1)S(1)}, bf16[1024,1024]{1,0:T(8,128)(2,1)}, u32[]{:S(2)}) copy-start(bf16[1024,1024]{1,0:T(8,128)(2,1)} %base.3) | copy-start | bytes 6291460
  52.3 1.3 copy-start.15
  52.3 2.1 copy-start.14
  53.6 48.7 %collective-permute-start.4 = (bf16[1024,128]{1,0:T(8,128)(2,1)S(1)}, bf16[1024,128]{1,0:T(8,128)(2,1)S(1)}, u32[]{:S(2)}, u32[]{:S(2)}) collective-permute-start(bf16[1024,128]{1,0:T(8,128)(2,1)S(1)} %copy-done.15), channel_id=1, source_target_pairs={{0,3},{1,2},{2,1},{3,0},{4,7},{5,6},{6,5},{7,4},{8,11},{9,10},{10,... | collective-permute-start | bytes 786440 | tf_op jit(solution)/shard_map/ppermute | solution.py:317
  54.4 53.5 %collective-permute-start.5 = (bf16[128,1024]{1,0:T(8,128)(2,1)S(1)}, bf16[128,1024]{1,0:T(8,128)(2,1)S(1)}, u32[]{:S(2)}, u32[]{:S(2)}) collective-permute-start(bf16[128,1024]{1,0:T(8,128)(2,1)S(1)} %copy-done.14), channel_id=1, source_target_pairs={{0,3},{1,2},{2,1},{3,0},{4,7},{5,6},{6,5},{7,4},{8,11},{9,10},{10,... | collective-permute-start | bytes 786440 | tf_op jit(solution)/shard_map/ppermute | solution.py:317
  102.3 5.7 %copy-start.10 = (bf16[1024,128]{1,0:T(8,128)(2,1)}, bf16[1024,128]{1,0:T(8,128)(2,1)S(1)}, u32[]{:S(2)}) copy-start(bf16[1024,128]{1,0:T(8,128)(2,1)S(1)} %collective-permute-done.4.rest_0_.rest_6_) | copy-start | bytes 786436
  107.9 0.7 copy-start.11
  107.9 12.5 %copy-start.9 = (bf16[1024,640]{1,0:T(8,128)(2,1)S(1)}, bf16[1024,640]{1,0:T(8,128)(2,1)}, u32[]{:S(2)}) copy-start(bf16[1024,640]{1,0:T(8,128)(2,1)} %dynamic-slice_bitcast_fusion.5) | copy-start | bytes 3932164
  107.9 14.3 %copy-start.20 = (bf16[2,1024]{1,0:T(2,128)(2,1)S(1)}, bf16[2,1024]{1,0:T(2,128)(2,1)}, u32[]{:S(2)}) copy-start(bf16[2,1024]{1,0:T(2,128)(2,1)} %param.11) | copy-start | bytes 12292
  107.9 14.9 %copy-start.21 = (bf16[2,1024]{1,0:T(2,128)(2,1)S(1)}, bf16[2,1024]{1,0:T(2,128)(2,1)}, u32[]{:S(2)}) copy-start(bf16[2,1024]{1,0:T(2,128)(2,1)} %param.13) | copy-start | bytes 12292
  107.9 14.9 %copy-start.22 = (bf16[2,1024]{1,0:T(2,128)(2,1)S(1)}, bf16[2,1024]{1,0:T(2,128)(2,1)}, u32[]{:S(2)}) copy-start(bf16[2,1024]{1,0:T(2,128)(2,1)} %param.12) | copy-start | bytes 12292
  108.6 107.0 %all-to-all-start.1 = ((bf16[16,128,1024]{2,1,0:T(8,128)(2,1)}), bf16[16,128,1024]{2,1,0:T(8,128)(2,1)}, u32[]{:S(2)}, u32[]{:S(2)}) async-start(bf16[16,128,1024]{2,1,0:T(8,128)(2,1)} %bitcast.42), calls=%async_computation.1 | async-start | bytes 8388608 | tf_op jit(solution)/shard_map/all_to_all | solution.py:308
  120.4 44.8 %collective-permute-start.6 = (bf16[1024,640]{1,0:T(8,128)(2,1)S(1)}, bf16[1024,640]{1,0:T(8,128)(2,1)S(1)}, u32[]{:S(2)}, u32[]{:S(2)}) collective-permute-start(bf16[1024,640]{1,0:T(8,128)(2,1)S(1)} %copy-done.9), channel_id=1, source_target_pairs={{0,3},{1,2},{2,1},{3,0},{4,7},{5,6},{6,5},{7,4},{8,11},{9,10},{10,... | collective-permute-start | bytes 3932168 | tf_op jit(solution)/shard_map/ppermute | solution.py:317
  122.0 57.0 %collective-permute-start.7 = (bf16[640,1024]{1,0:T(8,128)(2,1)S(1)}, bf16[640,1024]{1,0:T(8,128)(2,1)S(1)}, u32[]{:S(2)}, u32[]{:S(2)}) collective-permute-start(bf16[640,1024]{1,0:T(8,128)(2,1)S(1)} %dynamic-slice_bitcast_fusion.4), channel_id=1, source_target_pairs={{0,3},{1,2},{2,1},{3,0},{4,7},{5,6},{6,5},{7,4},{8,11},{9,10},{10,... | collective-permute-start | bytes 3932168 | tf_op jit(solution)/shard_map/ppermute | solution.py:317
  123.4 57.1 %copy-start.13 = (bf16[1024,256]{1,0:T(8,128)(2,1)S(1)}, bf16[1024,256]{1,0:T(8,128)(2,1)}, u32[]{:S(2)}) copy-start(bf16[1024,256]{1,0:T(8,128)(2,1)} %dynamic-slice_bitcast_fusion.7) | copy-start | bytes 1572868
  165.2 15.6 %copy-start.1 = (bf16[1024,640]{1,0:T(8,128)(2,1)}, bf16[1024,640]{1,0:T(8,128)(2,1)S(1)}, u32[]{:S(2)}) copy-start(bf16[1024,640]{1,0:T(8,128)(2,1)S(1)} %collective-permute-done.6.rest_2_.rest_8_) | copy-start | bytes 3932164
  179.0 1.8 copy-start.2
  179.0 16.2 %collective-permute-start.9 = (bf16[256,1024]{1,0:T(8,128)(2,1)}, bf16[256,1024]{1,0:T(8,128)(2,1)S(1)}, u32[]{:S(2)}, u32[]{:S(2)}) collective-permute-start(bf16[256,1024]{1,0:T(8,128)(2,1)} %dynamic-slice_bitcast_fusion.6), channel_id=1, source_target_pairs={{0,3},{1,2},{2,1},{3,0},{4,7},{5,6},{6,5},{7,4},{8,11},{9,10},{10,... | collective-permute-start | bytes 1572872 | tf_op jit(solution)/shard_map/ppermute | solution.py:317
  180.5 23.6 %collective-permute-start.8 = (bf16[1024,256]{1,0:T(8,128)(2,1)S(1)}, bf16[1024,256]{1,0:T(8,128)(2,1)S(1)}, u32[]{:S(2)}, u32[]{:S(2)}) collective-permute-start(bf16[1024,256]{1,0:T(8,128)(2,1)S(1)} %copy-done.13), channel_id=1, source_target_pairs={{0,3},{1,2},{2,1},{3,0},{4,7},{5,6},{6,5},{7,4},{8,11},{9,10},{10,... | collective-permute-start | bytes 1572872 | tf_op jit(solution)/shard_map/ppermute | solution.py:317
  195.2 8.9 %copy-start.3 = (bf16[256,1024]{1,0:T(8,128)(2,1)}, bf16[256,1024]{1,0:T(8,128)(2,1)S(1)}, u32[]{:S(2)}) copy-start(bf16[256,1024]{1,0:T(8,128)(2,1)S(1)} %collective-permute-done.9.second.rest_11_) | copy-start | bytes 1572868
  204.1 0.8 copy-start.4
  215.6 110.7 %all-to-all-start.2 = ((bf16[16,128,1024]{2,1,0:T(8,128)(2,1)}), bf16[16,128,1024]{2,1,0:T(8,128)(2,1)}, u32[]{:S(2)}, u32[]{:S(2)}) async-start(bf16[16,128,1024]{2,1,0:T(8,128)(2,1)} %bitcast.40), calls=%async_computation.2 | async-start | bytes 8388608 | tf_op jit(solution)/shard_map/all_to_all | solution.py:308
  232.1 82.5 %collective-permute-start.10 = (bf16[1024,1024]{1,0:T(8,128)(2,1)}, bf16[1024,1024]{1,0:T(8,128)(2,1)S(1)}, u32[]{:S(2)}, u32[]{:S(2)}) collective-permute-start(bf16[1024,1024]{1,0:T(8,128)(2,1)} %get-tuple-element.104), channel_id=1, source_target_pairs={{0,3},{1,2},{2,1},{3,0},{4,7},{5,6},{6,5},{7,4},{8,11},{9,10},{10,... | collective-permute-start | bytes 6291464 | tf_op jit(solution)/shard_map/ppermute | solution.py:317
  242.1 84.1 %collective-permute-start.11 = (bf16[1024,1024]{1,0:T(8,128)(2,1)}, bf16[1024,1024]{1,0:T(8,128)(2,1)}, u32[]{:S(2)}, u32[]{:S(2)}) collective-permute-start(bf16[1024,1024]{1,0:T(8,128)(2,1)} %out_weight_grad.5), channel_id=1, source_target_pairs={{0,2},{2,0},{1,3},{3,1},{4,6},{6,4},{5,7},{7,5},{8,10},{10,8},{9,1... | collective-permute-start | bytes 6291464 | tf_op jit(solution)/shard_map/ppermute | solution.py:314
  295.1 31.1 %collective-permute-start.12 = (f32[8,1024]{1,0:T(8,128)}, f32[8,1024]{1,0:T(8,128)S(1)}, u32[]{:S(2)}, u32[]{:S(2)}) collective-permute-start(f32[8,1024]{1,0:T(8,128)} %get-tuple-element.114), channel_id=1, source_target_pairs={{0,2},{2,0},{1,3},{3,1},{4,6},{6,4},{5,7},{7,5},{8,10},{10,8},{9,1... | collective-permute-start | bytes 98312 | tf_op jit(solution)/shard_map/ppermute | solution.py:314
  296.7 29.6 %collective-permute-start.13 = (f32[8,1024]{1,0:T(8,128)}, f32[8,1024]{1,0:T(8,128)S(1)}, u32[]{:S(2)}, u32[]{:S(2)}) collective-permute-start(f32[8,1024]{1,0:T(8,128)} %get-tuple-element.114), channel_id=1, source_target_pairs={{0,1},{1,0},{2,3},{3,2},{4,5},{5,4},{6,7},{7,6},{8,9},{9,8},{10,11... | collective-permute-start | bytes 98312 | tf_op jit(solution)/shard_map/ppermute | solution.py:314
  296.7 29.6 %collective-permute-start.14 = (f32[8,1024]{1,0:T(8,128)}, f32[8,1024]{1,0:T(8,128)S(1)}, u32[]{:S(2)}, u32[]{:S(2)}) collective-permute-start(f32[8,1024]{1,0:T(8,128)} %get-tuple-element.114), channel_id=1, source_target_pairs={{0,3},{1,2},{2,1},{3,0},{4,7},{5,6},{6,5},{7,4},{8,11},{9,10},{10,... | collective-permute-start | bytes 98312 | tf_op jit(solution)/shard_map/ppermute | solution.py:317
  314.6 9.3 %copy-start.6 = (bf16[1024,1024]{1,0:T(8,128)(2,1)}, bf16[1024,1024]{1,0:T(8,128)(2,1)S(1)}, u32[]{:S(2)}) copy-start(bf16[1024,1024]{1,0:T(8,128)(2,1)S(1)} %collective-permute-done.10.refs_0_) | copy-start | bytes 6291460
  326.3 7.8 %copy-start.7 = (bf16[1024,1024]{1,0:T(8,128)(2,1)S(1)}, bf16[1024,1024]{1,0:T(8,128)(2,1)}, u32[]{:S(2)}) copy-start(bf16[1024,1024]{1,0:T(8,128)(2,1)} %in_weight_grad.6) | copy-start | bytes 6291460
  326.3 104.9 %all-to-all-start.3 = ((bf16[16,128,1024]{2,1,0:T(8,128)(2,1)}), bf16[16,128,1024]{2,1,0:T(8,128)(2,1)}, u32[]{:S(2)}, u32[]{:S(2)}) async-start(bf16[16,128,1024]{2,1,0:T(8,128)(2,1)} %bitcast.41), calls=%async_computation.3 | async-start | bytes 8388608 | tf_op jit(solution)/shard_map/all_to_all | solution.py:308
  332.4 11.8 %copy-start.18 = (s32[1024,1]{0,1:T(1,128)S(1)}, s32[1024,1]{0,1:T(1,128)}, u32[]{:S(2)}) copy-start(s32[1024,1]{0,1:T(1,128)} %param.9) | copy-start | bytes 12292
  332.4 11.8 %copy-start.19 = (s32[1024]{0:T(1024)S(1)}, s32[1024]{0:T(1024)}, u32[]{:S(2)}) copy-start(s32[1024]{0:T(1024)} %get-tuple-element.134) | copy-start | bytes 12292
  332.4 40.1 %collective-permute-start.15 = (bf16[1024,1024]{1,0:T(8,128)(2,1)}, bf16[1024,1024]{1,0:T(8,128)(2,1)}, u32[]{:S(2)}, u32[]{:S(2)}) collective-permute-start(bf16[1024,1024]{1,0:T(8,128)(2,1)} %out_weight_grad.6), channel_id=1, source_target_pairs={{0,1},{1,0},{2,3},{3,2},{4,5},{5,4},{6,7},{7,6},{8,9},{9,8},{10,11... | collective-permute-start | bytes 6291464 | tf_op jit(solution)/shard_map/ppermute | solution.py:314
  332.9 49.5 %collective-permute-start.17 = (bf16[1024,1024]{1,0:T(8,128)(2,1)}, bf16[1024,1024]{1,0:T(8,128)(2,1)}, u32[]{:S(2)}, u32[]{:S(2)}) collective-permute-start(bf16[1024,1024]{1,0:T(8,128)(2,1)} %in_weight_grad.5), channel_id=1, source_target_pairs={{0,3},{1,2},{2,1},{3,0},{4,7},{5,6},{6,5},{7,4},{8,11},{9,10},{10,... | collective-permute-start | bytes 6291464 | tf_op jit(solution)/shard_map/ppermute | solution.py:317
  334.1 92.0 %collective-permute-start.16 = (bf16[1024,1024]{1,0:T(8,128)(2,1)S(1)}, bf16[1024,1024]{1,0:T(8,128)(2,1)}, u32[]{:S(2)}, u32[]{:S(2)}) collective-permute-start(bf16[1024,1024]{1,0:T(8,128)(2,1)S(1)} %copy-done.7), channel_id=1, source_target_pairs={{0,2},{2,0},{1,3},{3,1},{4,6},{6,4},{5,7},{7,5},{8,10},{10,8},{9,1... | collective-permute-start | bytes 6291464 | tf_op jit(solution)/shard_map/ppermute | solution.py:314
  343.7 38.7 %collective-permute-start.18 = (bf16[512,1024]{1,0:T(8,128)(2,1)}, bf16[512,1024]{1,0:T(8,128)(2,1)S(1)}, u32[]{:S(2)}, u32[]{:S(2)}) collective-permute-start(bf16[512,1024]{1,0:T(8,128)(2,1)} %get-tuple-element.128), channel_id=1, source_target_pairs={{0,1},{1,0},{2,3},{3,2},{4,5},{5,4},{6,7},{7,6},{8,9},{9,8},{10,11... | collective-permute-start | bytes 3145736 | tf_op jit(solution)/shard_map/ppermute | solution.py:314
  343.8 38.6 %collective-permute-start.19 = (bf16[512,1024]{1,0:T(8,128)(2,1)}, bf16[512,1024]{1,0:T(8,128)(2,1)}, u32[]{:S(2)}, u32[]{:S(2)}) collective-permute-start(bf16[512,1024]{1,0:T(8,128)(2,1)} %get-tuple-element.129), channel_id=1, source_target_pairs={{0,1},{1,0},{2,3},{3,2},{4,5},{5,4},{6,7},{7,6},{8,9},{9,8},{10,11... | collective-permute-start | bytes 3145736 | tf_op jit(solution)/shard_map/ppermute | solution.py:314
  363.1 8.7 %copy-start.16 = (f32[8,1024]{1,0:T(8,128)S(1)}, f32[8,1024]{1,0:T(8,128)}, u32[]{:S(2)}) copy-start(f32[8,1024]{1,0:T(8,128)} %get-tuple-element.114) | copy-start | bytes 98308
  382.4 1.0 copy-start.12

commit v4 on v3

--- a/solution.py
+++ b/solution.py
@@ -259,6 +259,45 @@
         [tiles(base, tile), tiles(slot, tile), whole(arrived)],
         [rows_out((count, width), dtype, tile)],
     )[0]
+
+
+def finish(number, own, across, held, base, slot, arrived, steps=2):
+    count, width = own.shape
+    tile, tokens = count // steps, base.shape[0] // steps
+
+    def kernel(number, own, across, base, slot, arrived, held, grad, out):
+        slots = lax.broadcasted_iota(jnp.int32, (tokens, arrived.shape[0]), 1)
+        chosen = jnp.where(slot[...] == slots, 1.0, 0.0).astype(BF16)
+        out[...] = base[...].astype(F32) + product(chosen, arrived[...])
+        grad[0] = own[...] + across[...].astype(F32)
+
+    def rows(tile, width):
+        return pl.BlockSpec((tile, width), lambda i, _: (i, 0))
+
+    return pl.pallas_call(
+        kernel,
+        grid_spec=pltpu.PrefetchScalarGridSpec(
+            num_scalar_prefetch=1,
+            grid=(steps,),
+            in_specs=[
+                rows(tile, width),
+                rows(tile, width),
+                rows(tokens, base.shape[1]),
+                rows(tokens, 1),
+                pl.BlockSpec(arrived.shape, lambda i, _: (0, 0), pipeline_mode=pl.Buffered(1)),
+                pl.BlockSpec(memory_space=pl.ANY),
+            ],
+            out_specs=[
+                pl.BlockSpec((1, tile, width), lambda i, number: (number[0], i, 0)),
+                rows(tokens, base.shape[1]),
+            ],
+        ),
+        out_shape=[jax.ShapeDtypeStruct(held.shape, F32), jax.ShapeDtypeStruct(base.shape, F32)],
+        input_output_aliases={6: 0},
+        compiler_params=pltpu.CompilerParams(vmem_limit_bytes=VMEM_LIMIT),
+        cost_estimate=pl.CostEstimate(flops=1000, transcendentals=0, bytes_accessed=1000),
+        name="in_weight_grad_own_and_tokens_grad",
+    )(number.astype(jnp.int32)[None], own, across, base, slot, arrived, held)
 
 
 def waited(array):
@@ -435,10 +474,9 @@
     out_wgrad = sums_into(half, [out_part(0, F32), out_across[0]], out_wgrad, "out_weight_grad_own")
     in_own, layer_out, out_wgrad = lax.optimization_barrier((in_part(0, F32), layer_out, out_wgrad))
     in_wgrad = sums_into(1 - half, [in_across[1], in_beside], None, "in_weight_grad_other")
-    in_wgrad = sums_into(half, [in_own, in_across[0]], in_wgrad, "in_weight_grad_own")
+    in_wgrad, tokens_grad = finish(half, in_own, in_across[0], in_wgrad, cotangent, slot[:, None], back)
     kept, other_sums = sums + moved[0], moved[1] + moved[2]
     small = jnp.where((jnp.arange(halves) == half)[:, None, None], kept[None], other_sums[None])
-    tokens_grad = taken_back(cotangent, slot[:, None], back, F32, "tokens_grad")
     return (layer_out, tokens_grad, small[:, 0], small[:, 1], small[:, 2], in_wgrad, out_wgrad)
 
 

time: 447 us -> 440 us (0.984)
    pallas_call x0 -> x1, Pallas kernels: none -> 11.3 us  [finish(): pl.pallas_call(kernel, grid_spec=pltpu.PrefetchScalarGridSpec(num_scalar_...]
    pallas_call x14 -> x13, Pallas kernels: 209 us -> 200 us  [call(): pl.pallas_call(kernel, grid=(steps,), in_specs=[spec(a.shape, block, inde...]
    pallas_call x4 -> x3, Pallas kernels: 20 us -> 14.9 us  [sums_into(): pl.pallas_call(kernel, grid_spec=pltpu.PrefetchScalarGridSpec(num_scalar_...]
where the time goes in v4:
time: 440 us; the launch traced here: 434 us
  Pallas kernels  227 us (52%)
  waiting for transfers between devices  121 us (28%)
  starting transfers between devices  43.1 us (10%)
  local copies, waits for them, and re-layouts  26.5 us (6%)
  matrix products  12.6 us (3%)
    pallas_call x13, Pallas kernels, call(): pl.pallas_call(kernel, grid=(steps,), in_specs=[spec(a.shape, block, inde...  200 us
    ppermute x11, waiting for transfers between devices, over(): return lax.ppermute(value, axis, [(i, size - 1 - i) for i in range(size)])  87.8 us
    ppermute x9, waiting for transfers between devices, diagonal(): return lax.ppermute(value, ('sub', 'half'), [(i, 3 - i) for i in range(4)])  33.4 us
    all_to_all x4, starting transfers between devices, exchange(): lax.all_to_all(rows, ('expert', 'half'), split_axis=0, concat_axis=0, til...  26.9 us
    pallas_call x3, Pallas kernels, sums_into(): pl.pallas_call(kernel, grid_spec=pltpu.PrefetchScalarGridSpec(num_scalar_...  14.9 us
    dot_general x2, matrix products, place(): return jnp.dot(chosen, values, preferred_element_type=F32).astype(BF16)  12.1 us
    pallas_call x1, Pallas kernels, finish(): pl.pallas_call(kernel, grid_spec=pltpu.PrefetchScalarGridSpec(num_scalar_...  11.3 us
    squeeze x4, local copies, waits for them, and re-layouts, pick(): return lax.dynamic_index_in_dim(stacked, index, 0, keepdims=False)  11.2 us
  transfers between devices with their start and end apart: 24, of which 8 were waited for; matrix products, arithmetic and copies ran while one was open for 9% of the time, Pallas kernels for 50%

profile of v4, /device:TPU:0, one launch (start us, length us, event | category | flops | bytes accessed | tf_op | source)
XLA Modules:
  0.0 433.7 jit_solution(3397147831073031080)
XLA Ops:
  1.2 1.9 dynamic-slice_bitcast_fusion.3.rest_0_
  3.1 2.6 collective-permute-start
  6.8 6.0 %fusion.5 = bf16[2048,1024]{1,0:T(8,128)(2,1)} fusion(bf16[1024,1024]{1,0:T(8,128)(2,1)S(1)} %copy-done.5, s32[1024]{0:T(1024)S(1)} %get-tuple-element.139), kind=kOutput, calls=%fused_computation.7 | convolution fusion | flops 4299161600 | bytes 6295552 | tf_op jit(solution)/shard_map/dot_general | solution.py:343
  12.8 6.0 %all-to-all-start = ((bf16[16,128,1024]{2,1,0:T(8,128)(2,1)}), bf16[16,128,1024]{2,1,0:T(8,128)(2,1)}, u32[]{:S(2)}, u32[]{:S(2)}) async-start(bf16[16,128,1024]{2,1,0:T(8,128)(2,1)} %bitcast.43), calls=%async_computation | async-start | bytes 8388608 | tf_op jit(solution)/shard_map/all_to_all | solution.py:347
  19.2 3.1 dynamic-slice_bitcast_fusion.2.rest_1_
  22.8 1.8 dynamic-slice_bitcast_fusion.9
  24.6 1.7 dynamic-slice_bitcast_fusion.8
  26.3 1.9 dynamic-slice_bitcast_fusion.7
  28.1 1.9 dynamic-slice_bitcast_fusion.6
  30.0 2.5 dynamic-slice_bitcast_fusion.5
  32.5 1.4 dynamic-slice_bitcast_fusion.4
  33.9 6.1 %fusion.6 = bf16[2048,1024]{1,0:T(8,128)(2,1)} fusion(bf16[1024,1024]{1,0:T(8,128)(2,1)S(1)} %copy-done.6, s32[1024]{0:T(1024)S(1)} %get-tuple-element.139), kind=kOutput, calls=%fused_computation.8 | convolution fusion | flops 4299161600 | bytes 6295552 | tf_op jit(solution)/shard_map/dot_general | solution.py:343
  40.0 12.2 %collective-permute-done.array.rest_4_ = bf16[1024,1024]{1,0:T(8,128)(2,1)} collective-permute-done((bf16[1024,1024]{1,0:T(8,128)(2,1)S(1)}, bf16[1024,1024]{1,0:T(8,128)(2,1)}, u32[]{:S(2)}, u32[]{:S(2)}) %collective-permute-start) | collective-permute-done | bytes 2097184 | tf_op jit(solution)/shard_map/ppermute | solution.py:353
  52.3 1.3 waited.1.rest_6_
  55.4 3.1 dynamic-slice_bitcast_fusion.1.rest_2_
  58.5 3.1 dynamic-slice_bitcast_fusion.rest_3_
  61.6 35.6 %collective-permute-done.3.rest_5_ = bf16[1024,1024]{1,0:T(8,128)(2,1)} collective-permute-done((bf16[1024,1024]{1,0:T(8,128)(2,1)}, bf16[1024,1024]{1,0:T(8,128)(2,1)}, u32[]{:S(2)}, u32[]{:S(2)}) %collective-permute-start.3) | collective-permute-done | bytes 2097184 | tf_op jit(solution)/shard_map/ppermute | solution.py:353
  97.2 5.1 %collective-permute-done.4.rest_0_.rest_6_ = bf16[1024,128]{1,0:T(8,128)(2,1)S(1)} collective-permute-done((bf16[1024,128]{1,0:T(8,128)(2,1)S(1)}, bf16[1024,128]{1,0:T(8,128)(2,1)S(1)}, u32[]{:S(2)}, u32[]{:S(2)}) %collective-permute-start.4) | collective-permute-done | bytes 262176 | tf_op jit(solution)/shard_map/ppermute | solution.py:356
  102.3 5.6 %collective-permute-done.5.rest_1_.rest_7_ = bf16[128,1024]{1,0:T(8,128)(2,1)S(1)} collective-permute-done((bf16[128,1024]{1,0:T(8,128)(2,1)S(1)}, bf16[128,1024]{1,0:T(8,128)(2,1)S(1)}, u32[]{:S(2)}, u32[]{:S(2)}) %collective-permute-start.5) | collective-permute-done | bytes 262176 | tf_op jit(solution)/shard_map/ppermute | solution.py:356
  108.6 7.9 %all-to-all-start.1 = ((bf16[16,128,1024]{2,1,0:T(8,128)(2,1)}), bf16[16,128,1024]{2,1,0:T(8,128)(2,1)}, u32[]{:S(2)}, u32[]{:S(2)}) async-start(bf16[16,128,1024]{2,1,0:T(8,128)(2,1)} %bitcast.42), calls=%async_computation.1 | async-start | bytes 8388608 | tf_op jit(solution)/shard_map/all_to_all | solution.py:347
  117.2 1.1 collective-permute-start.7
  119.6 41.8 %forward_near.1 = (bf16[2048,1024]{1,0:T(8,128)(2,1)}, bf16[2048,3072]{1,0:T(8,128)(2,1)}, bf16[2048,3072]{1,0:T(8,128)(2,1)}, f32[2048,1024]{1,0:T(8,128)}, f32[2048,128]{1,0:T(8,128)}) custom-call(bf16[2048,1024]{1,0:T(8,128)(2,1)} %bitcast.2.x, f32[1,1024]{1,0:T(1,128)} %dynamic-slice_convert_fusion.2.gain, f32[1,1024]{1,0:T(1,128)} %get-tuple-element.141.bias, ...), custom_call_target="tpu_custom_call" | custom-call | flops 1000 | bytes 1000 | tf_op jit(solution)/shard_map/forward_near/pallas_call | solution.py:135
  161.4 13.8 %collective-permute-done.7.rest_3_.rest_9_ = bf16[640,1024]{1,0:T(8,128)(2,1)S(1)} collective-permute-done((bf16[640,1024]{1,0:T(8,128)(2,1)S(1)}, bf16[640,1024]{1,0:T(8,128)(2,1)S(1)}, u32[]{:S(2)}, u32[]{:S(2)}) %collective-permute-start.7) | collective-permute-done | bytes 1310752 | tf_op jit(solution)/shard_map/ppermute | solution.py:356
  175.7 1.2 collective-permute-start.9
  176.9 14.4 %forward_more.1 = (bf16[2048,1024]{1,0:T(8,128)(2,1)}, bf16[2048,1024]{1,0:T(8,128)(2,1)}, f32[2048,1024]{1,0:T(8,128)}) custom-call(bf16[2048,1024]{1,0:T(8,128)(2,1)} %get-tuple-element.86.rows.a, f32[2048,1024]{1,0:T(8,128)} %get-tuple-element.87.near, bf16[1024,128]{1,0:T(8,128)(2,1)} %copy-done.10, bf16[128,1024]{1,0:T(8,128)(2,1)} %copy-done.11, ...), custom_call_target="tpu_custom_call" | custom-call | flops 1000 | bytes 1000 | tf_op jit(solution)/shard_map/forward_more/pallas_call | solution.py:135
  191.3 8.9 %collective-permute-done.9.second.rest_11_ = bf16[256,1024]{1,0:T(8,128)(2,1)S(1)} collective-permute-done((bf16[256,1024]{1,0:T(8,128)(2,1)S(1)}, bf16[256,1024]{1,0:T(8,128)(2,1)S(1)}, u32[]{:S(2)}, u32[]{:S(2)}) %collective-permute-start.9) | collective-permute-done | bytes 524320 | tf_op jit(solution)/shard_map/ppermute | solution.py:356
  201.0 10.7 %forward_last.1 = (bf16[2048,1024]{1,0:T(8,128)(2,1)}, bf16[2048,1024]{1,0:T(8,128)(2,1)}, bf16[2048,1024]{1,0:T(8,128)(2,1)}) custom-call(bf16[2048,1024]{1,0:T(8,128)(2,1)} %get-tuple-element.86.rows.a, f32[2048,1024]{1,0:T(8,128)} %get-tuple-element.92.near, f32[2048,128]{1,0:T(8,128)} %get-tuple-element.93.gates, ...), custom_call_target="tpu_custom_call", output_to_operand_aliasing={{0}: (5, {}), {1}: (6, {})} | custom-call | flops 1000 | bytes 1000 | tf_op jit(solution)/shard_map/forward_last/pallas_call | solution.py:135
  211.8 6.9 %all-to-all-start.2 = ((bf16[16,128,1024]{2,1,0:T(8,128)(2,1)}), bf16[16,128,1024]{2,1,0:T(8,128)(2,1)}, u32[]{:S(2)}, u32[]{:S(2)}) async-start(bf16[16,128,1024]{2,1,0:T(8,128)(2,1)} %bitcast.40), calls=%async_computation.2 | async-start | bytes 8388608 | tf_op jit(solution)/shard_map/all_to_all | solution.py:347
  218.6 9.6 %out_weight_grad.4 = (bf16[1024,1024]{1,0:T(8,128)(2,1)}, bf16[2048,1024]{1,0:T(8,128)(2,1)}) custom-call(bf16[2048,1024]{1,0:T(8,128)(2,1)} %get-tuple-element.104.a, bf16[2048,1024]{1,0:T(8,128)(2,1)} %bitcast.14.dy, f32[2048,128]{1,0:T(8,128)} %get-tuple-element.93.gates), custom_call_target="tpu_custom_call" | custom-call | flops 1000 | bytes 1000 | tf_op jit(solution)/shard_map/out_weight_grad/pallas_call | solution.py:135
  228.8 8.7 %out_weight_grad.5 = bf16[1024,1024]{1,0:T(8,128)(2,1)} custom-call(bf16[2048,3072]{1,0:T(8,128)(2,1)} %get-tuple-element.118.a, bf16[2048,1024]{1,0:T(8,128)(2,1)} %get-tuple-element.105.b), custom_call_target="tpu_custom_call" | custom-call | flops 1000 | bytes 1000 | tf_op jit(solution)/shard_map/out_weight_grad/pallas_call | solution.py:135
  237.5 1.5 collective-permute-start.11
  239.0 52.4 %backward.1 = (bf16[2048,3072]{1,0:T(8,128)(2,1)}, bf16[2048,1024]{1,0:T(8,128)(2,1)}, bf16[2048,1024]{1,0:T(8,128)(2,1)}, f32[8,1024]{1,0:T(8,128)}) custom-call(bf16[2048,1024]{1,0:T(8,128)(2,1)} %bitcast.2.x, bf16[2048,1024]{1,0:T(8,128)(2,1)} %bitcast.14.dy, bf16[2048,1024]{1,0:T(8,128)(2,1)} %get-tuple-element.108.gated, ...), custom_call_target="tpu_custom_call" | custom-call | flops 1000 | bytes 1000 | tf_op jit(solution)/shard_map/backward/pallas_call | solution.py:135
  292.0 1.6 collective-permute-start.14
  293.6 8.6 %out_weight_grad.6 = bf16[1024,1024]{1,0:T(8,128)(2,1)} custom-call(bf16[2048,3072]{1,0:T(8,128)(2,1)} %get-tuple-element.118.a, bf16[2048,1024]{1,0:T(8,128)(2,1)} %get-tuple-element.105.b), custom_call_target="tpu_custom_call" | custom-call | flops 1000 | bytes 1000 | tf_op jit(solution)/shard_map/out_weight_grad/pallas_call | solution.py:135
  302.2 8.7 %in_weight_grad.6 = bf16[1024,1024]{1,0:T(8,128)(2,1)} custom-call(bf16[2048,1024]{1,0:T(8,128)(2,1)} %get-tuple-element.86.rows.a, bf16[2048,3072]{1,0:T(8,128)(2,1)} %get-tuple-element.111.b), custom_call_target="tpu_custom_call" | custom-call | flops 1000 | bytes 1000 | tf_op jit(solution)/shard_map/in_weight_grad/pallas_call | solution.py:135
  310.9 9.3 %in_weight_grad.5 = bf16[1024,1024]{1,0:T(8,128)(2,1)} custom-call(bf16[2048,1024]{1,0:T(8,128)(2,1)} %get-tuple-element.86.rows.a, bf16[2048,1024]{1,0:T(8,128)(2,1)} %get-tuple-element.114.b), custom_call_target="tpu_custom_call" | custom-call | flops 1000 | bytes 1000 | tf_op jit(solution)/shard_map/in_weight_grad/pallas_call | solution.py:135
  320.2 2.2 collective-permute-done.12
  322.4 6.1 %all-to-all-start.3 = ((bf16[16,128,1024]{2,1,0:T(8,128)(2,1)}), bf16[16,128,1024]{2,1,0:T(8,128)(2,1)}, u32[]{:S(2)}, u32[]{:S(2)}) async-start(bf16[16,128,1024]{2,1,0:T(8,128)(2,1)} %bitcast.41), calls=%async_computation.3 | async-start | bytes 8388608 | tf_op jit(solution)/shard_map/all_to_all | solution.py:347
  329.3 1.5 collective-permute-start.16
  330.8 9.1 %in_weight_grad.7 = (bf16[512,1024]{1,0:T(8,128)(2,1)}, bf16[512,1024]{1,0:T(8,128)(2,1)}) custom-call(bf16[2048,1024]{1,0:T(8,128)(2,1)} %get-tuple-element.86.rows.a, bf16[2048,3072]{1,0:T(8,128)(2,1)} %get-tuple-element.111.b), custom_call_target="tpu_custom_call" | custom-call | flops 1000 | bytes 1000 | tf_op jit(solution)/shard_map/in_weight_grad/pallas_call | solution.py:135
  341.5 8.8 %in_weight_grad.4.own = f32[1024,1024]{1,0:T(8,128)} custom-call(bf16[2048,1024]{1,0:T(8,128)(2,1)} %get-tuple-element.86.rows.a, bf16[2048,3072]{1,0:T(8,128)(2,1)} %get-tuple-element.111.b), custom_call_target="tpu_custom_call" | custom-call | flops 1000 | bytes 1000 | tf_op jit(solution)/shard_map/in_weight_grad/pallas_call | solution.py:135
  350.3 8.9 %out_weight_grad.7.refs_0_ = f32[1024,1024]{1,0:T(8,128)} custom-call(bf16[2048,3072]{1,0:T(8,128)(2,1)} %get-tuple-element.118.a, bf16[2048,1024]{1,0:T(8,128)(2,1)} %get-tuple-element.105.b), custom_call_target="tpu_custom_call" | custom-call | flops 1000 | bytes 1000 | tf_op jit(solution)/shard_map/out_weight_grad/pallas_call | solution.py:135
  359.2 8.7 %layer_out.1 = bf16[1024,1024]{1,0:T(8,128)(2,1)} custom-call(bf16[1024,1024]{1,0:T(8,128)(2,1)} %base.2, s32[1024,1]{1,0:T(8,128)} %copy.24.slot, bf16[2048,1024]{1,0:T(8,128)(2,1)} %bitcast.17.arrived), custom_call_target="tpu_custom_call" | custom-call | flops 1000 | bytes 1000 | tf_op jit(solution)/shard_map/layer_out/pallas_call | solution.py:135
  368.6 4.8 %out_weight_grad_other.1.refs_2_ = f32[2,1024,1024]{2,1,0:T(8,128)} custom-call(s32[1]{0:T(128)} %bitcast.19.number, bf16[1024,1024]{1,0:T(8,128)(2,1)} %copy-done.7, bf16[1024,1024]{1,0:T(8,128)(2,1)} %collective-permute-done.15.refs_1_), custom_call_target="tpu_custom_call" | custom-call | flops 1000 | bytes 1000 | tf_op jit(solution)/shard_map/out_weight_grad_other/pallas_call | solution.py:230
  373.3 5.1 %out_weight_grad_own.1 = f32[2,1024,1024]{2,1,0:T(8,128)} custom-call(s32[1]{0:T(128)} %bitcast.18.number, f32[1024,1024]{1,0:T(8,128)} %out_weight_grad.7.refs_0_, bf16[1024,1024]{1,0:T(8,128)(2,1)} %collective-permute-done.11.refs_1_, f32[2,1024,1024]{2,1,0:T(8,128)} %out_weight_grad_other.1.refs_2_), custom_call_target="tpu_custom_call", output_to_operand_aliasing={{}: (3, {})} | custom-call | flops 1000 | bytes 1000 | tf_op jit(solution)/shard_map/out_weight_grad_own/pallas_call | solution.py:230
  379.4 5.0 %in_weight_grad_other.1.held = f32[2,1024,1024]{2,1,0:T(8,128)} custom-call(s32[1]{0:T(128)} %bitcast.19.number, bf16[1024,1024]{1,0:T(8,128)(2,1)} %collective-permute-done.17.refs_0_, bf16[512,1024]{1,0:T(8,128)(2,1)} %copy-done.12, bf16[512,1024]{1,0:T(8,128)(2,1)} %collective-permute-done.19.refs_2_), custom_call_target="tpu_custom_call" | custom-call | flops 1000 | bytes 1000 | tf_op jit(solution)/shard_map/in_weight_grad_other/pallas_call | solution.py:230
  384.4 37.8 %collective-permute-done.16.across = bf16[1024,1024]{1,0:T(8,128)(2,1)} collective-permute-done((bf16[1024,1024]{1,0:T(8,128)(2,1)S(1)}, bf16[1024,1024]{1,0:T(8,128)(2,1)}, u32[]{:S(2)}, u32[]{:S(2)}) %collective-permute-start.16) | collective-permute-done | bytes 2097184 | tf_op jit(solution)/shard_map/ppermute | solution.py:353
  422.2 11.3 %in_weight_grad_own_and_tokens_grad.1 = (f32[2,1024,1024]{2,1,0:T(8,128)}, f32[1024,1024]{1,0:T(8,128)}) custom-call(s32[1]{0:T(128)} %bitcast.18.number, f32[1024,1024]{1,0:T(8,128)} %in_weight_grad.4.own, bf16[1024,1024]{1,0:T(8,128)(2,1)} %collective-permute-done.16.across, bf16[1024,1024]{1,0:T(8,128)(2,1)} %base.3, ...), custom_call_target="tpu_custom_call", output_to_operand_aliasing={{0}: (6, {})} | custom-call | flops 1000 | bytes 1000 | tf_op jit(solution)/shard_map/in_weight_grad_own_and_tokens_grad/pallas_call | solution.py:277
  (87 shorter events, 13.4 us)
Async XLA Ops:
  0.6 5.0 %copy-start.17 = (s32[1024,1]{0,1:T(1,128)S(1)}, s32[1024,1]{0,1:T(1,128)}, u32[]{:S(2)}) copy-start(s32[1024,1]{0,1:T(1,128)} %param.9) | copy-start | bytes 12292
  0.6 54.7 %collective-permute-start.1 = (bf16[2,1024,1024]{2,1,0:T(8,128)(2,1)}, bf16[2,1024,1024]{2,1,0:T(8,128)(2,1)}, u32[]{:S(2)}, u32[]{:S(2)}) collective-permute-start(bf16[2,1024,1024]{2,1,0:T(8,128)(2,1)} %param.14), channel_id=1, source_target_pairs={{0,1},{1,0},{2,3},{3,2},{4,5},{5,4},{6,7},{7,6},{8,9},{9,8},{10,11... | collective-permute-start | bytes 12582920 | tf_op jit(solution)/shard_map/ppermute | solution.py:353
  1.2 5.6 %copy-start.5 = (bf16[1024,1024]{1,0:T(8,128)(2,1)S(1)}, bf16[1024,1024]{1,0:T(8,128)(2,1)}, u32[]{:S(2)}) copy-start(bf16[1024,1024]{1,0:T(8,128)(2,1)} %base.2) | copy-start | bytes 6291460
  3.1 9.7 %copy-start = (bf16[1024,1024]{1,0:T(8,128)(2,1)}, bf16[1024,1024]{1,0:T(8,128)(2,1)S(1)}, u32[]{:S(2)}) copy-start(bf16[1024,1024]{1,0:T(8,128)(2,1)S(1)} %dynamic-slice_bitcast_fusion.3.rest_0_) | copy-start | bytes 6291460
  3.1 49.2 %collective-permute-start = (bf16[1024,1024]{1,0:T(8,128)(2,1)S(1)}, bf16[1024,1024]{1,0:T(8,128)(2,1)}, u32[]{:S(2)}, u32[]{:S(2)}) collective-permute-start(bf16[1024,1024]{1,0:T(8,128)(2,1)S(1)} %dynamic-slice_bitcast_fusion.3.rest_0_), channel_id=1, source_target_pairs={{0,2},{2,0},{1,3},{3,1},{4,6},{6,4},{5,7},{7,5},{8,10},{10,8},{9,1... | collective-permute-start | bytes 6291464 | tf_op jit(solution)/shard_map/ppermute | solution.py:353
  12.8 95.1 %all-to-all-start = ((bf16[16,128,1024]{2,1,0:T(8,128)(2,1)}), bf16[16,128,1024]{2,1,0:T(8,128)(2,1)}, u32[]{:S(2)}, u32[]{:S(2)}) async-start(bf16[16,128,1024]{2,1,0:T(8,128)(2,1)} %bitcast.43), calls=%async_computation | async-start | bytes 8388608 | tf_op jit(solution)/shard_map/all_to_all | solution.py:347
  18.8 39.7 %collective-permute-start.2 = (bf16[2,1024,1024]{2,1,0:T(8,128)(2,1)}, bf16[2,1024,1024]{2,1,0:T(8,128)(2,1)}, u32[]{:S(2)}, u32[]{:S(2)}) collective-permute-start(bf16[2,1024,1024]{2,1,0:T(8,128)(2,1)} %param.15), channel_id=1, source_target_pairs={{0,1},{1,0},{2,3},{3,2},{4,5},{5,4},{6,7},{7,6},{8,9},{9,8},{10,11... | collective-permute-start | bytes 12582920 | tf_op jit(solution)/shard_map/ppermute | solution.py:353
  22.3 75.0 %collective-permute-start.3 = (bf16[1024,1024]{1,0:T(8,128)(2,1)}, bf16[1024,1024]{1,0:T(8,128)(2,1)}, u32[]{:S(2)}, u32[]{:S(2)}) collective-permute-start(bf16[1024,1024]{1,0:T(8,128)(2,1)} %dynamic-slice_bitcast_fusion.2.rest_1_), channel_id=1, source_target_pairs={{0,2},{2,0},{1,3},{3,1},{4,6},{6,4},{5,7},{7,5},{8,10},{10,8},{9,1... | collective-permute-start | bytes 6291464 | tf_op jit(solution)/shard_map/ppermute | solution.py:353
  22.8 11.1 %copy-start.6 = (bf16[1024,1024]{1,0:T(8,128)(2,1)S(1)}, bf16[1024,1024]{1,0:T(8,128)(2,1)}, u32[]{:S(2)}) copy-start(bf16[1024,1024]{1,0:T(8,128)(2,1)} %base.3) | copy-start | bytes 6291460
  52.3 1.3 copy-start.15
  52.3 2.2 copy-start.14
  53.6 48.7 %collective-permute-start.4 = (bf16[1024,128]{1,0:T(8,128)(2,1)S(1)}, bf16[1024,128]{1,0:T(8,128)(2,1)S(1)}, u32[]{:S(2)}, u32[]{:S(2)}) collective-permute-start(bf16[1024,128]{1,0:T(8,128)(2,1)S(1)} %copy-done.15), channel_id=1, source_target_pairs={{0,3},{1,2},{2,1},{3,0},{4,7},{5,6},{6,5},{7,4},{8,11},{9,10},{10,... | collective-permute-start | bytes 786440 | tf_op jit(solution)/shard_map/ppermute | solution.py:356
  54.4 53.5 %collective-permute-start.5 = (bf16[128,1024]{1,0:T(8,128)(2,1)S(1)}, bf16[128,1024]{1,0:T(8,128)(2,1)S(1)}, u32[]{:S(2)}, u32[]{:S(2)}) collective-permute-start(bf16[128,1024]{1,0:T(8,128)(2,1)S(1)} %copy-done.14), channel_id=1, source_target_pairs={{0,3},{1,2},{2,1},{3,0},{4,7},{5,6},{6,5},{7,4},{8,11},{9,10},{10,... | collective-permute-start | bytes 786440 | tf_op jit(solution)/shard_map/ppermute | solution.py:356
  102.3 5.7 %copy-start.10 = (bf16[1024,128]{1,0:T(8,128)(2,1)}, bf16[1024,128]{1,0:T(8,128)(2,1)S(1)}, u32[]{:S(2)}) copy-start(bf16[1024,128]{1,0:T(8,128)(2,1)S(1)} %collective-permute-done.4.rest_0_.rest_6_) | copy-start | bytes 786436
  107.9 0.7 copy-start.11
  107.9 8.6 %copy-start.9 = (bf16[1024,640]{1,0:T(8,128)(2,1)S(1)}, bf16[1024,640]{1,0:T(8,128)(2,1)}, u32[]{:S(2)}) copy-start(bf16[1024,640]{1,0:T(8,128)(2,1)} %dynamic-slice_bitcast_fusion.5) | copy-start | bytes 3932164
  107.9 10.4 %copy-start.20 = (bf16[2,1024]{1,0:T(2,128)(2,1)S(1)}, bf16[2,1024]{1,0:T(2,128)(2,1)}, u32[]{:S(2)}) copy-start(bf16[2,1024]{1,0:T(2,128)(2,1)} %param.11) | copy-start | bytes 12292
  107.9 11.0 %copy-start.21 = (bf16[2,1024]{1,0:T(2,128)(2,1)S(1)}, bf16[2,1024]{1,0:T(2,128)(2,1)}, u32[]{:S(2)}) copy-start(bf16[2,1024]{1,0:T(2,128)(2,1)} %param.13) | copy-start | bytes 12292
  107.9 11.0 %copy-start.22 = (bf16[2,1024]{1,0:T(2,128)(2,1)S(1)}, bf16[2,1024]{1,0:T(2,128)(2,1)}, u32[]{:S(2)}) copy-start(bf16[2,1024]{1,0:T(2,128)(2,1)} %param.12) | copy-start | bytes 12292
  108.6 103.1 %all-to-all-start.1 = ((bf16[16,128,1024]{2,1,0:T(8,128)(2,1)}), bf16[16,128,1024]{2,1,0:T(8,128)(2,1)}, u32[]{:S(2)}, u32[]{:S(2)}) async-start(bf16[16,128,1024]{2,1,0:T(8,128)(2,1)} %bitcast.42), calls=%async_computation.1 | async-start | bytes 8388608 | tf_op jit(solution)/shard_map/all_to_all | solution.py:347
  116.5 44.8 %collective-permute-start.6 = (bf16[1024,640]{1,0:T(8,128)(2,1)S(1)}, bf16[1024,640]{1,0:T(8,128)(2,1)S(1)}, u32[]{:S(2)}, u32[]{:S(2)}) collective-permute-start(bf16[1024,640]{1,0:T(8,128)(2,1)S(1)} %copy-done.9), channel_id=1, source_target_pairs={{0,3},{1,2},{2,1},{3,0},{4,7},{5,6},{6,5},{7,4},{8,11},{9,10},{10,... | collective-permute-start | bytes 3932168 | tf_op jit(solution)/shard_map/ppermute | solution.py:356
  117.2 57.9 %collective-permute-start.7 = (bf16[640,1024]{1,0:T(8,128)(2,1)S(1)}, bf16[640,1024]{1,0:T(8,128)(2,1)S(1)}, u32[]{:S(2)}, u32[]{:S(2)}) collective-permute-start(bf16[640,1024]{1,0:T(8,128)(2,1)S(1)} %dynamic-slice_bitcast_fusion.4), channel_id=1, source_target_pairs={{0,3},{1,2},{2,1},{3,0},{4,7},{5,6},{6,5},{7,4},{8,11},{9,10},{10,... | collective-permute-start | bytes 3932168 | tf_op jit(solution)/shard_map/ppermute | solution.py:356
  119.6 56.2 %copy-start.13 = (bf16[256,1024]{1,0:T(8,128)(2,1)S(1)}, bf16[256,1024]{1,0:T(8,128)(2,1)}, u32[]{:S(2)}) copy-start(bf16[256,1024]{1,0:T(8,128)(2,1)} %dynamic-slice_bitcast_fusion.6) | copy-start | bytes 1572868
  161.3 15.5 %copy-start.1 = (bf16[1024,640]{1,0:T(8,128)(2,1)}, bf16[1024,640]{1,0:T(8,128)(2,1)S(1)}, u32[]{:S(2)}) copy-start(bf16[1024,640]{1,0:T(8,128)(2,1)S(1)} %collective-permute-done.6.rest_2_.rest_8_) | copy-start | bytes 3932164
  175.1 1.8 copy-start.2
  175.1 16.2 %collective-permute-start.8 = (bf16[1024,256]{1,0:T(8,128)(2,1)}, bf16[1024,256]{1,0:T(8,128)(2,1)S(1)}, u32[]{:S(2)}, u32[]{:S(2)}) collective-permute-start(bf16[1024,256]{1,0:T(8,128)(2,1)} %dynamic-slice_bitcast_fusion.7), channel_id=1, source_target_pairs={{0,3},{1,2},{2,1},{3,0},{4,7},{5,6},{6,5},{7,4},{8,11},{9,10},{10,... | collective-permute-start | bytes 1572872 | tf_op jit(solution)/shard_map/ppermute | solution.py:356
  175.7 24.5 %collective-permute-start.9 = (bf16[256,1024]{1,0:T(8,128)(2,1)S(1)}, bf16[256,1024]{1,0:T(8,128)(2,1)S(1)}, u32[]{:S(2)}, u32[]{:S(2)}) collective-permute-start(bf16[256,1024]{1,0:T(8,128)(2,1)S(1)} %copy-done.13), channel_id=1, source_target_pairs={{0,3},{1,2},{2,1},{3,0},{4,7},{5,6},{6,5},{7,4},{8,11},{9,10},{10,... | collective-permute-start | bytes 1572872 | tf_op jit(solution)/shard_map/ppermute | solution.py:356
  191.3 8.9 %copy-start.3 = (bf16[1024,256]{1,0:T(8,128)(2,1)}, bf16[1024,256]{1,0:T(8,128)(2,1)S(1)}, u32[]{:S(2)}) copy-start(bf16[1024,256]{1,0:T(8,128)(2,1)S(1)} %collective-permute-done.8.first.rest_10_) | copy-start | bytes 1572868
  200.2 0.8 copy-start.4
  211.8 110.7 %all-to-all-start.2 = ((bf16[16,128,1024]{2,1,0:T(8,128)(2,1)}), bf16[16,128,1024]{2,1,0:T(8,128)(2,1)}, u32[]{:S(2)}, u32[]{:S(2)}) async-start(bf16[16,128,1024]{2,1,0:T(8,128)(2,1)} %bitcast.40), calls=%async_computation.2 | async-start | bytes 8388608 | tf_op jit(solution)/shard_map/all_to_all | solution.py:347
  228.3 82.7 %collective-permute-start.10 = (bf16[1024,1024]{1,0:T(8,128)(2,1)}, bf16[1024,1024]{1,0:T(8,128)(2,1)S(1)}, u32[]{:S(2)}, u32[]{:S(2)}) collective-permute-start(bf16[1024,1024]{1,0:T(8,128)(2,1)} %get-tuple-element.106), channel_id=1, source_target_pairs={{0,3},{1,2},{2,1},{3,0},{4,7},{5,6},{6,5},{7,4},{8,11},{9,10},{10,... | collective-permute-start | bytes 6291464 | tf_op jit(solution)/shard_map/ppermute | solution.py:356
  237.5 84.9 %collective-permute-start.11 = (bf16[1024,1024]{1,0:T(8,128)(2,1)}, bf16[1024,1024]{1,0:T(8,128)(2,1)}, u32[]{:S(2)}, u32[]{:S(2)}) collective-permute-start(bf16[1024,1024]{1,0:T(8,128)(2,1)} %out_weight_grad.5), channel_id=1, source_target_pairs={{0,2},{2,0},{1,3},{3,1},{4,6},{6,4},{5,7},{7,5},{8,10},{10,8},{9,1... | collective-permute-start | bytes 6291464 | tf_op jit(solution)/shard_map/ppermute | solution.py:353
  291.4 31.0 %collective-permute-start.12 = (f32[8,1024]{1,0:T(8,128)}, f32[8,1024]{1,0:T(8,128)S(1)}, u32[]{:S(2)}, u32[]{:S(2)}) collective-permute-start(f32[8,1024]{1,0:T(8,128)} %get-tuple-element.116), channel_id=1, source_target_pairs={{0,2},{2,0},{1,3},{3,1},{4,6},{6,4},{5,7},{7,5},{8,10},{10,8},{9,1... | collective-permute-start | bytes 98312 | tf_op jit(solution)/shard_map/ppermute | solution.py:353
  292.0 30.4 %collective-permute-start.13 = (f32[8,1024]{1,0:T(8,128)}, f32[8,1024]{1,0:T(8,128)S(1)}, u32[]{:S(2)}, u32[]{:S(2)}) collective-permute-start(f32[8,1024]{1,0:T(8,128)} %get-tuple-element.116), channel_id=1, source_target_pairs={{0,1},{1,0},{2,3},{3,2},{4,5},{5,4},{6,7},{7,6},{8,9},{9,8},{10,11... | collective-permute-start | bytes 98312 | tf_op jit(solution)/shard_map/ppermute | solution.py:353
  292.0 30.4 %collective-permute-start.14 = (f32[8,1024]{1,0:T(8,128)}, f32[8,1024]{1,0:T(8,128)S(1)}, u32[]{:S(2)}, u32[]{:S(2)}) collective-permute-start(f32[8,1024]{1,0:T(8,128)} %get-tuple-element.116), channel_id=1, source_target_pairs={{0,3},{1,2},{2,1},{3,0},{4,7},{5,6},{6,5},{7,4},{8,11},{9,10},{10,... | collective-permute-start | bytes 98312 | tf_op jit(solution)/shard_map/ppermute | solution.py:356
  310.9 9.3 %copy-start.7 = (bf16[1024,1024]{1,0:T(8,128)(2,1)}, bf16[1024,1024]{1,0:T(8,128)(2,1)S(1)}, u32[]{:S(2)}) copy-start(bf16[1024,1024]{1,0:T(8,128)(2,1)S(1)} %collective-permute-done.10.refs_0_) | copy-start | bytes 6291460
  322.4 6.9 %copy-start.8 = (bf16[1024,1024]{1,0:T(8,128)(2,1)S(1)}, bf16[1024,1024]{1,0:T(8,128)(2,1)}, u32[]{:S(2)}) copy-start(bf16[1024,1024]{1,0:T(8,128)(2,1)} %in_weight_grad.6) | copy-start | bytes 6291460
  322.4 99.8 %all-to-all-start.3 = ((bf16[16,128,1024]{2,1,0:T(8,128)(2,1)}), bf16[16,128,1024]{2,1,0:T(8,128)(2,1)}, u32[]{:S(2)}, u32[]{:S(2)}) async-start(bf16[16,128,1024]{2,1,0:T(8,128)(2,1)} %bitcast.41), calls=%async_computation.3 | async-start | bytes 8388608 | tf_op jit(solution)/shard_map/all_to_all | solution.py:347
  328.6 11.8 %copy-start.18 = (s32[1024,1]{0,1:T(1,128)S(1)}, s32[1024,1]{0,1:T(1,128)}, u32[]{:S(2)}) copy-start(s32[1024,1]{0,1:T(1,128)} %param.9) | copy-start | bytes 12292
  328.6 11.8 %copy-start.19 = (s32[1024]{0:T(1024)S(1)}, s32[1024]{0:T(1024)}, u32[]{:S(2)}) copy-start(s32[1024]{0:T(1024)} %get-tuple-element.138) | copy-start | bytes 12292
  328.6 40.0 %collective-permute-start.15 = (bf16[1024,1024]{1,0:T(8,128)(2,1)}, bf16[1024,1024]{1,0:T(8,128)(2,1)}, u32[]{:S(2)}, u32[]{:S(2)}) collective-permute-start(bf16[1024,1024]{1,0:T(8,128)(2,1)} %out_weight_grad.6), channel_id=1, source_target_pairs={{0,1},{1,0},{2,3},{3,2},{4,5},{5,4},{6,7},{7,6},{8,9},{9,8},{10,11... | collective-permute-start | bytes 6291464 | tf_op jit(solution)/shard_map/ppermute | solution.py:353
  329.0 49.4 %collective-permute-start.17 = (bf16[1024,1024]{1,0:T(8,128)(2,1)}, bf16[1024,1024]{1,0:T(8,128)(2,1)}, u32[]{:S(2)}, u32[]{:S(2)}) collective-permute-start(bf16[1024,1024]{1,0:T(8,128)(2,1)} %in_weight_grad.5), channel_id=1, source_target_pairs={{0,3},{1,2},{2,1},{3,0},{4,7},{5,6},{6,5},{7,4},{8,11},{9,10},{10,... | collective-permute-start | bytes 6291464 | tf_op jit(solution)/shard_map/ppermute | solution.py:356
  329.3 92.9 %collective-permute-start.16 = (bf16[1024,1024]{1,0:T(8,128)(2,1)S(1)}, bf16[1024,1024]{1,0:T(8,128)(2,1)}, u32[]{:S(2)}, u32[]{:S(2)}) collective-permute-start(bf16[1024,1024]{1,0:T(8,128)(2,1)S(1)} %copy-done.8), channel_id=1, source_target_pairs={{0,2},{2,0},{1,3},{3,1},{4,6},{6,4},{5,7},{7,5},{8,10},{10,8},{9,1... | collective-permute-start | bytes 6291464 | tf_op jit(solution)/shard_map/ppermute | solution.py:353
  339.9 38.6 %collective-permute-start.18 = (bf16[512,1024]{1,0:T(8,128)(2,1)}, bf16[512,1024]{1,0:T(8,128)(2,1)S(1)}, u32[]{:S(2)}, u32[]{:S(2)}) collective-permute-start(bf16[512,1024]{1,0:T(8,128)(2,1)} %get-tuple-element.127), channel_id=1, source_target_pairs={{0,1},{1,0},{2,3},{3,2},{4,5},{5,4},{6,7},{7,6},{8,9},{9,8},{10,11... | collective-permute-start | bytes 3145736 | tf_op jit(solution)/shard_map/ppermute | solution.py:353
  340.0 38.5 %collective-permute-start.19 = (bf16[512,1024]{1,0:T(8,128)(2,1)}, bf16[512,1024]{1,0:T(8,128)(2,1)}, u32[]{:S(2)}, u32[]{:S(2)}) collective-permute-start(bf16[512,1024]{1,0:T(8,128)(2,1)} %get-tuple-element.128), channel_id=1, source_target_pairs={{0,1},{1,0},{2,3},{3,2},{4,5},{5,4},{6,7},{7,6},{8,9},{9,8},{10,11... | collective-permute-start | bytes 3145736 | tf_op jit(solution)/shard_map/ppermute | solution.py:353
  359.2 8.7 %copy-start.16 = (f32[8,1024]{1,0:T(8,128)S(1)}, f32[8,1024]{1,0:T(8,128)}, u32[]{:S(2)}) copy-start(f32[8,1024]{1,0:T(8,128)} %get-tuple-element.116) | copy-start | bytes 98308
  378.5 1.0 copy-start.12

commit v5 on v4

--- a/solution.py
+++ b/solution.py
@@ -410,15 +410,16 @@
         [some, some, rows_out((arriving, width), F32, tile)],
     )
     far += last
-    some = ((arriving, units), BF16, (tile, units - ends[2]), lambda i: (i, ends[2] // (units - ends[2])))
+    large = min(2 * TILE, arriving)
+    some = ((arriving, units), BF16, (large, units - ends[2]), lambda i: (i, ends[2] // (units - ends[2])))
     hidden2, slope2, gated = call(
         forward_last,
         "forward_last",
-        arriving // tile,
-        [tiles(normed, tile), tiles(mixed, tile), tiles(gates, tile)]
+        arriving // large,
+        [tiles(normed, large), tiles(mixed, large), tiles(gates, large)]
         + [whole(w) for w in last]
         + [(hidden2, "out", None), (slope2, "out", None)],
-        [some, some, rows_out((arriving, width), BF16, tile)],
+        [some, some, rows_out((arriving, width), BF16, large)],
         input_output_aliases={5: 0, 6: 1},
     )
     gated, dy = lax.optimization_barrier((gated, dy))

time: 440 us -> 440 us (level)
  no operation moved by 1% of the time
where the time goes in v5:
time: 440 us; the launch traced here: 434 us
  Pallas kernels  227 us (52%)
  waiting for transfers between devices  121 us (28%)
  starting transfers between devices  43.8 us (10%)
  local copies, waits for them, and re-layouts  26.5 us (6%)
  matrix products  12.6 us (3%)
    pallas_call x13, Pallas kernels, call(): pl.pallas_call(kernel, grid=(steps,), in_specs=[spec(a.shape, block, inde...  199 us
    ppermute x11, waiting for transfers between devices, over(): return lax.ppermute(value, axis, [(i, size - 1 - i) for i in range(size)])  88 us
    ppermute x9, waiting for transfers between devices, diagonal(): return lax.ppermute(value, ('sub', 'half'), [(i, 3 - i) for i in range(4)])  33.4 us
    all_to_all x4, starting transfers between devices, exchange(): lax.all_to_all(rows, ('expert', 'half'), split_axis=0, concat_axis=0, til...  27.5 us
    pallas_call x3, Pallas kernels, sums_into(): pl.pallas_call(kernel, grid_spec=pltpu.PrefetchScalarGridSpec(num_scalar_...  14.9 us
    dot_general x2, matrix products, place(): return jnp.dot(chosen, values, preferred_element_type=F32).astype(BF16)  12.1 us
    pallas_call x1, Pallas kernels, finish(): pl.pallas_call(kernel, grid_spec=pltpu.PrefetchScalarGridSpec(num_scalar_...  11.3 us
    squeeze x4, local copies, waits for them, and re-layouts, pick(): return lax.dynamic_index_in_dim(stacked, index, 0, keepdims=False)  11.2 us
  transfers between devices with their start and end apart: 24, of which 8 were waited for; matrix products, arithmetic and copies ran while one was open for 9% of the time, Pallas kernels for 50%

profile of v5, /device:TPU:0, one launch (start us, length us, event | category | flops | bytes accessed | tf_op | source)
XLA Modules:
  0.0 434.1 jit_solution(16411068514487428868)
XLA Ops:
  1.2 1.9 dynamic-slice_bitcast_fusion.3.rest_0_
  3.1 2.6 collective-permute-start
  6.8 6.0 %fusion.5 = bf16[2048,1024]{1,0:T(8,128)(2,1)} fusion(bf16[1024,1024]{1,0:T(8,128)(2,1)S(1)} %copy-done.5, s32[1024]{0:T(1024)S(1)} %get-tuple-element.139), kind=kOutput, calls=%fused_computation.7 | convolution fusion | flops 4299161600 | bytes 6295552 | tf_op jit(solution)/shard_map/dot_general | solution.py:343
  12.8 6.0 %all-to-all-start = ((bf16[16,128,1024]{2,1,0:T(8,128)(2,1)}), bf16[16,128,1024]{2,1,0:T(8,128)(2,1)}, u32[]{:S(2)}, u32[]{:S(2)}) async-start(bf16[16,128,1024]{2,1,0:T(8,128)(2,1)} %bitcast.43), calls=%async_computation | async-start | bytes 8388608 | tf_op jit(solution)/shard_map/all_to_all | solution.py:347
  19.2 3.1 dynamic-slice_bitcast_fusion.2.rest_1_
  22.8 1.8 dynamic-slice_bitcast_fusion.9
  24.6 1.7 dynamic-slice_bitcast_fusion.8
  26.3 1.9 dynamic-slice_bitcast_fusion.7
  28.1 1.9 dynamic-slice_bitcast_fusion.6
  30.0 2.5 dynamic-slice_bitcast_fusion.5
  32.5 1.4 dynamic-slice_bitcast_fusion.4
  33.9 6.1 %fusion.6 = bf16[2048,1024]{1,0:T(8,128)(2,1)} fusion(bf16[1024,1024]{1,0:T(8,128)(2,1)S(1)} %copy-done.6, s32[1024]{0:T(1024)S(1)} %get-tuple-element.139), kind=kOutput, calls=%fused_computation.8 | convolution fusion | flops 4299161600 | bytes 6295552 | tf_op jit(solution)/shard_map/dot_general | solution.py:343
  40.0 12.2 %collective-permute-done.array.rest_4_ = bf16[1024,1024]{1,0:T(8,128)(2,1)} collective-permute-done((bf16[1024,1024]{1,0:T(8,128)(2,1)S(1)}, bf16[1024,1024]{1,0:T(8,128)(2,1)}, u32[]{:S(2)}, u32[]{:S(2)}) %collective-permute-start) | collective-permute-done | bytes 2097184 | tf_op jit(solution)/shard_map/ppermute | solution.py:353
  52.3 1.3 waited.1.rest_6_
  55.4 3.1 dynamic-slice_bitcast_fusion.1.rest_2_
  58.5 3.1 dynamic-slice_bitcast_fusion.rest_3_
  61.6 35.6 %collective-permute-done.3.rest_5_ = bf16[1024,1024]{1,0:T(8,128)(2,1)} collective-permute-done((bf16[1024,1024]{1,0:T(8,128)(2,1)}, bf16[1024,1024]{1,0:T(8,128)(2,1)}, u32[]{:S(2)}, u32[]{:S(2)}) %collective-permute-start.3) | collective-permute-done | bytes 2097184 | tf_op jit(solution)/shard_map/ppermute | solution.py:353
  97.2 5.1 %collective-permute-done.4.rest_0_.rest_6_ = bf16[1024,128]{1,0:T(8,128)(2,1)S(1)} collective-permute-done((bf16[1024,128]{1,0:T(8,128)(2,1)S(1)}, bf16[1024,128]{1,0:T(8,128)(2,1)S(1)}, u32[]{:S(2)}, u32[]{:S(2)}) %collective-permute-start.4) | collective-permute-done | bytes 262176 | tf_op jit(solution)/shard_map/ppermute | solution.py:356
  102.3 5.6 %collective-permute-done.5.rest_1_.rest_7_ = bf16[128,1024]{1,0:T(8,128)(2,1)S(1)} collective-permute-done((bf16[128,1024]{1,0:T(8,128)(2,1)S(1)}, bf16[128,1024]{1,0:T(8,128)(2,1)S(1)}, u32[]{:S(2)}, u32[]{:S(2)}) %collective-permute-start.5) | collective-permute-done | bytes 262176 | tf_op jit(solution)/shard_map/ppermute | solution.py:356
  108.6 7.9 %all-to-all-start.1 = ((bf16[16,128,1024]{2,1,0:T(8,128)(2,1)}), bf16[16,128,1024]{2,1,0:T(8,128)(2,1)}, u32[]{:S(2)}, u32[]{:S(2)}) async-start(bf16[16,128,1024]{2,1,0:T(8,128)(2,1)} %bitcast.42), calls=%async_computation.1 | async-start | bytes 8388608 | tf_op jit(solution)/shard_map/all_to_all | solution.py:347
  117.2 1.1 collective-permute-start.7
  119.6 41.8 %forward_near.1 = (bf16[2048,1024]{1,0:T(8,128)(2,1)}, bf16[2048,3072]{1,0:T(8,128)(2,1)}, bf16[2048,3072]{1,0:T(8,128)(2,1)}, f32[2048,1024]{1,0:T(8,128)}, f32[2048,128]{1,0:T(8,128)}) custom-call(bf16[2048,1024]{1,0:T(8,128)(2,1)} %bitcast.2.x, f32[1,1024]{1,0:T(1,128)} %dynamic-slice_convert_fusion.2.gain, f32[1,1024]{1,0:T(1,128)} %get-tuple-element.141.bias, ...), custom_call_target="tpu_custom_call" | custom-call | flops 1000 | bytes 1000 | tf_op jit(solution)/shard_map/forward_near/pallas_call | solution.py:135
  161.4 13.8 %collective-permute-done.7.rest_3_.rest_9_ = bf16[640,1024]{1,0:T(8,128)(2,1)S(1)} collective-permute-done((bf16[640,1024]{1,0:T(8,128)(2,1)S(1)}, bf16[640,1024]{1,0:T(8,128)(2,1)S(1)}, u32[]{:S(2)}, u32[]{:S(2)}) %collective-permute-start.7) | collective-permute-done | bytes 1310752 | tf_op jit(solution)/shard_map/ppermute | solution.py:356
  175.7 1.2 collective-permute-start.9
  176.9 14.4 %forward_more.1 = (bf16[2048,1024]{1,0:T(8,128)(2,1)}, bf16[2048,1024]{1,0:T(8,128)(2,1)}, f32[2048,1024]{1,0:T(8,128)}) custom-call(bf16[2048,1024]{1,0:T(8,128)(2,1)} %get-tuple-element.86.rows.a, f32[2048,1024]{1,0:T(8,128)} %get-tuple-element.87.near, bf16[1024,128]{1,0:T(8,128)(2,1)} %copy-done.10, bf16[128,1024]{1,0:T(8,128)(2,1)} %copy-done.11, ...), custom_call_target="tpu_custom_call" | custom-call | flops 1000 | bytes 1000 | tf_op jit(solution)/shard_map/forward_more/pallas_call | solution.py:135
  191.3 8.9 %collective-permute-done.9.second.rest_11_ = bf16[256,1024]{1,0:T(8,128)(2,1)S(1)} collective-permute-done((bf16[256,1024]{1,0:T(8,128)(2,1)S(1)}, bf16[256,1024]{1,0:T(8,128)(2,1)S(1)}, u32[]{:S(2)}, u32[]{:S(2)}) %collective-permute-start.9) | collective-permute-done | bytes 524320 | tf_op jit(solution)/shard_map/ppermute | solution.py:356
  201.0 10.6 %forward_last.1 = (bf16[2048,1024]{1,0:T(8,128)(2,1)}, bf16[2048,1024]{1,0:T(8,128)(2,1)}, bf16[2048,1024]{1,0:T(8,128)(2,1)}) custom-call(bf16[2048,1024]{1,0:T(8,128)(2,1)} %get-tuple-element.86.rows.a, f32[2048,1024]{1,0:T(8,128)} %get-tuple-element.92.near, f32[2048,128]{1,0:T(8,128)} %get-tuple-element.93.gates, ...), custom_call_target="tpu_custom_call", output_to_operand_aliasing={{0}: (5, {}), {1}: (6, {})} | custom-call | flops 1000 | bytes 1000 | tf_op jit(solution)/shard_map/forward_last/pallas_call | solution.py:135
  211.6 7.3 %all-to-all-start.2 = ((bf16[16,128,1024]{2,1,0:T(8,128)(2,1)}), bf16[16,128,1024]{2,1,0:T(8,128)(2,1)}, u32[]{:S(2)}, u32[]{:S(2)}) async-start(bf16[16,128,1024]{2,1,0:T(8,128)(2,1)} %bitcast.40), calls=%async_computation.2 | async-start | bytes 8388608 | tf_op jit(solution)/shard_map/all_to_all | solution.py:347
  218.9 9.6 %out_weight_grad.4 = (bf16[1024,1024]{1,0:T(8,128)(2,1)}, bf16[2048,1024]{1,0:T(8,128)(2,1)}) custom-call(bf16[2048,1024]{1,0:T(8,128)(2,1)} %get-tuple-element.104.a, bf16[2048,1024]{1,0:T(8,128)(2,1)} %bitcast.14.dy, f32[2048,128]{1,0:T(8,128)} %get-tuple-element.93.gates), custom_call_target="tpu_custom_call" | custom-call | flops 1000 | bytes 1000 | tf_op jit(solution)/shard_map/out_weight_grad/pallas_call | solution.py:135
  229.2 8.7 %out_weight_grad.5 = bf16[1024,1024]{1,0:T(8,128)(2,1)} custom-call(bf16[2048,3072]{1,0:T(8,128)(2,1)} %get-tuple-element.118.a, bf16[2048,1024]{1,0:T(8,128)(2,1)} %get-tuple-element.105.b), custom_call_target="tpu_custom_call" | custom-call | flops 1000 | bytes 1000 | tf_op jit(solution)/shard_map/out_weight_grad/pallas_call | solution.py:135
  237.9 1.5 collective-permute-start.11
  239.4 52.0 %backward.1 = (bf16[2048,3072]{1,0:T(8,128)(2,1)}, bf16[2048,1024]{1,0:T(8,128)(2,1)}, bf16[2048,1024]{1,0:T(8,128)(2,1)}, f32[8,1024]{1,0:T(8,128)}) custom-call(bf16[2048,1024]{1,0:T(8,128)(2,1)} %bitcast.2.x, bf16[2048,1024]{1,0:T(8,128)(2,1)} %bitcast.14.dy, bf16[2048,1024]{1,0:T(8,128)(2,1)} %get-tuple-element.108.gated, ...), custom_call_target="tpu_custom_call" | custom-call | flops 1000 | bytes 1000 | tf_op jit(solution)/shard_map/backward/pallas_call | solution.py:135
  292.1 1.6 collective-permute-start.14
  293.7 8.6 %out_weight_grad.6 = bf16[1024,1024]{1,0:T(8,128)(2,1)} custom-call(bf16[2048,3072]{1,0:T(8,128)(2,1)} %get-tuple-element.118.a, bf16[2048,1024]{1,0:T(8,128)(2,1)} %get-tuple-element.105.b), custom_call_target="tpu_custom_call" | custom-call | flops 1000 | bytes 1000 | tf_op jit(solution)/shard_map/out_weight_grad/pallas_call | solution.py:135
  302.3 8.7 %in_weight_grad.6 = bf16[1024,1024]{1,0:T(8,128)(2,1)} custom-call(bf16[2048,1024]{1,0:T(8,128)(2,1)} %get-tuple-element.86.rows.a, bf16[2048,3072]{1,0:T(8,128)(2,1)} %get-tuple-element.111.b), custom_call_target="tpu_custom_call" | custom-call | flops 1000 | bytes 1000 | tf_op jit(solution)/shard_map/in_weight_grad/pallas_call | solution.py:135
  311.0 9.3 %in_weight_grad.5 = bf16[1024,1024]{1,0:T(8,128)(2,1)} custom-call(bf16[2048,1024]{1,0:T(8,128)(2,1)} %get-tuple-element.86.rows.a, bf16[2048,1024]{1,0:T(8,128)(2,1)} %get-tuple-element.114.b), custom_call_target="tpu_custom_call" | custom-call | flops 1000 | bytes 1000 | tf_op jit(solution)/shard_map/in_weight_grad/pallas_call | solution.py:135
  320.3 2.4 collective-permute-done.12
  322.7 6.3 %all-to-all-start.3 = ((bf16[16,128,1024]{2,1,0:T(8,128)(2,1)}), bf16[16,128,1024]{2,1,0:T(8,128)(2,1)}, u32[]{:S(2)}, u32[]{:S(2)}) async-start(bf16[16,128,1024]{2,1,0:T(8,128)(2,1)} %bitcast.41), calls=%async_computation.3 | async-start | bytes 8388608 | tf_op jit(solution)/shard_map/all_to_all | solution.py:347
  329.8 1.5 collective-permute-start.16
  331.3 9.1 %in_weight_grad.7 = (bf16[512,1024]{1,0:T(8,128)(2,1)}, bf16[512,1024]{1,0:T(8,128)(2,1)}) custom-call(bf16[2048,1024]{1,0:T(8,128)(2,1)} %get-tuple-element.86.rows.a, bf16[2048,3072]{1,0:T(8,128)(2,1)} %get-tuple-element.111.b), custom_call_target="tpu_custom_call" | custom-call | flops 1000 | bytes 1000 | tf_op jit(solution)/shard_map/in_weight_grad/pallas_call | solution.py:135
  341.9 8.8 %in_weight_grad.4.own = f32[1024,1024]{1,0:T(8,128)} custom-call(bf16[2048,1024]{1,0:T(8,128)(2,1)} %get-tuple-element.86.rows.a, bf16[2048,3072]{1,0:T(8,128)(2,1)} %get-tuple-element.111.b), custom_call_target="tpu_custom_call" | custom-call | flops 1000 | bytes 1000 | tf_op jit(solution)/shard_map/in_weight_grad/pallas_call | solution.py:135
  350.8 8.9 %out_weight_grad.7.refs_0_ = f32[1024,1024]{1,0:T(8,128)} custom-call(bf16[2048,3072]{1,0:T(8,128)(2,1)} %get-tuple-element.118.a, bf16[2048,1024]{1,0:T(8,128)(2,1)} %get-tuple-element.105.b), custom_call_target="tpu_custom_call" | custom-call | flops 1000 | bytes 1000 | tf_op jit(solution)/shard_map/out_weight_grad/pallas_call | solution.py:135
  359.6 8.7 %layer_out.1 = bf16[1024,1024]{1,0:T(8,128)(2,1)} custom-call(bf16[1024,1024]{1,0:T(8,128)(2,1)} %base.2, s32[1024,1]{1,0:T(8,128)} %copy.24.slot, bf16[2048,1024]{1,0:T(8,128)(2,1)} %bitcast.17.arrived), custom_call_target="tpu_custom_call" | custom-call | flops 1000 | bytes 1000 | tf_op jit(solution)/shard_map/layer_out/pallas_call | solution.py:135
  369.0 4.8 %out_weight_grad_other.1.refs_2_ = f32[2,1024,1024]{2,1,0:T(8,128)} custom-call(s32[1]{0:T(128)} %bitcast.19.number, bf16[1024,1024]{1,0:T(8,128)(2,1)} %copy-done.7, bf16[1024,1024]{1,0:T(8,128)(2,1)} %collective-permute-done.15.refs_1_), custom_call_target="tpu_custom_call" | custom-call | flops 1000 | bytes 1000 | tf_op jit(solution)/shard_map/out_weight_grad_other/pallas_call | solution.py:230
  373.8 5.1 %out_weight_grad_own.1 = f32[2,1024,1024]{2,1,0:T(8,128)} custom-call(s32[1]{0:T(128)} %bitcast.18.number, f32[1024,1024]{1,0:T(8,128)} %out_weight_grad.7.refs_0_, bf16[1024,1024]{1,0:T(8,128)(2,1)} %collective-permute-done.11.refs_1_, f32[2,1024,1024]{2,1,0:T(8,128)} %out_weight_grad_other.1.refs_2_), custom_call_target="tpu_custom_call", output_to_operand_aliasing={{}: (3, {})} | custom-call | flops 1000 | bytes 1000 | tf_op jit(solution)/shard_map/out_weight_grad_own/pallas_call | solution.py:230
  379.9 5.0 %in_weight_grad_other.1.held = f32[2,1024,1024]{2,1,0:T(8,128)} custom-call(s32[1]{0:T(128)} %bitcast.19.number, bf16[1024,1024]{1,0:T(8,128)(2,1)} %collective-permute-done.17.refs_0_, bf16[512,1024]{1,0:T(8,128)(2,1)} %copy-done.12, bf16[512,1024]{1,0:T(8,128)(2,1)} %collective-permute-done.19.refs_2_), custom_call_target="tpu_custom_call" | custom-call | flops 1000 | bytes 1000 | tf_op jit(solution)/shard_map/in_weight_grad_other/pallas_call | solution.py:230
  384.9 37.8 %collective-permute-done.16.across = bf16[1024,1024]{1,0:T(8,128)(2,1)} collective-permute-done((bf16[1024,1024]{1,0:T(8,128)(2,1)S(1)}, bf16[1024,1024]{1,0:T(8,128)(2,1)}, u32[]{:S(2)}, u32[]{:S(2)}) %collective-permute-start.16) | collective-permute-done | bytes 2097184 | tf_op jit(solution)/shard_map/ppermute | solution.py:353
  422.7 11.3 %in_weight_grad_own_and_tokens_grad.1 = (f32[2,1024,1024]{2,1,0:T(8,128)}, f32[1024,1024]{1,0:T(8,128)}) custom-call(s32[1]{0:T(128)} %bitcast.18.number, f32[1024,1024]{1,0:T(8,128)} %in_weight_grad.4.own, bf16[1024,1024]{1,0:T(8,128)(2,1)} %collective-permute-done.16.across, bf16[1024,1024]{1,0:T(8,128)(2,1)} %base.3, ...), custom_call_target="tpu_custom_call", output_to_operand_aliasing={{0}: (6, {})} | custom-call | flops 1000 | bytes 1000 | tf_op jit(solution)/shard_map/in_weight_grad_own_and_tokens_grad/pallas_call | solution.py:277
  (87 shorter events, 13.5 us)
Async XLA Ops:
  0.6 5.0 %copy-start.17 = (s32[1024,1]{0,1:T(1,128)S(1)}, s32[1024,1]{0,1:T(1,128)}, u32[]{:S(2)}) copy-start(s32[1024,1]{0,1:T(1,128)} %param.9) | copy-start | bytes 12292
  0.6 54.7 %collective-permute-start.1 = (bf16[2,1024,1024]{2,1,0:T(8,128)(2,1)}, bf16[2,1024,1024]{2,1,0:T(8,128)(2,1)}, u32[]{:S(2)}, u32[]{:S(2)}) collective-permute-start(bf16[2,1024,1024]{2,1,0:T(8,128)(2,1)} %param.14), channel_id=1, source_target_pairs={{0,1},{1,0},{2,3},{3,2},{4,5},{5,4},{6,7},{7,6},{8,9},{9,8},{10,11... | collective-permute-start | bytes 12582920 | tf_op jit(solution)/shard_map/ppermute | solution.py:353
  1.2 5.6 %copy-start.5 = (bf16[1024,1024]{1,0:T(8,128)(2,1)S(1)}, bf16[1024,1024]{1,0:T(8,128)(2,1)}, u32[]{:S(2)}) copy-start(bf16[1024,1024]{1,0:T(8,128)(2,1)} %base.2) | copy-start | bytes 6291460
  3.1 9.7 %copy-start = (bf16[1024,1024]{1,0:T(8,128)(2,1)}, bf16[1024,1024]{1,0:T(8,128)(2,1)S(1)}, u32[]{:S(2)}) copy-start(bf16[1024,1024]{1,0:T(8,128)(2,1)S(1)} %dynamic-slice_bitcast_fusion.3.rest_0_) | copy-start | bytes 6291460
  3.1 49.2 %collective-permute-start = (bf16[1024,1024]{1,0:T(8,128)(2,1)S(1)}, bf16[1024,1024]{1,0:T(8,128)(2,1)}, u32[]{:S(2)}, u32[]{:S(2)}) collective-permute-start(bf16[1024,1024]{1,0:T(8,128)(2,1)S(1)} %dynamic-slice_bitcast_fusion.3.rest_0_), channel_id=1, source_target_pairs={{0,2},{2,0},{1,3},{3,1},{4,6},{6,4},{5,7},{7,5},{8,10},{10,8},{9,1... | collective-permute-start | bytes 6291464 | tf_op jit(solution)/shard_map/ppermute | solution.py:353
  12.8 95.1 %all-to-all-start = ((bf16[16,128,1024]{2,1,0:T(8,128)(2,1)}), bf16[16,128,1024]{2,1,0:T(8,128)(2,1)}, u32[]{:S(2)}, u32[]{:S(2)}) async-start(bf16[16,128,1024]{2,1,0:T(8,128)(2,1)} %bitcast.43), calls=%async_computation | async-start | bytes 8388608 | tf_op jit(solution)/shard_map/all_to_all | solution.py:347
  18.8 39.7 %collective-permute-start.2 = (bf16[2,1024,1024]{2,1,0:T(8,128)(2,1)}, bf16[2,1024,1024]{2,1,0:T(8,128)(2,1)}, u32[]{:S(2)}, u32[]{:S(2)}) collective-permute-start(bf16[2,1024,1024]{2,1,0:T(8,128)(2,1)} %param.15), channel_id=1, source_target_pairs={{0,1},{1,0},{2,3},{3,2},{4,5},{5,4},{6,7},{7,6},{8,9},{9,8},{10,11... | collective-permute-start | bytes 12582920 | tf_op jit(solution)/shard_map/ppermute | solution.py:353
  22.3 75.0 %collective-permute-start.3 = (bf16[1024,1024]{1,0:T(8,128)(2,1)}, bf16[1024,1024]{1,0:T(8,128)(2,1)}, u32[]{:S(2)}, u32[]{:S(2)}) collective-permute-start(bf16[1024,1024]{1,0:T(8,128)(2,1)} %dynamic-slice_bitcast_fusion.2.rest_1_), channel_id=1, source_target_pairs={{0,2},{2,0},{1,3},{3,1},{4,6},{6,4},{5,7},{7,5},{8,10},{10,8},{9,1... | collective-permute-start | bytes 6291464 | tf_op jit(solution)/shard_map/ppermute | solution.py:353
  22.8 11.1 %copy-start.6 = (bf16[1024,1024]{1,0:T(8,128)(2,1)S(1)}, bf16[1024,1024]{1,0:T(8,128)(2,1)}, u32[]{:S(2)}) copy-start(bf16[1024,1024]{1,0:T(8,128)(2,1)} %base.3) | copy-start | bytes 6291460
  52.3 1.3 copy-start.15
  52.3 2.2 copy-start.14
  53.6 48.7 %collective-permute-start.4 = (bf16[1024,128]{1,0:T(8,128)(2,1)S(1)}, bf16[1024,128]{1,0:T(8,128)(2,1)S(1)}, u32[]{:S(2)}, u32[]{:S(2)}) collective-permute-start(bf16[1024,128]{1,0:T(8,128)(2,1)S(1)} %copy-done.15), channel_id=1, source_target_pairs={{0,3},{1,2},{2,1},{3,0},{4,7},{5,6},{6,5},{7,4},{8,11},{9,10},{10,... | collective-permute-start | bytes 786440 | tf_op jit(solution)/shard_map/ppermute | solution.py:356
  54.4 53.5 %collective-permute-start.5 = (bf16[128,1024]{1,0:T(8,128)(2,1)S(1)}, bf16[128,1024]{1,0:T(8,128)(2,1)S(1)}, u32[]{:S(2)}, u32[]{:S(2)}) collective-permute-start(bf16[128,1024]{1,0:T(8,128)(2,1)S(1)} %copy-done.14), channel_id=1, source_target_pairs={{0,3},{1,2},{2,1},{3,0},{4,7},{5,6},{6,5},{7,4},{8,11},{9,10},{10,... | collective-permute-start | bytes 786440 | tf_op jit(solution)/shard_map/ppermute | solution.py:356
  102.3 5.7 %copy-start.10 = (bf16[1024,128]{1,0:T(8,128)(2,1)}, bf16[1024,128]{1,0:T(8,128)(2,1)S(1)}, u32[]{:S(2)}) copy-start(bf16[1024,128]{1,0:T(8,128)(2,1)S(1)} %collective-permute-done.4.rest_0_.rest_6_) | copy-start | bytes 786436
  107.9 0.7 copy-start.11
  107.9 8.6 %copy-start.9 = (bf16[1024,640]{1,0:T(8,128)(2,1)S(1)}, bf16[1024,640]{1,0:T(8,128)(2,1)}, u32[]{:S(2)}) copy-start(bf16[1024,640]{1,0:T(8,128)(2,1)} %dynamic-slice_bitcast_fusion.5) | copy-start | bytes 3932164
  107.9 10.4 %copy-start.20 = (bf16[2,1024]{1,0:T(2,128)(2,1)S(1)}, bf16[2,1024]{1,0:T(2,128)(2,1)}, u32[]{:S(2)}) copy-start(bf16[2,1024]{1,0:T(2,128)(2,1)} %param.11) | copy-start | bytes 12292
  107.9 11.0 %copy-start.21 = (bf16[2,1024]{1,0:T(2,128)(2,1)S(1)}, bf16[2,1024]{1,0:T(2,128)(2,1)}, u32[]{:S(2)}) copy-start(bf16[2,1024]{1,0:T(2,128)(2,1)} %param.13) | copy-start | bytes 12292
  107.9 11.0 %copy-start.22 = (bf16[2,1024]{1,0:T(2,128)(2,1)S(1)}, bf16[2,1024]{1,0:T(2,128)(2,1)}, u32[]{:S(2)}) copy-start(bf16[2,1024]{1,0:T(2,128)(2,1)} %param.12) | copy-start | bytes 12292
  108.6 103.0 %all-to-all-start.1 = ((bf16[16,128,1024]{2,1,0:T(8,128)(2,1)}), bf16[16,128,1024]{2,1,0:T(8,128)(2,1)}, u32[]{:S(2)}, u32[]{:S(2)}) async-start(bf16[16,128,1024]{2,1,0:T(8,128)(2,1)} %bitcast.42), calls=%async_computation.1 | async-start | bytes 8388608 | tf_op jit(solution)/shard_map/all_to_all | solution.py:347
  116.5 44.8 %collective-permute-start.6 = (bf16[1024,640]{1,0:T(8,128)(2,1)S(1)}, bf16[1024,640]{1,0:T(8,128)(2,1)S(1)}, u32[]{:S(2)}, u32[]{:S(2)}) collective-permute-start(bf16[1024,640]{1,0:T(8,128)(2,1)S(1)} %copy-done.9), channel_id=1, source_target_pairs={{0,3},{1,2},{2,1},{3,0},{4,7},{5,6},{6,5},{7,4},{8,11},{9,10},{10,... | collective-permute-start | bytes 3932168 | tf_op jit(solution)/shard_map/ppermute | solution.py:356
  117.2 57.9 %collective-permute-start.7 = (bf16[640,1024]{1,0:T(8,128)(2,1)S(1)}, bf16[640,1024]{1,0:T(8,128)(2,1)S(1)}, u32[]{:S(2)}, u32[]{:S(2)}) collective-permute-start(bf16[640,1024]{1,0:T(8,128)(2,1)S(1)} %dynamic-slice_bitcast_fusion.4), channel_id=1, source_target_pairs={{0,3},{1,2},{2,1},{3,0},{4,7},{5,6},{6,5},{7,4},{8,11},{9,10},{10,... | collective-permute-start | bytes 3932168 | tf_op jit(solution)/shard_map/ppermute | solution.py:356
  119.6 56.2 %copy-start.13 = (bf16[256,1024]{1,0:T(8,128)(2,1)S(1)}, bf16[256,1024]{1,0:T(8,128)(2,1)}, u32[]{:S(2)}) copy-start(bf16[256,1024]{1,0:T(8,128)(2,1)} %dynamic-slice_bitcast_fusion.6) | copy-start | bytes 1572868
  161.3 15.5 %copy-start.1 = (bf16[1024,640]{1,0:T(8,128)(2,1)}, bf16[1024,640]{1,0:T(8,128)(2,1)S(1)}, u32[]{:S(2)}) copy-start(bf16[1024,640]{1,0:T(8,128)(2,1)S(1)} %collective-permute-done.6.rest_2_.rest_8_) | copy-start | bytes 3932164
  175.1 1.8 copy-start.2
  175.1 16.2 %collective-permute-start.8 = (bf16[1024,256]{1,0:T(8,128)(2,1)}, bf16[1024,256]{1,0:T(8,128)(2,1)S(1)}, u32[]{:S(2)}, u32[]{:S(2)}) collective-permute-start(bf16[1024,256]{1,0:T(8,128)(2,1)} %dynamic-slice_bitcast_fusion.7), channel_id=1, source_target_pairs={{0,3},{1,2},{2,1},{3,0},{4,7},{5,6},{6,5},{7,4},{8,11},{9,10},{10,... | collective-permute-start | bytes 1572872 | tf_op jit(solution)/shard_map/ppermute | solution.py:356
  175.7 24.5 %collective-permute-start.9 = (bf16[256,1024]{1,0:T(8,128)(2,1)S(1)}, bf16[256,1024]{1,0:T(8,128)(2,1)S(1)}, u32[]{:S(2)}, u32[]{:S(2)}) collective-permute-start(bf16[256,1024]{1,0:T(8,128)(2,1)S(1)} %copy-done.13), channel_id=1, source_target_pairs={{0,3},{1,2},{2,1},{3,0},{4,7},{5,6},{6,5},{7,4},{8,11},{9,10},{10,... | collective-permute-start | bytes 1572872 | tf_op jit(solution)/shard_map/ppermute | solution.py:356
  191.3 8.9 %copy-start.3 = (bf16[1024,256]{1,0:T(8,128)(2,1)}, bf16[1024,256]{1,0:T(8,128)(2,1)S(1)}, u32[]{:S(2)}) copy-start(bf16[1024,256]{1,0:T(8,128)(2,1)S(1)} %collective-permute-done.8.first.rest_10_) | copy-start | bytes 1572868
  200.2 0.8 copy-start.4
  211.6 111.1 %all-to-all-start.2 = ((bf16[16,128,1024]{2,1,0:T(8,128)(2,1)}), bf16[16,128,1024]{2,1,0:T(8,128)(2,1)}, u32[]{:S(2)}, u32[]{:S(2)}) async-start(bf16[16,128,1024]{2,1,0:T(8,128)(2,1)} %bitcast.40), calls=%async_computation.2 | async-start | bytes 8388608 | tf_op jit(solution)/shard_map/all_to_all | solution.py:347
  228.6 82.4 %collective-permute-start.10 = (bf16[1024,1024]{1,0:T(8,128)(2,1)}, bf16[1024,1024]{1,0:T(8,128)(2,1)S(1)}, u32[]{:S(2)}, u32[]{:S(2)}) collective-permute-start(bf16[1024,1024]{1,0:T(8,128)(2,1)} %get-tuple-element.106), channel_id=1, source_target_pairs={{0,3},{1,2},{2,1},{3,0},{4,7},{5,6},{6,5},{7,4},{8,11},{9,10},{10,... | collective-permute-start | bytes 6291464 | tf_op jit(solution)/shard_map/ppermute | solution.py:356
  237.9 84.8 %collective-permute-start.11 = (bf16[1024,1024]{1,0:T(8,128)(2,1)}, bf16[1024,1024]{1,0:T(8,128)(2,1)}, u32[]{:S(2)}, u32[]{:S(2)}) collective-permute-start(bf16[1024,1024]{1,0:T(8,128)(2,1)} %out_weight_grad.5), channel_id=1, source_target_pairs={{0,2},{2,0},{1,3},{3,1},{4,6},{6,4},{5,7},{7,5},{8,10},{10,8},{9,1... | collective-permute-start | bytes 6291464 | tf_op jit(solution)/shard_map/ppermute | solution.py:353
  291.5 31.2 %collective-permute-start.12 = (f32[8,1024]{1,0:T(8,128)}, f32[8,1024]{1,0:T(8,128)S(1)}, u32[]{:S(2)}, u32[]{:S(2)}) collective-permute-start(f32[8,1024]{1,0:T(8,128)} %get-tuple-element.116), channel_id=1, source_target_pairs={{0,2},{2,0},{1,3},{3,1},{4,6},{6,4},{5,7},{7,5},{8,10},{10,8},{9,1... | collective-permute-start | bytes 98312 | tf_op jit(solution)/shard_map/ppermute | solution.py:353
  292.1 30.7 %collective-permute-start.13 = (f32[8,1024]{1,0:T(8,128)}, f32[8,1024]{1,0:T(8,128)S(1)}, u32[]{:S(2)}, u32[]{:S(2)}) collective-permute-start(f32[8,1024]{1,0:T(8,128)} %get-tuple-element.116), channel_id=1, source_target_pairs={{0,1},{1,0},{2,3},{3,2},{4,5},{5,4},{6,7},{7,6},{8,9},{9,8},{10,11... | collective-permute-start | bytes 98312 | tf_op jit(solution)/shard_map/ppermute | solution.py:353
  292.1 30.7 %collective-permute-start.14 = (f32[8,1024]{1,0:T(8,128)}, f32[8,1024]{1,0:T(8,128)S(1)}, u32[]{:S(2)}, u32[]{:S(2)}) collective-permute-start(f32[8,1024]{1,0:T(8,128)} %get-tuple-element.116), channel_id=1, source_target_pairs={{0,3},{1,2},{2,1},{3,0},{4,7},{5,6},{6,5},{7,4},{8,11},{9,10},{10,... | collective-permute-start | bytes 98312 | tf_op jit(solution)/shard_map/ppermute | solution.py:356
  311.0 9.3 %copy-start.7 = (bf16[1024,1024]{1,0:T(8,128)(2,1)}, bf16[1024,1024]{1,0:T(8,128)(2,1)S(1)}, u32[]{:S(2)}) copy-start(bf16[1024,1024]{1,0:T(8,128)(2,1)S(1)} %collective-permute-done.10.refs_0_) | copy-start | bytes 6291460
  322.7 7.1 %copy-start.8 = (bf16[1024,1024]{1,0:T(8,128)(2,1)S(1)}, bf16[1024,1024]{1,0:T(8,128)(2,1)}, u32[]{:S(2)}) copy-start(bf16[1024,1024]{1,0:T(8,128)(2,1)} %in_weight_grad.6) | copy-start | bytes 6291460
  322.7 99.9 %all-to-all-start.3 = ((bf16[16,128,1024]{2,1,0:T(8,128)(2,1)}), bf16[16,128,1024]{2,1,0:T(8,128)(2,1)}, u32[]{:S(2)}, u32[]{:S(2)}) async-start(bf16[16,128,1024]{2,1,0:T(8,128)(2,1)} %bitcast.41), calls=%async_computation.3 | async-start | bytes 8388608 | tf_op jit(solution)/shard_map/all_to_all | solution.py:347
  329.0 11.8 %copy-start.18 = (s32[1024,1]{0,1:T(1,128)S(1)}, s32[1024,1]{0,1:T(1,128)}, u32[]{:S(2)}) copy-start(s32[1024,1]{0,1:T(1,128)} %param.9) | copy-start | bytes 12292
  329.1 11.8 %copy-start.19 = (s32[1024]{0:T(1024)S(1)}, s32[1024]{0:T(1024)}, u32[]{:S(2)}) copy-start(s32[1024]{0:T(1024)} %get-tuple-element.138) | copy-start | bytes 12292
  329.1 40.0 %collective-permute-start.15 = (bf16[1024,1024]{1,0:T(8,128)(2,1)}, bf16[1024,1024]{1,0:T(8,128)(2,1)}, u32[]{:S(2)}, u32[]{:S(2)}) collective-permute-start(bf16[1024,1024]{1,0:T(8,128)(2,1)} %out_weight_grad.6), channel_id=1, source_target_pairs={{0,1},{1,0},{2,3},{3,2},{4,5},{5,4},{6,7},{7,6},{8,9},{9,8},{10,11... | collective-permute-start | bytes 6291464 | tf_op jit(solution)/shard_map/ppermute | solution.py:353
  329.5 49.4 %collective-permute-start.17 = (bf16[1024,1024]{1,0:T(8,128)(2,1)}, bf16[1024,1024]{1,0:T(8,128)(2,1)}, u32[]{:S(2)}, u32[]{:S(2)}) collective-permute-start(bf16[1024,1024]{1,0:T(8,128)(2,1)} %in_weight_grad.5), channel_id=1, source_target_pairs={{0,3},{1,2},{2,1},{3,0},{4,7},{5,6},{6,5},{7,4},{8,11},{9,10},{10,... | collective-permute-start | bytes 6291464 | tf_op jit(solution)/shard_map/ppermute | solution.py:356
  329.8 92.9 %collective-permute-start.16 = (bf16[1024,1024]{1,0:T(8,128)(2,1)S(1)}, bf16[1024,1024]{1,0:T(8,128)(2,1)}, u32[]{:S(2)}, u32[]{:S(2)}) collective-permute-start(bf16[1024,1024]{1,0:T(8,128)(2,1)S(1)} %copy-done.8), channel_id=1, source_target_pairs={{0,2},{2,0},{1,3},{3,1},{4,6},{6,4},{5,7},{7,5},{8,10},{10,8},{9,1... | collective-permute-start | bytes 6291464 | tf_op jit(solution)/shard_map/ppermute | solution.py:353
  340.4 38.6 %collective-permute-start.18 = (bf16[512,1024]{1,0:T(8,128)(2,1)}, bf16[512,1024]{1,0:T(8,128)(2,1)S(1)}, u32[]{:S(2)}, u32[]{:S(2)}) collective-permute-start(bf16[512,1024]{1,0:T(8,128)(2,1)} %get-tuple-element.127), channel_id=1, source_target_pairs={{0,1},{1,0},{2,3},{3,2},{4,5},{5,4},{6,7},{7,6},{8,9},{9,8},{10,11... | collective-permute-start | bytes 3145736 | tf_op jit(solution)/shard_map/ppermute | solution.py:353
  340.4 38.5 %collective-permute-start.19 = (bf16[512,1024]{1,0:T(8,128)(2,1)}, bf16[512,1024]{1,0:T(8,128)(2,1)}, u32[]{:S(2)}, u32[]{:S(2)}) collective-permute-start(bf16[512,1024]{1,0:T(8,128)(2,1)} %get-tuple-element.128), channel_id=1, source_target_pairs={{0,1},{1,0},{2,3},{3,2},{4,5},{5,4},{6,7},{7,6},{8,9},{9,8},{10,11... | collective-permute-start | bytes 3145736 | tf_op jit(solution)/shard_map/ppermute | solution.py:353
  359.6 8.7 %copy-start.16 = (f32[8,1024]{1,0:T(8,128)S(1)}, f32[8,1024]{1,0:T(8,128)}, u32[]{:S(2)}) copy-start(f32[8,1024]{1,0:T(8,128)} %get-tuple-element.116) | copy-start | bytes 98308
  378.9 1.0 copy-start.12
